TPU v7x, 256 devices: a whole 4x4x8 slice. The times are simulated.
256 devices in a mesh: seg: 32 (over y, x, core), ctx: 8 (over z).
Axes of the slice: x: 4, y: 4, z: 8, core: 2. Of those that a mesh axis runs over, the one named last changes fastest.
Arguments:
- token_ids: int32 [65536], P(('seg', 'ctx')), may hold values from 65 to 116, as said below
- query_in: bfloat16 [65536, 2048], P(('seg', 'ctx')), may hold values from -6 to 6
- key_in: bfloat16 [65536, 2048], P(('seg', 'ctx')), may hold values from -6 to 6
- value_in: bfloat16 [65536, 2048], P(('seg', 'ctx')), may hold values from -6 to 6
- short_filters: float32 [3, 7, 2048], replicated, may hold values from -2 to 2
- long_filter: bfloat16 [128, 128], replicated, may hold values from -0.6 to 0.6
- skip_gain: float32 [2048], replicated, may hold values from 0.5 to 1.5
- out_grad: bfloat16 [65536, 2048], P(('seg', 'ctx')), may hold values from -9 to 9
Outputs:
- block_out: bfloat16 [65536, 2048], P(('seg', 'ctx'))
- grad_query: bfloat16 [65536, 2048], P(('seg', 'ctx'))
- grad_key: bfloat16 [65536, 2048], P(('seg', 'ctx'))
- grad_value: bfloat16 [65536, 2048], P(('seg', 'ctx'))
- grad_long: float32 [128, 128], replicated
- grad_skip: float32 [2048], replicated
- grad_short: float32 [3, 7, 2048], replicated
Inputs may be any that keep to these rules, and one draw needn't show every extreme that they name: `token_ids`: Case comes in aligned runs of 32 positions, except that the first position is always 65 and the last always 116, whatever the case of their runs.
All inputs are finite; a program needn't handle non-finite values.
Results may differ from a plain program's by a relative error of at most 0.011.
Values may be sent and summed in bfloat16 or wider, within the bound.
No kernel may reach another device: no remote copies, remote signals or barrier semaphores. Data moves between devices by JAX's collectives and lax.ppermute only.
A program may use at most 192 MiB of HBM per device.

v0:
```python
import jax
import jax.numpy as jnp
from jax import lax
from jax.sharding import PartitionSpec as P

GROUP = 16
TAPS = 128
SHORT = 7


def from_behind(value, axis, steps):
    count = lax.axis_size(axis)
    first, last = (max(0, -steps), min(count, count - steps))
    return lax.ppermute(value, axis, [(source, source + steps) for source in range(first, last)])


def featurize(framed, weights):
    margin = weights.shape[0] - 1
    length = framed.shape[0] - margin
    running = jnp.zeros((length, framed.shape[1]), jnp.float32)
    for offset in range(margin + 1):
        running = running + weights[offset][None, :] * framed[
            margin - offset : margin - offset + length
        ].astype(jnp.float32)
    return running


def featurize_back(framed, weights):
    margin = weights.shape[0] - 1
    length = framed.shape[0] - margin
    running = jnp.zeros((length, framed.shape[1]), jnp.float32)
    for offset in range(margin + 1):
        running = running + weights[offset][None, :] * framed[offset : offset + length].astype(
            jnp.float32
        )
    return running


def short_grad(grad_act, framed, margin):
    length = grad_act.shape[0]
    parts = [
        jnp.sum(
            grad_act.astype(jnp.float32)
            * framed[margin - offset : margin - offset + length].astype(jnp.float32),
            axis=0,
        )
        for offset in range(margin + 1)
    ]
    return jnp.stack(parts)


def forward_table(long_filter):
    groups = long_filter.shape[0]
    pattern = jnp.concatenate(
        [
            jnp.zeros((groups, 1), long_filter.dtype),
            long_filter[:, ::-1],
            jnp.zeros((groups, TAPS), long_filter.dtype),
        ],
        axis=1,
    )
    tiled = jnp.tile(pattern, (1, TAPS))[:, : TAPS * 2 * TAPS]
    return tiled.reshape(groups, TAPS, 2 * TAPS)


def backward_table(long_filter):
    groups = long_filter.shape[0]
    pattern = jnp.concatenate(
        [long_filter, jnp.zeros((groups, TAPS + 1), long_filter.dtype)], axis=1
    )
    tiled = jnp.tile(pattern, (1, TAPS))[:, : TAPS * 2 * TAPS]
    return tiled.reshape(groups, TAPS, 2 * TAPS)


def group_major(rows_block, groups):
    total = rows_block.shape[0]
    return rows_block.reshape(total, groups, GROUP).transpose(2, 0, 1)


def make_windows(framed, groups):
    count = framed.shape[0] // TAPS - 1
    blocks = group_major(framed, groups).reshape(GROUP, count + 1, TAPS, groups)
    return jnp.concatenate([blocks[:, :-1], blocks[:, 1:]], axis=2)


def apply_table(toeplitz, windows_x):
    count = windows_x.shape[1]
    groups = windows_x.shape[3]
    result = jnp.einsum("gts,kbsg->kbtg", toeplitz, windows_x, preferred_element_type=jnp.float32)
    return (
        result.reshape(GROUP, count * TAPS, groups)
        .transpose(1, 2, 0)
        .reshape(count * TAPS, groups * GROUP)
    )


def skew_sum(products):
    groups = products.shape[0]
    flattened = products.reshape(groups, TAPS * 2 * TAPS)
    extended = jnp.concatenate([flattened, jnp.zeros((groups, TAPS), jnp.float32)], axis=1)
    extended = extended.reshape(groups, TAPS, 2 * TAPS + 1)
    return jnp.sum(extended, axis=1)[:, TAPS:0:-1]


def take_left(block):
    return from_behind(block, ("seg", "ctx"), 1)


def take_right(block):
    return from_behind(block, ("seg", "ctx"), -1)


def per_device(
    token_ids, query_in, key_in, value_in, short_filters, long_filter, skip_gain, out_grad
):
    length, channels = query_in.shape
    groups = channels // GROUP
    margin = SHORT - 1
    filter_reach = TAPS - 1
    tail_rows = jnp.concatenate([query_in[-margin:], key_in[-margin:], value_in[-margin:]], axis=0)
    received = take_left(tail_rows)
    framed_q = jnp.concatenate([received[:margin], query_in], axis=0)
    framed_k = jnp.concatenate([received[margin : 2 * margin], key_in], axis=0)
    framed_v = jnp.concatenate([received[2 * margin :], value_in], axis=0)
    query_act = featurize(framed_q, short_filters[0])
    key_act = featurize(framed_k, short_filters[1])
    value_act = featurize(framed_v, short_filters[2])
    gated = (key_act * value_act).astype(jnp.bfloat16)
    gated_rim = take_left(gated[-filter_reach:])
    framed_x = jnp.concatenate([jnp.zeros((1, channels), jnp.bfloat16), gated_rim, gated], axis=0)
    windows_x = make_windows(framed_x, groups)
    filtered = apply_table(forward_table(long_filter), windows_x) + skip_gain[
        None, :
    ] * gated.astype(jnp.float32)
    block_out = (query_act * filtered).astype(jnp.bfloat16)
    loss_weight = jnp.where(token_ids >= 97, 0.1, 1.0).astype(jnp.float32)
    grad_out = out_grad.astype(jnp.float32) * loss_weight[:, None]
    grad_scaled = (grad_out * query_act).astype(jnp.bfloat16)
    grad_act_query = (grad_out * filtered).astype(jnp.bfloat16)
    grad_rim = take_right(grad_scaled[:filter_reach])
    framed_g = jnp.concatenate(
        [grad_scaled, grad_rim, jnp.zeros((1, channels), jnp.bfloat16)], axis=0
    )
    grad_gated = skip_gain[None, :] * grad_scaled.astype(jnp.float32) + apply_table(
        backward_table(long_filter), make_windows(framed_g, groups)
    )
    grad_act_key = (grad_gated * value_act).astype(jnp.bfloat16)
    grad_act_value = (grad_gated * key_act).astype(jnp.bfloat16)
    head_rows = jnp.concatenate(
        [grad_act_query[:margin], grad_act_key[:margin], grad_act_value[:margin]], axis=0
    )
    next_heads = take_right(head_rows)
    grad_query = featurize_back(
        jnp.concatenate([grad_act_query, next_heads[:margin]], axis=0), short_filters[0]
    ).astype(jnp.bfloat16)
    grad_key = featurize_back(
        jnp.concatenate([grad_act_key, next_heads[margin : 2 * margin]], axis=0), short_filters[1]
    ).astype(jnp.bfloat16)
    grad_value = featurize_back(
        jnp.concatenate([grad_act_value, next_heads[2 * margin :]], axis=0), short_filters[2]
    ).astype(jnp.bfloat16)
    count = windows_x.shape[1]
    grad_blocks = group_major(grad_scaled, groups).reshape(GROUP, count, TAPS, groups)
    products = jnp.einsum(
        "kbtg,kbsg->gts", grad_blocks, windows_x, preferred_element_type=jnp.float32
    )
    long_part = skew_sum(products)
    skip_part = jnp.sum(grad_scaled.astype(jnp.float32) * gated.astype(jnp.float32), axis=0)
    short_part = jnp.stack(
        [
            short_grad(grad_act_query, framed_q, margin),
            short_grad(grad_act_key, framed_k, margin),
            short_grad(grad_act_value, framed_v, margin),
        ]
    )
    long_total, skip_total, short_total = lax.psum(
        (long_part, skip_part, short_part), ("seg", "ctx")
    )
    norm_scale = float(length * lax.axis_size("seg") * lax.axis_size("ctx")) ** (-0.5)
    return (
        block_out,
        grad_query,
        grad_key,
        grad_value,
        long_total * norm_scale,
        skip_total * norm_scale,
        short_total * norm_scale,
    )


def solution(mesh):
    placed = (
        P(("seg", "ctx")),
        P(("seg", "ctx"), None),
        P(("seg", "ctx"), None),
        P(("seg", "ctx"), None),
        P(),
        P(),
        P(),
        P(("seg", "ctx"), None),
    )
    return jax.shard_map(
        per_device,
        mesh=mesh,
        in_specs=placed,
        out_specs=(
            P(("seg", "ctx"), None),
            P(("seg", "ctx"), None),
            P(("seg", "ctx"), None),
            P(("seg", "ctx"), None),
            P(),
            P(),
            P(),
        ),
        check_vma=False,
    )
```

profile of v0, /device:TPU:1, one launch (start us, length us, event | category | flops | bytes accessed | tf_op | source)
XLA Modules:
  0.0 607.0 jit_solution(17364536329712293574)
XLA Ops:
  10.0 4.4 collective-permute-start
  15.3 1.7 fusion.110
  17.7 2.3 copy.80
  21.2 1.6 copy.83
  24.1 6.3 %collective-permute-done = bf16[18,2048]{0,1:T(8,128)(2,1)S(1)} collective-permute-done((bf16[18,2048]{0,1:T(8,128)(2,1)S(1)}, bf16[18,2048]{0,1:T(8,128)(2,1)S(1)}, u32[]{:S(2)}, u32[]{:S(2)}) %collective-permute-start) | collective-permute-done | bytes 73760 | tf_op jit(solution)/shard_map/ppermute | solution.py:14
  30.9 16.8 %fusion.20 = (f32[2048]{0:T(1024)S(1)}, bf16[256,2048]{0,1:T(8,128)(2,1)S(1)}, bf16[256,2048]{0,1:T(8,128)(2,1)S(1)}, f32[256,2048]{0,1:T(8,128)}, f32[256,2048]{0,1:T(8,128)}, /*index=5*/f32[256,2048]{0,1:T(8,128)}) fusion(f32[256]{0:T(256)S(1)} %compare_select_fusion, bf16[256,2048]{0,1:T(8,128)(2,1)S(1)} %copy-done.11, ...), kind=kLoop, calls=%fused_computation.99 | loop fusion | flops 65009664 | bytes 12837888 | tf_op jit(solution)/shard_map/reduce_sum | solution.py:168
  48.7 3.9 collective-permute-start.2
  53.6 1.9 collective-permute-start.1
  56.1 4.4 tile.8
  60.5 12.9 %tile.9 = bf16[128,32896]{0,1:T(8,128)(2,1)} reshape(bf16[128,128,257]{0,2,1:T(8,128)(2,1)} %tile.8) | data formatting | bytes 16842752 | tf_op jit(solution)/shard_map/tile | solution.py:62
  73.5 7.1 %slice.435 = bf16[128,32768]{0,1:T(8,128)(2,1)} slice(bf16[128,32896]{0,1:T(8,128)(2,1)} %tile.9), slice={[0:128], [0:32768]} | slice | bytes 16777216 | tf_op jit(solution)/shard_map/slice | solution.py:62
  80.5 12.4 %copy.110 = bf16[128,128,256,1]{2,1,3,0:T(8,128)(2,1)} copy(bf16[128,128,256,1]{0,2,1,3:T(8,128)(2,1)} %bitcast.103) | data formatting | bytes 16777216 | tf_op jit(solution)/shard_map/reshape | solution.py:63
  93.0 4.4 tile.20
  97.4 12.9 %tile.21 = bf16[128,32896]{0,1:T(8,128)(2,1)} reshape(bf16[128,128,257]{0,2,1:T(8,128)(2,1)} %tile.20) | data formatting | bytes 16842752 | tf_op jit(solution)/shard_map/tile | solution.py:71
  110.3 7.0 %slice.440 = bf16[128,32768]{0,1:T(8,128)(2,1)} slice(bf16[128,32896]{0,1:T(8,128)(2,1)} %tile.21), slice={[0:128], [0:32768]} | slice | bytes 16777216 | tf_op jit(solution)/shard_map/slice | solution.py:71
  117.4 12.3 %copy.111 = bf16[128,128,256,1]{2,1,3,0:T(8,128)(2,1)} copy(bf16[128,128,256,1]{0,2,1,3:T(8,128)(2,1)} %bitcast.104) | data formatting | bytes 16777216 | tf_op jit(solution)/shard_map/reshape | solution.py:72
  130.7 1.7 copy.103
  132.4 78.3 %psum.22 = f32[2048]{0:T(1024)S(1)} all-reduce(f32[2048]{0:T(1024)S(1)} %get-tuple-element.51), channel_id=1, replica_groups=mesh['seg'=32,'ctx'=8] {'seg','ctx'}, use_global_device_ids=true, to_apply=%region_3.4 | all-reduce | flops 2048 | bytes 16384 | tf_op jit(solution)/shard_map/psum | solution.py:176
  211.4 3.8 pad_maximum_fusion.2
  215.1 2.1 copy.87
  217.3 1.7 fusion.107
  219.0 1.9 copy.121
  221.0 2.3 copy.120
  223.3 8.1 %convolution_bitcast_fusion.1 = f32[16,2,128,128]{2,0,1,3:T(8,128)} fusion(bf16[128,128,256,1]{2,1,3,0:T(8,128)(2,1)} %copy.110, bf16[16,2,128,128]{2,0,1,3:T(8,128)(2,1)S(1)} %copy.121, bf16[16,2,128,128]{2,0,1,3:T(8,128)(2,1)S(1)} %copy.120), kind=kOutput, calls=%fused_computation.185 | convolution fusion | flops 272629760 | bytes 12582912 | tf_op jit(solution)/shard_map/gts,kbsg->kbtg/dot_general | solution.py:89
  231.4 3.0 copy.92
  234.4 3.1 copy.93
  237.5 2.1 copy.95
  239.6 1.8 fusion.106
  241.4 2.8 copy.123
  244.2 1.8 copy.122
  246.0 7.0 %fusion.67 = f32[16,2,128,128]{2,0,1,3:T(8,128)S(1)} fusion(bf16[128,128,256,1]{2,1,3,0:T(8,128)(2,1)} %copy.111, bf16[16,2,128,128]{2,0,1,3:T(8,128)(2,1)} %copy.123, bf16[16,2,128,128]{2,0,1,3:T(8,128)(2,1)} %copy.122), kind=kOutput, calls=%fused_computation.184 | convolution fusion | flops 272629760 | bytes 12582912 | tf_op jit(solution)/shard_map/gts,kbsg->kbtg/dot_general | solution.py:89
  252.9 1.9 copy.100
  254.9 2.2 copy.101
  257.2 12.1 %fusion.62 = (f32[2048]{0:T(1024)S(1)}, f32[2048]{0:T(1024)S(1)}, f32[2048]{0:T(1024)S(1)}, f32[2048]{0:T(1024)S(1)}, f32[2048]{0:T(1024)S(1)}, /*index=5*/f32[2...) fusion(bf16[256,2048]{0,1:T(8,128)(2,1)} %copy.85, bf16[6,2048]{0,1:T(8,128)(2,1)} %copy-done.24, ...), kind=kLoop, calls=%fused_computation.141 | loop fusion | flops 23578624 | bytes 7430144 | tf_op jit(solution)/shard_map/reduce_sum | solution.py:42
  270.3 5.6 fusion.48
  276.0 6.3 %fusion.34 = (f32[2048]{0:T(1024)S(1)}, f32[2048]{0:T(1024)S(1)}, f32[2048]{0:T(1024)S(1)}, f32[2048]{0:T(1024)S(1)}, f32[2048]{0:T(1024)S(1)}, /*index=5*/f32[2...) fusion(bf16[256,2048]{0,1:T(8,128)(2,1)S(1)} %copy-done.10, ...), kind=kLoop, calls=%fused_computation.113 | loop fusion | flops 25675776 | bytes 9528320 | tf_op jit(solution)/shard_map/reduce_sum | solution.py:42
  282.9 2.4 collective-permute-start.3
  285.3 8.1 %convolution_bitcast_fusion = f32[128,128,256]{2,1,0:T(8,128)} fusion(bf16[16,2,128,128]{2,0,1,3:T(8,128)(2,1)S(1)} %copy-done.25, bf16[16,2,128,128]{2,0,1,3:T(8,128)(2,1)S(1)} %copy-done.6, bf16[16,2,128,128]{2,0,1,3:T(8,128)(2,1)S(1)} %copy-done.8), kind=kOutput, calls=%fused_computation | convolution fusion | flops 272629760 | bytes 19922944 | tf_op jit(solution)/shard_map/kbtg,kbsg->gts/dot_general | solution.py:164
  296.5 17.8 %copy.119 = f32[128,128,256]{0,2,1:T(8,128)} copy(f32[128,128,256]{2,1,0:T(8,128)} %convolution_bitcast_fusion) | data formatting | bytes 33554432 | tf_op jit(solution)/shard_map/reshape | solution.py:99
  314.3 13.3 %concatenate.59 = f32[128,32896]{0,1:T(8,128)} pad(f32[128,32768]{0,1:T(8,128)} %bitcast.102, f32[]{:T(128)} %constant.10.clone.1), padding=0_0x0_128 | pad | bytes 33619972 | tf_op jit(solution)/shard_map/concatenate | solution.py:100
  327.6 17.5 %reshape.121 = f32[128,128,257]{0,2,1:T(8,128)} reshape(f32[128,32896]{0,1:T(8,128)} %concatenate.59) | data formatting | bytes 33685504 | tf_op jit(solution)/shard_map/reshape | solution.py:101
  345.1 6.7 %reduce_sum.207 = f32[128,257]{0,1:T(8,128)S(1)} reduce(f32[128,128,257]{0,2,1:T(8,128)} %reshape.121, f32[]{:T(128)} %constant.10.clone.1), dimensions={1}, to_apply=%region_0.1 | reduce | flops 4177792 | bytes 16974340 | tf_op jit(solution)/shard_map/reduce_sum | solution.py:102
  352.8 5.9 fusion.27
  358.8 5.9 fusion.41
  364.8 5.9 fusion.55
  370.7 1.4 copy.106
  375.0 222.0 %all-reduce.5.cloned.1.call-done = (f32[128,128]{0,1:T(8,128)}, f32[3,7,2048]{2,1,0:T(8,128)}) async-done(((f32[128,128]{0,1:T(8,128)}, f32[3,7,2048]{2,1,0:T(8,128)}), (f32[128,128]{0,1:T(8,128)}, f32[3,7,2048]{2,1,0:T(8,128)})) %all-reduce.5.cloned.1.call-update) | async-done | bytes 237584 | tf_op jit(solution)/shard_map/psum | solution.py:176
  598.5 1.6 broadcast_multiply_fusion
  (106 shorter events, 21.7 us)
Async XLA Ops:
  7.2 12.8 %copy-start.27 = (bf16[256,2048]{1,0:T(8,128)(2,1)S(1)}, bf16[256,2048]{1,0:T(8,128)(2,1)}, u32[]{:S(2)}) copy-start(bf16[256,2048]{1,0:T(8,128)(2,1)} %param.11) | copy-start | bytes 3145732
  7.2 589.8 %all-reduce.5.cloned.1.call-start = ((), (), s32[]{:S(2)}) async-start(), calls=%async_computation | async-start | bytes 524288 | tf_op jit(solution)/shard_map/psum | solution.py:176
  10.0 20.5 %collective-permute-start = (bf16[18,2048]{0,1:T(8,128)(2,1)S(1)}, bf16[18,2048]{0,1:T(8,128)(2,1)S(1)}, u32[]{:S(2)}, u32[]{:S(2)}) collective-permute-start(bf16[18,2048]{0,1:T(8,128)(2,1)S(1)} %copy.81), channel_id=1, source_target_pairs={{0,1},{1,2},{2,3},{3,4},{4,5},{5,6},{6,7},{7,8},{8,9},{9,10},{10,1... | collective-permute-start | bytes 221192 | tf_op jit(solution)/shard_map/ppermute | solution.py:14
  21.2 1.6 copy-start.28
  22.8 8.0 %copy-start.2 = (bf16[256,2048]{0,1:T(8,128)(2,1)}, bf16[256,2048]{0,1:T(8,128)(2,1)S(1)}, u32[]{:S(2)}) copy-start(bf16[256,2048]{0,1:T(8,128)(2,1)S(1)} %copy.83) | copy-start | bytes 3145732
  24.1 6.7 %copy-start.4 = (bf16[256,2048]{0,1:T(8,128)(2,1)S(1)}, bf16[256,2048]{0,1:T(8,128)(2,1)}, u32[]{:S(2)}) copy-start(bf16[256,2048]{0,1:T(8,128)(2,1)} %copy.85) | copy-start | bytes 3145732
  24.1 6.7 %copy-start.9 = (bf16[256,2048]{0,1:T(8,128)(2,1)S(1)}, bf16[256,2048]{0,1:T(8,128)(2,1)}, u32[]{:S(2)}) copy-start(bf16[256,2048]{0,1:T(8,128)(2,1)} %copy.80) | copy-start | bytes 3145732
  24.1 6.7 %copy-start.11 = (bf16[256,2048]{0,1:T(8,128)(2,1)S(1)}, bf16[256,2048]{0,1:T(8,128)(2,1)}, u32[]{:S(2)}) copy-start(bf16[256,2048]{0,1:T(8,128)(2,1)} %copy.94) | copy-start | bytes 3145732
  30.8 16.9 %copy-start.20 = (bf16[6,2048]{0,1:T(8,128)(2,1)}, bf16[6,2048]{0,1:T(8,128)(2,1)S(1)}, u32[]{:S(2)}) copy-start(bf16[6,2048]{0,1:T(8,128)(2,1)S(1)} %get-tuple-element.70) | copy-start | bytes 73732
  30.8 16.9 %copy-start.22 = (bf16[6,2048]{0,1:T(8,128)(2,1)}, bf16[6,2048]{0,1:T(8,128)(2,1)S(1)}, u32[]{:S(2)}) copy-start(bf16[6,2048]{0,1:T(8,128)(2,1)S(1)} %get-tuple-element.72) | copy-start | bytes 73732
  30.8 16.9 %copy-start.24 = (bf16[6,2048]{0,1:T(8,128)(2,1)}, bf16[6,2048]{0,1:T(8,128)(2,1)S(1)}, u32[]{:S(2)}) copy-start(bf16[6,2048]{0,1:T(8,128)(2,1)S(1)} %get-tuple-element.71) | copy-start | bytes 73732
  47.7 163.6 %copy-start = (bf16[256,2048]{0,1:T(8,128)(2,1)}, bf16[256,2048]{0,1:T(8,128)(2,1)S(1)}, u32[]{:S(2)}) copy-start(bf16[256,2048]{0,1:T(8,128)(2,1)S(1)} %get-tuple-element.53) | copy-start | bytes 3145732
  47.7 7.8 %copy-start.29 = (bf16[128,128]{1,0:T(8,128)(2,1)S(1)}, bf16[128,128]{1,0:T(8,128)(2,1)}, u32[]{:S(2)}) copy-start(bf16[128,128]{1,0:T(8,128)(2,1)} %param.13) | copy-start | bytes 98308
  48.7 162.6 %collective-permute-start.2 = (bf16[127,2048]{0,1:T(8,128)(2,1)}, bf16[127,2048]{0,1:T(8,128)(2,1)}, u32[]{:S(2)}, u32[]{:S(2)}) collective-permute-start(bf16[127,2048]{0,1:T(8,128)(2,1)} %slice.437), channel_id=1, source_target_pairs={{1,0},{2,1},{3,2},{4,3},{5,4},{6,5},{7,6},{8,7},{9,8},{10,9},{11,1... | collective-permute-start | bytes 1560584 | tf_op jit(solution)/shard_map/ppermute | solution.py:14
  53.6 157.6 %collective-permute-start.1 = (bf16[127,2048]{0,1:T(8,128)(2,1)}, bf16[127,2048]{0,1:T(8,128)(2,1)}, u32[]{:S(2)}, u32[]{:S(2)}) collective-permute-start(bf16[127,2048]{0,1:T(8,128)(2,1)} %slice.432), channel_id=1, source_target_pairs={{0,1},{1,2},{2,3},{3,4},{4,5},{5,6},{6,7},{7,8},{8,9},{9,10},{10,1... | collective-permute-start | bytes 1560584 | tf_op jit(solution)/shard_map/ppermute | solution.py:14
  220.9 10.5 %copy-start.5 = (bf16[16,2,128,128]{2,0,1,3:T(8,128)(2,1)}, bf16[16,2,128,128]{2,0,1,3:T(8,128)(2,1)S(1)}, u32[]{:S(2)}) copy-start(bf16[16,2,128,128]{2,0,1,3:T(8,128)(2,1)S(1)} %copy.121) | copy-start | bytes 3145732
  223.3 8.1 %copy-start.7 = (bf16[16,2,128,128]{2,0,1,3:T(8,128)(2,1)}, bf16[16,2,128,128]{2,0,1,3:T(8,128)(2,1)S(1)}, u32[]{:S(2)}) copy-start(bf16[16,2,128,128]{2,0,1,3:T(8,128)(2,1)S(1)} %copy.120) | copy-start | bytes 3145732
  241.4 2.8 copy-start.26
  254.9 2.3 copy-start.30
  257.1 13.1 %copy-start.3 = (bf16[256,2048]{0,1:T(8,128)(2,1)S(1)}, bf16[256,2048]{0,1:T(8,128)(2,1)}, u32[]{:S(2)}) copy-start(bf16[256,2048]{0,1:T(8,128)(2,1)} %copy-done.2) | copy-start | bytes 3145732
  257.2 13.1 %copy-start.15 = (f32[256,2048]{0,1:T(8,128)S(1)}, f32[256,2048]{0,1:T(8,128)}, u32[]{:S(2)}) copy-start(f32[256,2048]{0,1:T(8,128)} %get-tuple-element.54) | copy-start | bytes 6291460
  257.2 13.1 %copy-start.23 = (bf16[6,2048]{0,1:T(8,128)(2,1)S(1)}, bf16[6,2048]{0,1:T(8,128)(2,1)}, u32[]{:S(2)}) copy-start(bf16[6,2048]{0,1:T(8,128)(2,1)} %copy-done.22) | copy-start | bytes 73732
  269.2 1.0 copy-start.16
  270.2 5.8 copy-start.1
  270.2 5.8 copy-start.10
  270.3 5.8 copy-start.12
  270.3 5.7 copy-start.13
  270.3 5.7 copy-start.14
  270.3 5.7 copy-start.21
  275.9 6.4 %copy-start.18 = (bf16[256,2048]{0,1:T(8,128)(2,1)}, bf16[256,2048]{0,1:T(8,128)(2,1)S(1)}, u32[]{:S(2)}) copy-start(bf16[256,2048]{0,1:T(8,128)(2,1)S(1)} %get-tuple-element.58) | copy-start | bytes 3145732
  282.3 2.9 copy-start.6
  282.3 2.9 copy-start.8
  282.3 2.9 copy-start.25
  282.9 69.6 %collective-permute-start.3 = (bf16[18,2048]{0,1:T(8,128)(2,1)S(1)}, bf16[18,2048]{0,1:T(8,128)(2,1)S(1)}, u32[]{:S(2)}, u32[]{:S(2)}) collective-permute-start(bf16[18,2048]{0,1:T(8,128)(2,1)S(1)} %pad_maximum_fusion.11), channel_id=1, source_target_pairs={{1,0},{2,1},{3,2},{4,3},{5,4},{6,5},{7,6},{8,7},{9,8},{10,9},{11,1... | collective-permute-start | bytes 221192 | tf_op jit(solution)/shard_map/ppermute | solution.py:14
  352.8 6.0 copy-start.19
  352.8 11.9 %copy-start.17 = (bf16[256,2048]{0,1:T(8,128)(2,1)S(1)}, bf16[256,2048]{0,1:T(8,128)(2,1)}, u32[]{:S(2)}) copy-start(bf16[256,2048]{0,1:T(8,128)(2,1)} %copy-done.16) | copy-start | bytes 3145732
Sparse Core Ops, SparseCore 0:
  352.6 244.3 all-reduce.4
where the time goes:
time: 611 us; the launch traced here: 607 us
  waiting for transfers between devices  228 us (37%)
  local copies, waits for them, and re-layouts  176 us (29%)
  blocking collectives  78.3 us (13%)
  other arithmetic  74.2 us (12%)
  matrix products  23.2 us (4%)
  between operations  14.6 us (2%)
  starting transfers between devices  12.6 us (2%)
    psum x1, waiting for transfers between devices, per_device(): lax.psum((long_part, skip_part, short_part), ('seg', 'ctx'))  222 us
    psum x1, blocking collectives, per_device(): lax.psum((long_part, skip_part, short_part), ('seg', 'ctx'))  78.3 us
    reduce_sum x3, other arithmetic, short_grad(): jnp.sum(grad_act.astype(jnp.float32) * framed[margin - offset:margin - of...  23.9 us
    unnamed x76, local copies, waits for them, and re-layouts  22.8 us
    reshape x1, local copies, waits for them, and re-layouts, skew_sum(): flattened = products.reshape(groups, TAPS * 2 * TAPS)  17.8 us
    reshape x1, local copies, waits for them, and re-layouts, skew_sum(): extended = extended.reshape(groups, TAPS, 2 * TAPS + 1)  17.5 us
    another operation x2, local copies, waits for them, and re-layouts, forward_table(): tiled = jnp.tile(pattern, (1, TAPS))[:, :TAPS * 2 * TAPS]  17.4 us
    another operation x2, local copies, waits for them, and re-layouts, backward_table(): tiled = jnp.tile(pattern, (1, TAPS))[:, :TAPS * 2 * TAPS]  17.3 us
  transfers between devices with their start and end apart: 5, of which 2 were waited for; matrix products, arithmetic and copies ran while one was open for 29% of the time, Pallas kernels for 0%

commit v1 on v0

v1 whole, which is shorter than its diff:
```python
import functools

import jax
import jax.numpy as jnp
from jax import lax
from jax.experimental import pallas as pl
from jax.experimental.pallas import tpu as pltpu
from jax.sharding import PartitionSpec as P

GROUP = 16
TAPS = 128
SHORT = 7
LANES = 128
PER_TILE = LANES // GROUP
EDGE = 16
RUN = 32
PART_ROWS = 32
AXES = ("seg", "ctx")
MIB = 1024 * 1024
F32 = jnp.float32
BF16 = jnp.bfloat16


def causal(frame, which, taps, start, count):
    total = taps[which, 0:1] * frame[pl.ds(start, count)]
    for j in range(1, SHORT):
        total = total + taps[which, j : j + 1] * frame[pl.ds(start - j, count)]
    return total


def weight_of(repeat):
    return jnp.where(repeat > 0.5, F32(0.1), F32(1.0))


def mark_repeats(ids, marks):
    rows = marks.shape[0]
    row = lax.broadcasted_iota(jnp.int32, (RUN, LANES), 0)

    def mark(at):
        return jnp.full((RUN, LANES), (ids[at] >= 97).astype(F32))

    for r in range(0, rows, RUN):
        run = mark(r + 1)
        if r == 0:
            run = jnp.where(row == 0, mark(0), run)
        if r + RUN == rows:
            run = jnp.where(row == RUN - 1, mark(rows - 1), run)
        marks[r : r + RUN] = run


def edges_kernel(
    ids, q, g, k_edge, k, v_edge, v, q_tail, taps_ref, right, left, kf, vf, qf, rep
):
    @pl.when(pl.program_id(0) == 0)
    def _():
        mark_repeats(ids, rep)

    for lt in range(q.shape[1] // LANES):
        ls = slice(lt * LANES, (lt + 1) * LANES)
        taps = taps_ref[:, :, ls]
        kf[:EDGE] = k_edge[:, ls].astype(F32)
        vf[:EDGE] = v_edge[:, ls].astype(F32)
        kf[EDGE:] = k[:, ls].astype(F32)
        vf[EDGE:] = v[:, ls].astype(F32)
        qf[...] = q[:, ls].astype(F32)
        for r in range(0, TAPS, 64):
            act_k = causal(kf, 1, taps, EDGE + r, 64)
            act_v = causal(vf, 2, taps, EDGE + r, 64)
            right[r : r + 64, ls] = (act_k * act_v).astype(BF16)
        right[TAPS : TAPS + EDGE, ls] = k[TAPS - EDGE :, ls]
        right[TAPS + EDGE : TAPS + 2 * EDGE, ls] = v[TAPS - EDGE :, ls]
        right[TAPS + 2 * EDGE : TAPS + 3 * EDGE, ls] = q_tail[:, ls]
        for r, count in ((EDGE, 48), (EDGE + 48, 64)):
            act_q = causal(qf, 0, taps, r, count)
            grad = g[r : r + count, ls].astype(F32) * weight_of(rep[r : r + count])
            left[r - EDGE : r - EDGE + count, ls] = (grad * act_q).astype(BF16)
        left[TAPS - EDGE : TAPS, ls] = q[:EDGE, ls]
        left[TAPS : TAPS + EDGE, ls] = g[:EDGE, ls]
        left[TAPS + EDGE : TAPS + 2 * EDGE, ls] = rep[:EDGE].astype(BF16)


def tables_kernel(taps, fwd, bwd, plain, backwards):
    row = lax.broadcasted_iota(jnp.int32, (TAPS, TAPS), 0)
    col = lax.broadcasted_iota(jnp.int32, (TAPS, TAPS), 1)
    tile = pl.program_id(0)

    @pl.when(tile == 0)
    def _():
        mirror = ((row + col == TAPS) | ((row == 0) & (col == 0))).astype(BF16)
        plain[...] = taps[...].astype(F32)
        backwards[...] = jnp.dot(taps[...], mirror, preferred_element_type=F32)

    first = pl.multiple_of(tile * PER_TILE, PER_TILE)
    plain_rows = plain[pl.ds(first, PER_TILE)]
    backward_rows = backwards[pl.ds(first, PER_TILE)]

    def rings(source, g):
        spread = jnp.broadcast_to(source[g : g + 1], (TAPS, TAPS))
        return pltpu.roll(spread, 0, 1, stride=1, stride_axis=0)

    for g in range(PER_TILE):
        ring = rings(backward_rows, g)
        fwd[g, :, :TAPS] = jnp.where(col > row, ring, 0.0).astype(BF16)
        fwd[g, :, TAPS:] = jnp.where(col <= row, ring, 0.0).astype(BF16)
        ring = rings(plain_rows, g)
        bwd[g, :, :TAPS] = jnp.where(col >= row, ring, 0.0).astype(BF16)
        bwd[g, :, TAPS:] = jnp.where(col < row, ring, 0.0).astype(BF16)


def main_kernel(
    ids, q, k, v, g, taps_ref, skip_ref, fwd, bwd, from_left, from_right,
    out, gq, gk, gv, heads, part,
    qf, kf, vf, xs, gs, act_q, act_k, act_v, prod_p, prod_f, prod_b, diag, rep,
):
    tile = pl.program_id(0)

    @pl.when(tile == 0)
    def _():
        mark_repeats(ids, rep)

    rows = q.shape[0]
    step = 64
    taps = taps_ref[...]
    skip = skip_ref[...]
    qf[EDGE : EDGE + rows] = q[...].astype(F32)
    kf[EDGE : EDGE + rows] = k[...].astype(F32)
    vf[EDGE : EDGE + rows] = v[...].astype(F32)
    kf[:EDGE] = from_left[TAPS : TAPS + EDGE].astype(F32)
    vf[:EDGE] = from_left[TAPS + EDGE : TAPS + 2 * EDGE].astype(F32)
    qf[:EDGE] = from_left[TAPS + 2 * EDGE : TAPS + 3 * EDGE].astype(F32)
    qf[EDGE + rows :] = from_right[TAPS - EDGE : TAPS].astype(F32)
    xs[:TAPS] = from_left[:TAPS]
    gs[rows + EDGE :] = from_right[: TAPS - EDGE]

    skip_sum = jnp.zeros((8, LANES), F32)
    for r in range(0, rows, step):
        a_q = causal(qf, 0, taps, EDGE + r, step)
        a_k = causal(kf, 1, taps, EDGE + r, step)
        a_v = causal(vf, 2, taps, EDGE + r, step)
        act_q[r : r + step] = a_q
        act_k[r : r + step] = a_k
        act_v[r : r + step] = a_v
        gated = (a_k * a_v).astype(BF16)
        xs[TAPS + r : TAPS + r + step] = gated
        grad = g[r : r + step].astype(F32) * weight_of(rep[r : r + step])
        scaled = (grad * a_q).astype(BF16)
        gs[r : r + step] = scaled
        both = scaled.astype(F32) * gated.astype(F32)
        skip_sum = skip_sum + jnp.sum(both.reshape(step // 8, 8, LANES), axis=0)
    a_q = causal(qf, 0, taps, EDGE + rows, EDGE)
    grad = from_right[TAPS : TAPS + EDGE].astype(F32) * weight_of(
        from_right[TAPS + EDGE : TAPS + 2 * EDGE].astype(F32)
    )
    gs[rows : rows + EDGE] = (grad * a_q).astype(BF16)

    lane_group = lax.broadcasted_iota(jnp.int32, (8, LANES), 1) // GROUP
    group2 = jnp.concatenate([lane_group, lane_group], axis=1)
    win_g = jnp.concatenate([gs[: 2 * TAPS], gs[TAPS:]], axis=1)
    own_x = jnp.concatenate([xs[TAPS : 2 * TAPS], xs[2 * TAPS :]], axis=1)

    def spread(table, windows, prod):
        prod[...] = jnp.dot(
            table[...].reshape(PER_TILE * TAPS, 2 * TAPS), windows, preferred_element_type=F32
        )

    def gather(prod, r, count):
        block, at = divmod(r, TAPS)
        ls = slice(block * LANES, (block + 1) * LANES)
        picks = jnp.broadcast_to(lane_group[0:1], (count, LANES))
        total = prod[at : at + count, ls]
        for n in range(1, PER_TILE):
            total = jnp.where(picks == n, prod[n * TAPS + at : n * TAPS + at + count, ls], total)
        return total

    def short_sums(sums, grads, frame, r):
        wide_grads = grads.astype(F32)
        return [
            total
            + jnp.sum(
                (wide_grads * frame[pl.ds(EDGE + r - j, step)]).reshape(step // 8, 8, LANES),
                axis=0,
            )
            for j, total in enumerate(sums)
        ]

    zeros = [jnp.zeros((8, LANES), F32)] * SHORT
    sums_q, sums_k, sums_v = zeros, zeros, zeros
    win_x = jnp.concatenate([xs[: 2 * TAPS], xs[TAPS:]], axis=1)
    spread(fwd, win_x, prod_f)
    spread(bwd, win_g, prod_b)
    wide = jnp.broadcast_to(group2[0:1], (TAPS, 2 * LANES))
    masked = jnp.concatenate(
        [jnp.where(wide == n, own_x, jnp.zeros_like(own_x)) for n in range(PER_TILE)], axis=0
    )
    prod_p[...] = lax.dot_general(
        masked, win_g, (((1,), (1,)), ((), ())), preferred_element_type=F32
    )
    for r in range(0, rows, step):
        filtered = gather(prod_f, r, step) + skip * xs[TAPS + r : TAPS + r + step].astype(F32)
        out[r : r + step] = (act_q[r : r + step] * filtered).astype(BF16)
        grad = g[r : r + step].astype(F32) * weight_of(rep[r : r + step])
        grads = (grad * filtered).astype(BF16)
        gq[r : r + step] = grads
        sums_q = short_sums(sums_q, grads, qf, r)
    for r in range(0, rows, step):
        grad_gated = skip * gs[r : r + step].astype(F32) + gather(prod_b, r, step)
        grads = (grad_gated * act_v[r : r + step]).astype(BF16)
        gk[r : r + step] = grads
        sums_k = short_sums(sums_k, grads, kf, r)
        grads = (grad_gated * act_k[r : r + step]).astype(BF16)
        gv[r : r + step] = grads
        sums_v = short_sums(sums_v, grads, vf, r)
    sub = lax.broadcasted_iota(jnp.int32, (8, LANES), 0)
    lane = lax.broadcasted_iota(jnp.int32, (8, LANES), 1)
    for n in range(PER_TILE):
        total = jnp.zeros((8, LANES), F32)
        for m in range(TAPS // 8):
            r = n * TAPS + m * 8
            ring = jnp.where(
                lane >= sub + m * 8, prod_p[r : r + 8, :LANES], prod_p[r : r + 8, LANES:]
            )
            total = total + (pltpu.roll(ring, LANES - 8 * m, 1) if m else ring)
        diag[n * 8 : n * 8 + 8] = total
    long_part = diag[pl.ds(0, PER_TILE, stride=8)]
    for r in range(1, 8):
        long_part = long_part + pltpu.roll(diag[pl.ds(r, PER_TILE, stride=8)], LANES - r, 1)
    part[0, :PER_TILE] = long_part

    heads[:EDGE] = gq[:EDGE]
    heads[EDGE : 2 * EDGE] = gk[:EDGE]
    heads[2 * EDGE :] = gv[:EDGE]
    lines = [jnp.sum(s, axis=0, keepdims=True) for s in sums_q + sums_k + sums_v + [skip_sum]]
    lines.append(jnp.zeros((PART_ROWS - PER_TILE - len(lines), LANES), F32))
    part[0, PER_TILE:] = jnp.concatenate(lines, axis=0)


def back_kernel(grads, heads, taps_ref, result, frame):
    rows = grads.shape[0]
    step = 64
    for lt in range(grads.shape[1] // LANES):
        ls = slice(lt * LANES, (lt + 1) * LANES)
        frame[:rows] = grads[:, ls].astype(F32)
        frame[rows:] = heads[:, ls].astype(F32)
        for r in range(0, rows, step):
            total = taps_ref[0, 0:1, ls] * frame[pl.ds(r, step)]
            for j in range(1, SHORT):
                total = total + taps_ref[0, j : j + 1, ls] * frame[pl.ds(r + j, step)]
            result[r : r + step, ls] = total.astype(BF16)


def params(limit=60):
    return pltpu.CompilerParams(
        dimension_semantics=("arbitrary",), vmem_limit_bytes=limit * MIB
    )


def columns(rows, width):
    return pl.BlockSpec((rows, width), lambda i: (0, i))


def fixed(shape):
    return pl.BlockSpec(shape, lambda i: (0,) * len(shape))


def along_tile(count, width):
    return pl.BlockSpec((3, count, width), lambda i: (0, 0, i))


def make_edges(ids, q, k, v, g, taps):
    rows, channels = q.shape
    width = 512
    first = pl.BlockSpec((TAPS, width), lambda i: (0, i))
    last = pl.BlockSpec((TAPS, width), lambda i: (rows // TAPS - 1, i))
    ahead = pl.BlockSpec((EDGE, width), lambda i: ((rows - TAPS) // EDGE - 1, i))
    tail = pl.BlockSpec((EDGE, width), lambda i: (rows // EDGE - 1, i))
    return pl.pallas_call(
        edges_kernel,
        grid=(channels // width,),
        in_specs=[pl.BlockSpec(memory_space=pltpu.SMEM), first, first, ahead, last, ahead, last]
        + [tail, along_tile(SHORT, width)],
        out_specs=[columns(TAPS + 3 * EDGE, width), columns(TAPS + 2 * EDGE, width)],
        out_shape=[
            jax.ShapeDtypeStruct((TAPS + 3 * EDGE, channels), BF16),
            jax.ShapeDtypeStruct((TAPS + 2 * EDGE, channels), BF16),
        ],
        scratch_shapes=[
            pltpu.VMEM((TAPS + EDGE, LANES), F32),
            pltpu.VMEM((TAPS + EDGE, LANES), F32),
            pltpu.VMEM((TAPS, LANES), F32),
            pltpu.VMEM((rows, LANES), F32),
        ],
        compiler_params=params(),
        name="edges",
    )(ids, q, g, k, k, v, v, q, taps)


def make_tables(long_filter):
    groups = long_filter.shape[0]
    wide = pl.BlockSpec((PER_TILE, TAPS, 2 * TAPS), lambda i: (i, 0, 0))
    return pl.pallas_call(
        tables_kernel,
        grid=(groups // PER_TILE,),
        in_specs=[fixed(long_filter.shape)],
        out_specs=[wide, wide],
        out_shape=[jax.ShapeDtypeStruct((groups, TAPS, 2 * TAPS), BF16)] * 2,
        scratch_shapes=[pltpu.VMEM((groups, TAPS), F32)] * 2,
        compiler_params=params(),
        cost_estimate=pl.CostEstimate(
            flops=0, bytes_accessed=32 * groups * TAPS * TAPS, transcendentals=0
        ),
        name="tables",
    )(long_filter)


def make_main(ids, q, k, v, g, taps, skip, fwd, bwd, from_left, from_right):
    rows, channels = q.shape
    tiles = channels // LANES
    wide = pl.BlockSpec((PER_TILE, TAPS, 2 * TAPS), lambda i: (i, 0, 0))
    big = jax.ShapeDtypeStruct((rows, channels), BF16)
    return pl.pallas_call(
        main_kernel,
        grid=(tiles,),
        in_specs=[pl.BlockSpec(memory_space=pltpu.SMEM)]
        + [columns(rows, LANES)] * 4
        + [along_tile(SHORT, LANES), columns(1, LANES), wide, wide]
        + [columns(from_left.shape[0], LANES), columns(from_right.shape[0], LANES)],
        out_specs=[columns(rows, LANES)] * 4
        + [columns(3 * EDGE, LANES), pl.BlockSpec((1, PART_ROWS, LANES), lambda i: (i, 0, 0))],
        out_shape=[big] * 4
        + [
            jax.ShapeDtypeStruct((3 * EDGE, channels), BF16),
            jax.ShapeDtypeStruct((tiles, PART_ROWS, LANES), F32),
        ],
        scratch_shapes=[
            pltpu.VMEM((rows + 2 * EDGE, LANES), F32),
            pltpu.VMEM((rows + EDGE, LANES), F32),
            pltpu.VMEM((rows + EDGE, LANES), F32),
            pltpu.VMEM((rows + TAPS, LANES), BF16),
            pltpu.VMEM((rows + TAPS, LANES), BF16),
            pltpu.VMEM((rows, LANES), F32),
            pltpu.VMEM((rows, LANES), F32),
            pltpu.VMEM((rows, LANES), F32),
            pltpu.VMEM((PER_TILE * TAPS, 2 * TAPS), F32),
            pltpu.VMEM((PER_TILE * TAPS, 2 * TAPS), F32),
            pltpu.VMEM((PER_TILE * TAPS, 2 * TAPS), F32),
            pltpu.VMEM((PER_TILE * 8, LANES), F32),
            pltpu.VMEM((rows, LANES), F32),
        ],
        compiler_params=params(),
        name="main",
    )(ids, q, k, v, g, taps, skip, fwd, bwd, from_left, from_right)


def make_back(which, grads, heads, taps):
    rows, channels = grads.shape
    width = 512
    return pl.pallas_call(
        back_kernel,
        grid=(channels // width,),
        in_specs=[
            columns(rows, width),
            pl.BlockSpec((EDGE, width), lambda i: (which, i)),
            pl.BlockSpec((1, SHORT, width), lambda i: (which, 0, i)),
        ],
        out_specs=columns(rows, width),
        out_shape=jax.ShapeDtypeStruct((rows, channels), BF16),
        scratch_shapes=[pltpu.VMEM((rows + EDGE, LANES), F32)],
        compiler_params=params(),
        cost_estimate=pl.CostEstimate(
            flops=14 * rows * channels, bytes_accessed=8 * rows * channels, transcendentals=0
        ),
        name="back",
    )(grads, heads, taps)


def from_behind(value, steps):
    count = lax.axis_size("seg") * lax.axis_size("ctx")
    first, last = max(0, -steps), min(count, count - steps)
    return lax.ppermute(value, AXES, [(s, s + steps) for s in range(first, last)])


def swap(value, mask):
    count = lax.axis_size("seg") * lax.axis_size("ctx")
    return lax.ppermute(value, AXES, [(s, s ^ mask) for s in range(count)])


def ring_masks(size):
    masks = []
    span = 1
    while span < size:
        masks.append(span if 2 * span < size or size == 2 else span + span // 2)
        span *= 2
    return masks


def total_over_all(value, work):
    ctx = lax.axis_size("ctx")
    seg = lax.axis_size("seg")
    me = lax.axis_index("seg") * ctx + lax.axis_index("ctx")
    cores = 2
    along = 1
    while along * along * cores < seg:
        along *= 2
    halving = [ctx, cores * ctx]
    doubling = [cores * ctx * m for m in ring_masks(along)]
    doubling += [cores * ctx * along * m for m in ring_masks(seg // (cores * along))]
    doubling = [m for m in doubling if m not in halving] + ring_masks(ctx)
    mine = []
    done = []
    pending = list(work)
    for mask in halving:
        half = value.shape[0] // 2
        high = ((me // mask) % 2) == 1
        if mask != ctx:
            high = high ^ (((me // (2 * mask)) % 2) == 1)
        low_part, high_part = value[:half], value[half:]
        mine.append(high)
        got = swap(jnp.where(high, low_part, high_part), mask)
        value = jnp.where(high, high_part, low_part) + got
    for n, mask in enumerate(doubling):
        job = pending.pop(0) if pending and n >= 1 else None
        if job is None:
            value = value + swap(value, mask)
            continue
        run, inputs = job
        value, inputs = lax.optimization_barrier((value, inputs))
        got = swap(value, mask)
        value, result = lax.optimization_barrier((value + got, run(*inputs)))
        done.append(result)
    done += [run(*inputs) for run, inputs in pending]
    for mask, high in zip(reversed(halving), reversed(mine)):
        got = swap(value, mask)
        value = jnp.where(
            high, jnp.concatenate([got, value]), jnp.concatenate([value, got])
        )
    return value, done


def per_device(
    token_ids, query_in, key_in, value_in, short_filters, long_filter, skip_gain, out_grad
):
    length, channels = query_in.shape
    tiles = channels // LANES
    to_right, to_left = make_edges(
        token_ids, query_in, key_in, value_in, out_grad, short_filters
    )
    from_left = from_behind(to_right, 1)
    from_right = from_behind(to_left, -1)
    fwd, bwd = make_tables(long_filter)
    out, gq, gk, gv, heads, part = make_main(
        token_ids, query_in, key_in, value_in, out_grad, short_filters,
        skip_gain.reshape(1, channels), fwd, bwd, from_left, from_right,
    )
    next_heads = from_behind(heads, -1)
    jobs = [
        (functools.partial(make_back, i), (grads, next_heads, short_filters))
        for i, grads in enumerate((gq, gk, gv))
    ]
    total, (grad_query, grad_key, grad_value) = total_over_all(
        part.reshape(tiles * PART_ROWS, LANES), jobs
    )
    norm_scale = float(length * lax.axis_size("seg") * lax.axis_size("ctx")) ** (-0.5)
    total = total.reshape(tiles, PART_ROWS, LANES) * norm_scale
    grad_long = total[:, :PER_TILE].reshape(tiles * PER_TILE, TAPS)
    short_lines = 3 * SHORT
    grad_short = (
        total[:, PER_TILE : PER_TILE + short_lines]
        .transpose(1, 0, 2)
        .reshape(3, SHORT, channels)
    )
    grad_skip = total[:, PER_TILE + short_lines].reshape(channels)
    return out, grad_query, grad_key, grad_value, grad_long, grad_skip, grad_short


def solution(mesh):
    sharded = P(("seg", "ctx"), None)
    return jax.shard_map(
        per_device,
        mesh=mesh,
        in_specs=(P(("seg", "ctx")), sharded, sharded, sharded, P(), P(), P(), sharded),
        out_specs=(sharded, sharded, sharded, sharded, P(), P(), P()),
        check_vma=False,
    )
```

time: 611 us -> 107 us (0.18)
  waiting for transfers between devices: 228 us -> 14.7 us
  local copies, waits for them, and re-layouts: 176 us -> 3.11 us
  blocking collectives: 78.3 us -> 0 us
  other arithmetic: 74.2 us -> 1.12 us
  Pallas kernels: 0 us -> 49.3 us
  starting transfers between devices: 12.6 us -> 36.5 us
  matrix products: 23.2 us -> 0 us
  between operations: 14.6 us -> 0.87 us
    psum x1 -> x0, waiting for transfers between devices: 222 us -> none  [per_device(): lax.psum((long_part, skip_part, short_part), ('seg', 'ctx'))]
    psum x1 -> x0, blocking collectives: 78.3 us -> none  [per_device(): lax.psum((long_part, skip_part, short_part), ('seg', 'ctx'))]
    reshape x5 -> x2, local copies, waits for them, and re-layouts: 61.8 us -> 1.34 us  [the longest x1 0.7 us: per_device(): grad_short = total[:, PER_TILE:PER_TILE + short_lines].transpose(1, 0, 2)...]
    pallas_call x0 -> x6, Pallas kernels: none -> 49.3 us  [the longest x1 21.4 us: make_main(): pl.pallas_call(main_kernel, grid=(tiles,), in_specs=[pl.BlockSpec(memory_...]
    reduce_sum x5 -> x0, other arithmetic: 47.5 us -> none  [the longest x3 23.9 us: short_grad(): jnp.sum(grad_act.astype(jnp.float32) * framed[margin - offset:margin - of...]
    another operation x8 -> x0, local copies, waits for them, and re-layouts: 35.8 us -> none  [the longest x2 17.4 us: forward_table(): tiled = jnp.tile(pattern, (1, TAPS))[:, :TAPS * 2 * TAPS]]
    slice x17 -> x2, local copies, waits for them, and re-layouts: 25.4 us -> 0.63 us  [the longest x1 0.61 us: per_device(): grad_skip = total[:, PER_TILE + short_lines].reshape(channels)]
    ppermute x4 -> x13, starting transfers between devices: 12.6 us -> 36.5 us  [the longest x10 19.6 us: swap(): return lax.ppermute(value, AXES, [(s, s ^ mask) for s in range(count)])]
  transfers between devices with their start and end apart: 5 -> 13, of which waited for: 2 -> 7; matrix products, arithmetic and copies ran while one was open for 29% -> 0% of each run, Pallas kernels for 0% -> 22%
where the time goes in v1:
time: 107 us; the launch traced here: 106 us
  Pallas kernels  49.3 us (46%)
  starting transfers between devices  36.5 us (34%)
  waiting for transfers between devices  14.7 us (14%)
  local copies, waits for them, and re-layouts  3.11 us (3%)
  other arithmetic  1.12 us (1%)
    pallas_call x1, Pallas kernels, make_main(): pl.pallas_call(main_kernel, grid=(tiles,), in_specs=[pl.BlockSpec(memory_...  21.4 us
    ppermute x10, starting transfers between devices, swap(): return lax.ppermute(value, AXES, [(s, s ^ mask) for s in range(count)])  19.6 us
    ppermute x3, starting transfers between devices, from_behind(): lax.ppermute(value, AXES, [(s, s + steps) for s in range(first, last)])  16.9 us
    ppermute x10, waiting for transfers between devices, swap(): return lax.ppermute(value, AXES, [(s, s ^ mask) for s in range(count)])  12.2 us
    pallas_call x3, Pallas kernels, make_back(): pl.pallas_call(back_kernel, grid=(channels // width,), in_specs=[columns(...  11.8 us
    pallas_call x1, Pallas kernels, make_tables(): pl.pallas_call(tables_kernel, grid=(groups // PER_TILE,), in_specs=[fixed...  11.7 us
    pallas_call x1, Pallas kernels, make_edges(): pl.pallas_call(edges_kernel, grid=(channels // width,), in_specs=[pl.Bloc...  4.52 us
    ppermute x3, waiting for transfers between devices, from_behind(): lax.ppermute(value, AXES, [(s, s + steps) for s in range(first, last)])  2.41 us
  transfers between devices with their start and end apart: 13, of which 7 were waited for; matrix products, arithmetic and copies ran while one was open for 0% of the time, Pallas kernels for 22%

profile of v1, /device:TPU:1, one launch (start us, length us, event | category | flops | bytes accessed | tf_op | source)
XLA Modules:
  0.0 105.6 jit_solution(11151329781121999016)
XLA Ops:
  0.6 4.5 %edges.1 = (bf16[176,2048]{1,0:T(8,128)(2,1)}, bf16[160,2048]{1,0:T(8,128)(2,1)}) custom-call(s32[256]{0:T(256)} %ids.3, bf16[256,2048]{1,0:T(8,128)(2,1)} %q.3, bf16[256,2048]{1,0:T(8,128)(2,1)} %g.3, bf16[256,2048]{1,0:T(8,128)(2,1)} %k.3, bf16[256,2048]{1,0:T(8,128)(2,1)} %k.3, bf16[256,2048]{1,0:T(8,128)(2,1)} %v.3, bf16[256,2048]{1,0:T(8,128)(2,1)} %v.3, ...), custom_call_target="tpu_custom_call" | custom-call | tf_op jit(solution)/shard_map/edges/pallas_call | solution.py:276
  5.2 4.4 %collective-permute-start = (bf16[176,2048]{1,0:T(8,128)(2,1)}, bf16[176,2048]{1,0:T(8,128)(2,1)S(1)}, u32[]{:S(2)}, u32[]{:S(2)}) collective-permute-start(bf16[176,2048]{1,0:T(8,128)(2,1)} %get-tuple-element.37), channel_id=1, source_target_pairs={{0,1},{1,2},{2,3},{3,4},{4,5},{5,6},{6,7},{7,8},{8,9},{9,10},{10,1... | collective-permute-start | bytes 2162696 | tf_op jit(solution)/shard_map/ppermute | solution.py:379
  9.5 6.4 %collective-permute-start.1 = (bf16[160,2048]{1,0:T(8,128)(2,1)}, bf16[160,2048]{1,0:T(8,128)(2,1)S(1)}, u32[]{:S(2)}, u32[]{:S(2)}) collective-permute-start(bf16[160,2048]{1,0:T(8,128)(2,1)} %get-tuple-element.38), channel_id=1, source_target_pairs={{1,0},{2,1},{3,2},{4,3},{5,4},{6,5},{7,6},{8,7},{9,8},{10,9},{11,1... | collective-permute-start | bytes 1966088 | tf_op jit(solution)/shard_map/ppermute | solution.py:379
  16.0 11.7 %tables.1 = (bf16[128,128,256]{2,1,0:T(8,128)(2,1)}, bf16[128,128,256]{2,1,0:T(8,128)(2,1)}) custom-call(bf16[128,128]{1,0:T(8,128)(2,1)} %taps.1), custom_call_target="tpu_custom_call" | custom-call | bytes 67108864 | tf_op jit(solution)/shard_map/tables/pallas_call | solution.py:300
  27.6 0.0 collective-permute-done.1.from_right
  27.7 0.0 copy-start.2
  27.7 2.4 %collective-permute-done.from_left = bf16[176,2048]{1,0:T(8,128)(2,1)S(1)} collective-permute-done((bf16[176,2048]{1,0:T(8,128)(2,1)}, bf16[176,2048]{1,0:T(8,128)(2,1)S(1)}, u32[]{:S(2)}, u32[]{:S(2)}) %collective-permute-start) | collective-permute-done | bytes 720928 | tf_op jit(solution)/shard_map/ppermute | solution.py:379
  30.1 0.0 copy-start.1
  30.1 0.0 copy-done.2
  30.1 0.9 copy-done.1
  30.9 21.4 %main.1 = (bf16[256,2048]{1,0:T(8,128)(2,1)}, bf16[256,2048]{1,0:T(8,128)(2,1)}, bf16[256,2048]{1,0:T(8,128)(2,1)}, bf16[256,2048]{1,0:T(8,128)(2,1)}, bf16[48,2048]{1,0:T(8,128)(2,1)}, /*index=5*/f32[16,32,128]{2,1,0:T(8,128)}) custom-call(s32[256]{0:T(256)} %ids.3, bf16[256,2048]{1,0:T(8,128)(2,1)} %q.3, bf16[256,2048]{1,0:T(8,128)(2,1)} %k.3, ...), custom_call_target="tpu_custom_call" | custom-call | tf_op jit(solution)/shard_map/main/pallas_call | solution.py:320
  52.3 1.0 slice_select_fusion.1
  53.3 0.1 collective-permute-start.2
  53.4 1.3 %collective-permute-done.2 = f32[256,128]{1,0:T(8,128)S(1)} collective-permute-done((f32[256,128]{1,0:T(8,128)S(1)}, f32[256,128]{1,0:T(8,128)S(1)}, u32[]{:S(2)}, u32[]{:S(2)}) %collective-permute-start.2) | collective-permute-done | bytes 131104 | tf_op jit(solution)/shard_map/ppermute | solution.py:384
  54.8 2.3 %collective-permute-start.3 = (f32[128,128]{1,0:T(8,128)S(1)}, f32[128,128]{1,0:T(8,128)S(1)}, u32[]{:S(2)}, u32[]{:S(2)}) collective-permute-start(f32[128,128]{1,0:T(8,128)S(1)} %slice_select_fusion.2), channel_id=1, source_target_pairs={{0,16},{1,17},{2,18},{3,19},{4,20},{5,21},{6,22},{7,23},{8,24},{9,... | collective-permute-start | bytes 196616 | tf_op jit(solution)/shard_map/ppermute | solution.py:384
  57.0 6.1 %collective-permute-start.5 = (bf16[48,2048]{1,0:T(8,128)(2,1)}, bf16[48,2048]{1,0:T(8,128)(2,1)S(1)}, u32[]{:S(2)}, u32[]{:S(2)}) collective-permute-start(bf16[48,2048]{1,0:T(8,128)(2,1)} %get-tuple-element.42), channel_id=1, source_target_pairs={{1,0},{2,1},{3,2},{4,3},{5,4},{6,5},{7,6},{8,7},{9,8},{10,9},{11,1... | collective-permute-start | bytes 589832 | tf_op jit(solution)/shard_map/ppermute | solution.py:379
  63.2 0.0 collective-permute-done.3
  63.2 1.6 %collective-permute-start.4 = (f32[128,128]{1,0:T(8,128)S(1)}, f32[128,128]{1,0:T(8,128)S(1)}, u32[]{:S(2)}, u32[]{:S(2)}) collective-permute-start(f32[128,128]{1,0:T(8,128)S(1)} %select_add_fusion), channel_id=1, source_target_pairs={{0,48},{1,49},{2,50},{3,51},{4,52},{5,53},{6,54},{7,55},{8,56},{9,... | collective-permute-start | bytes 196616 | tf_op jit(solution)/shard_map/ppermute | solution.py:384
  64.8 3.7 %collective-permute-done.4 = f32[128,128]{1,0:T(8,128)S(1)} collective-permute-done((f32[128,128]{1,0:T(8,128)S(1)}, f32[128,128]{1,0:T(8,128)S(1)}, u32[]{:S(2)}, u32[]{:S(2)}) %collective-permute-start.4) | collective-permute-done | bytes 65568 | tf_op jit(solution)/shard_map/ppermute | solution.py:384
  68.6 0.0 collective-permute-done.5.heads
  68.6 0.0 copy-start
  68.6 0.4 collective-permute-start.6
  69.0 0.2 copy-done
  69.2 3.9 %back.3 = bf16[256,2048]{1,0:T(8,128)(2,1)} custom-call(bf16[256,2048]{1,0:T(8,128)(2,1)} %get-tuple-element.44.grads, bf16[48,2048]{1,0:T(8,128)(2,1)} %copy-done, f32[3,7,2048]{2,1,0:T(8,128)} %taps_ref.6), custom_call_target="tpu_custom_call" | custom-call | flops 7340032 | bytes 4194304 | tf_op jit(solution)/shard_map/back/pallas_call | solution.py:357
  73.2 0.0 collective-permute-done.6
  73.2 1.9 %collective-permute-start.7 = (f32[128,128]{1,0:T(8,128)S(1)}, f32[128,128]{1,0:T(8,128)S(1)}, u32[]{:S(2)}, u32[]{:S(2)}) collective-permute-start(f32[128,128]{1,0:T(8,128)S(1)} %add.47), channel_id=1, source_target_pairs={{0,192},{1,193},{2,194},{3,195},{4,196},{5,197},{6,198},{7,199},{8... | collective-permute-start | bytes 196616 | tf_op jit(solution)/shard_map/ppermute | solution.py:384
  75.1 3.9 %back.4 = bf16[256,2048]{1,0:T(8,128)(2,1)} custom-call(bf16[256,2048]{1,0:T(8,128)(2,1)} %get-tuple-element.51.grads, bf16[48,2048]{1,0:T(8,128)(2,1)} %copy-done, f32[3,7,2048]{2,1,0:T(8,128)} %taps_ref.6), custom_call_target="tpu_custom_call" | custom-call | flops 7340032 | bytes 4194304 | tf_op jit(solution)/shard_map/back/pallas_call | solution.py:357
  79.0 0.0 collective-permute-done.7
  79.0 0.1 collective-permute-start.8
  79.1 3.9 %back.5 = bf16[256,2048]{1,0:T(8,128)(2,1)} custom-call(bf16[256,2048]{1,0:T(8,128)(2,1)} %get-tuple-element.58.grads, bf16[48,2048]{1,0:T(8,128)(2,1)} %copy-done, f32[3,7,2048]{2,1,0:T(8,128)} %taps_ref.6), custom_call_target="tpu_custom_call" | custom-call | flops 7340032 | bytes 4194304 | tf_op jit(solution)/shard_map/back/pallas_call | solution.py:357
  83.0 0.0 collective-permute-done.8
  83.0 3.2 %collective-permute-start.9 = (f32[128,128]{1,0:T(8,128)S(1)}, f32[128,128]{1,0:T(8,128)S(1)}, u32[]{:S(2)}, u32[]{:S(2)}) collective-permute-start(f32[128,128]{1,0:T(8,128)S(1)} %add.49), channel_id=1, source_target_pairs={{0,2},{1,3},{2,0},{3,1},{4,6},{5,7},{6,4},{7,5},{8,10},{9,11},{10,... | collective-permute-start | bytes 196616 | tf_op jit(solution)/shard_map/ppermute | solution.py:384
  86.3 2.4 %collective-permute-done.9 = f32[128,128]{1,0:T(8,128)S(1)} collective-permute-done((f32[128,128]{1,0:T(8,128)S(1)}, f32[128,128]{1,0:T(8,128)S(1)}, u32[]{:S(2)}, u32[]{:S(2)}) %collective-permute-start.9) | collective-permute-done | bytes 65568 | tf_op jit(solution)/shard_map/ppermute | solution.py:384
  88.6 4.0 %collective-permute-start.10 = (f32[128,128]{1,0:T(8,128)S(1)}, f32[128,128]{1,0:T(8,128)S(1)}, u32[]{:S(2)}, u32[]{:S(2)}) collective-permute-start(f32[128,128]{1,0:T(8,128)S(1)} %add.50), channel_id=1, source_target_pairs={{0,6},{1,7},{2,4},{3,5},{4,2},{5,3},{6,0},{7,1},{8,14},{9,15},{10,... | collective-permute-start | bytes 196616 | tf_op jit(solution)/shard_map/ppermute | solution.py:384
  92.7 1.7 %collective-permute-done.10 = f32[128,128]{1,0:T(8,128)S(1)} collective-permute-done((f32[128,128]{1,0:T(8,128)S(1)}, f32[128,128]{1,0:T(8,128)S(1)}, u32[]{:S(2)}, u32[]{:S(2)}) %collective-permute-start.10) | collective-permute-done | bytes 65568 | tf_op jit(solution)/shard_map/ppermute | solution.py:384
  94.4 1.0 collective-permute-start.11
  95.4 2.2 %collective-permute-done.11 = f32[128,128]{1,0:T(8,128)S(1)} collective-permute-done((f32[128,128]{1,0:T(8,128)S(1)}, f32[128,128]{1,0:T(8,128)S(1)}, u32[]{:S(2)}, u32[]{:S(2)}) %collective-permute-start.11) | collective-permute-done | bytes 65568 | tf_op jit(solution)/shard_map/ppermute | solution.py:384
  97.6 4.9 %collective-permute-start.12 = (f32[256,128]{1,0:T(8,128)S(1)}, f32[256,128]{1,0:T(8,128)S(1)}, u32[]{:S(2)}, u32[]{:S(2)}) collective-permute-start(f32[256,128]{1,0:T(8,128)S(1)} %maximum_select_fusion.1), channel_id=1, source_target_pairs={{0,8},{1,9},{2,10},{3,11},{4,12},{5,13},{6,14},{7,15},{8,0},{9,1},... | collective-permute-start | bytes 393224 | tf_op jit(solution)/shard_map/ppermute | solution.py:384
  102.5 1.0 collective-permute-done.12
  103.6 0.6 slice_bitcast_fusion
  104.2 0.6 slice.33
  104.9 0.7 reshape.39
  (13 shorter events, 0.2 us)
Async XLA Ops:
  5.2 24.9 %collective-permute-start = (bf16[176,2048]{1,0:T(8,128)(2,1)}, bf16[176,2048]{1,0:T(8,128)(2,1)S(1)}, u32[]{:S(2)}, u32[]{:S(2)}) collective-permute-start(bf16[176,2048]{1,0:T(8,128)(2,1)} %get-tuple-element.37), channel_id=1, source_target_pairs={{0,1},{1,2},{2,3},{3,4},{4,5},{5,6},{6,7},{7,8},{8,9},{9,10},{10,1... | collective-permute-start | bytes 2162696 | tf_op jit(solution)/shard_map/ppermute | solution.py:379
  9.5 18.1 %collective-permute-start.1 = (bf16[160,2048]{1,0:T(8,128)(2,1)}, bf16[160,2048]{1,0:T(8,128)(2,1)S(1)}, u32[]{:S(2)}, u32[]{:S(2)}) collective-permute-start(bf16[160,2048]{1,0:T(8,128)(2,1)} %get-tuple-element.38), channel_id=1, source_target_pairs={{1,0},{2,1},{3,2},{4,3},{5,4},{6,5},{7,6},{8,7},{9,8},{10,9},{11,1... | collective-permute-start | bytes 1966088 | tf_op jit(solution)/shard_map/ppermute | solution.py:379
  27.7 2.4 %copy-start.2 = (bf16[160,2048]{1,0:T(8,128)(2,1)}, bf16[160,2048]{1,0:T(8,128)(2,1)S(1)}, u32[]{:S(2)}) copy-start(bf16[160,2048]{1,0:T(8,128)(2,1)S(1)} %collective-permute-done.1.from_right) | copy-start | bytes 1966084
  30.1 0.9 copy-start.1
  53.3 1.4 %collective-permute-start.2 = (f32[256,128]{1,0:T(8,128)S(1)}, f32[256,128]{1,0:T(8,128)S(1)}, u32[]{:S(2)}, u32[]{:S(2)}) collective-permute-start(f32[256,128]{1,0:T(8,128)S(1)} %bitcast.15), channel_id=1, source_target_pairs={{0,8},{1,9},{2,10},{3,11},{4,12},{5,13},{6,14},{7,15},{8,0},{9,1},... | collective-permute-start | bytes 393224 | tf_op jit(solution)/shard_map/ppermute | solution.py:384
  54.8 8.4 %collective-permute-start.3 = (f32[128,128]{1,0:T(8,128)S(1)}, f32[128,128]{1,0:T(8,128)S(1)}, u32[]{:S(2)}, u32[]{:S(2)}) collective-permute-start(f32[128,128]{1,0:T(8,128)S(1)} %slice_select_fusion.2), channel_id=1, source_target_pairs={{0,16},{1,17},{2,18},{3,19},{4,20},{5,21},{6,22},{7,23},{8,24},{9,... | collective-permute-start | bytes 196616 | tf_op jit(solution)/shard_map/ppermute | solution.py:384
  57.0 11.5 %collective-permute-start.5 = (bf16[48,2048]{1,0:T(8,128)(2,1)}, bf16[48,2048]{1,0:T(8,128)(2,1)S(1)}, u32[]{:S(2)}, u32[]{:S(2)}) collective-permute-start(bf16[48,2048]{1,0:T(8,128)(2,1)} %get-tuple-element.42), channel_id=1, source_target_pairs={{1,0},{2,1},{3,2},{4,3},{5,4},{6,5},{7,6},{8,7},{9,8},{10,9},{11,1... | collective-permute-start | bytes 589832 | tf_op jit(solution)/shard_map/ppermute | solution.py:379
  63.2 5.4 %collective-permute-start.4 = (f32[128,128]{1,0:T(8,128)S(1)}, f32[128,128]{1,0:T(8,128)S(1)}, u32[]{:S(2)}, u32[]{:S(2)}) collective-permute-start(f32[128,128]{1,0:T(8,128)S(1)} %select_add_fusion), channel_id=1, source_target_pairs={{0,48},{1,49},{2,50},{3,51},{4,52},{5,53},{6,54},{7,55},{8,56},{9,... | collective-permute-start | bytes 196616 | tf_op jit(solution)/shard_map/ppermute | solution.py:384
  68.6 0.7 copy-start
  68.6 4.6 %collective-permute-start.6 = (f32[128,128]{1,0:T(8,128)S(1)}, f32[128,128]{1,0:T(8,128)S(1)}, u32[]{:S(2)}, u32[]{:S(2)}) collective-permute-start(f32[128,128]{1,0:T(8,128)S(1)} %add.46), channel_id=1, source_target_pairs={{0,64},{1,65},{2,66},{3,67},{4,68},{5,69},{6,70},{7,71},{8,72},{9,... | collective-permute-start | bytes 196616 | tf_op jit(solution)/shard_map/ppermute | solution.py:384
  73.2 5.8 %collective-permute-start.7 = (f32[128,128]{1,0:T(8,128)S(1)}, f32[128,128]{1,0:T(8,128)S(1)}, u32[]{:S(2)}, u32[]{:S(2)}) collective-permute-start(f32[128,128]{1,0:T(8,128)S(1)} %add.47), channel_id=1, source_target_pairs={{0,192},{1,193},{2,194},{3,195},{4,196},{5,197},{6,198},{7,199},{8... | collective-permute-start | bytes 196616 | tf_op jit(solution)/shard_map/ppermute | solution.py:384
  79.0 4.0 %collective-permute-start.8 = (f32[128,128]{1,0:T(8,128)S(1)}, f32[128,128]{1,0:T(8,128)S(1)}, u32[]{:S(2)}, u32[]{:S(2)}) collective-permute-start(f32[128,128]{1,0:T(8,128)S(1)} %add.48), channel_id=1, source_target_pairs={{0,1},{1,0},{2,3},{3,2},{4,5},{5,4},{6,7},{7,6},{8,9},{9,8},{10,11... | collective-permute-start | bytes 196616 | tf_op jit(solution)/shard_map/ppermute | solution.py:384
  83.0 5.6 %collective-permute-start.9 = (f32[128,128]{1,0:T(8,128)S(1)}, f32[128,128]{1,0:T(8,128)S(1)}, u32[]{:S(2)}, u32[]{:S(2)}) collective-permute-start(f32[128,128]{1,0:T(8,128)S(1)} %add.49), channel_id=1, source_target_pairs={{0,2},{1,3},{2,0},{3,1},{4,6},{5,7},{6,4},{7,5},{8,10},{9,11},{10,... | collective-permute-start | bytes 196616 | tf_op jit(solution)/shard_map/ppermute | solution.py:384
  88.6 5.7 %collective-permute-start.10 = (f32[128,128]{1,0:T(8,128)S(1)}, f32[128,128]{1,0:T(8,128)S(1)}, u32[]{:S(2)}, u32[]{:S(2)}) collective-permute-start(f32[128,128]{1,0:T(8,128)S(1)} %add.50), channel_id=1, source_target_pairs={{0,6},{1,7},{2,4},{3,5},{4,2},{5,3},{6,0},{7,1},{8,14},{9,15},{10,... | collective-permute-start | bytes 196616 | tf_op jit(solution)/shard_map/ppermute | solution.py:384
  94.4 3.3 %collective-permute-start.11 = (f32[128,128]{1,0:T(8,128)S(1)}, f32[128,128]{1,0:T(8,128)S(1)}, u32[]{:S(2)}, u32[]{:S(2)}) collective-permute-start(f32[128,128]{1,0:T(8,128)S(1)} %add.51), channel_id=1, source_target_pairs={{0,16},{1,17},{2,18},{3,19},{4,20},{5,21},{6,22},{7,23},{8,24},{9,... | collective-permute-start | bytes 196616 | tf_op jit(solution)/shard_map/ppermute | solution.py:384
  97.6 5.9 %collective-permute-start.12 = (f32[256,128]{1,0:T(8,128)S(1)}, f32[256,128]{1,0:T(8,128)S(1)}, u32[]{:S(2)}, u32[]{:S(2)}) collective-permute-start(f32[256,128]{1,0:T(8,128)S(1)} %maximum_select_fusion.1), channel_id=1, source_target_pairs={{0,8},{1,9},{2,10},{3,11},{4,12},{5,13},{6,14},{7,15},{8,0},{9,1},... | collective-permute-start | bytes 393224 | tf_op jit(solution)/shard_map/ppermute | solution.py:384

commit v2 on v1

--- a/solution.py
+++ b/solution.py
@@ -15,6 +15,10 @@
 EDGE = 16
 RUN = 32
 PART_ROWS = 32
+PER_STEP = 2
+WIDE = PER_STEP * LANES
+STEP = 64
+TAIL = 8
 AXES = ("seg", "ctx")
 MIB = 1024 * 1024
 F32 = jnp.float32
@@ -67,9 +71,9 @@
             act_k = causal(kf, 1, taps, EDGE + r, 64)
             act_v = causal(vf, 2, taps, EDGE + r, 64)
             right[r : r + 64, ls] = (act_k * act_v).astype(BF16)
-        right[TAPS : TAPS + EDGE, ls] = k[TAPS - EDGE :, ls]
-        right[TAPS + EDGE : TAPS + 2 * EDGE, ls] = v[TAPS - EDGE :, ls]
-        right[TAPS + 2 * EDGE : TAPS + 3 * EDGE, ls] = q_tail[:, ls]
+        tails = [kf[TAPS + EDGE - TAIL :], vf[TAPS + EDGE - TAIL :]]
+        tails += [q_tail[:, ls].astype(F32)[EDGE - TAIL :], jnp.zeros((TAIL, LANES), F32)]
+        right[TAPS:, ls] = jnp.concatenate(tails, axis=0).astype(BF16)
         for r, count in ((EDGE, 48), (EDGE + 48, 64)):
             act_q = causal(qf, 0, taps, r, count)
             grad = g[r : r + count, ls].astype(F32) * weight_of(rep[r : r + count])
@@ -107,131 +111,188 @@
         bwd[g, :, TAPS:] = jnp.where(col < row, ring, 0.0).astype(BF16)
 
 
+def together(*jobs):
+    jobs = list(jobs)
+    while jobs:
+        for job in list(jobs):
+            if next(job, jobs) is jobs:
+                jobs.remove(job)
+
+
+def short_sums(sums, grads, frame, start):
+    wide = grads.astype(F32)
+    count = wide.shape[0]
+    for j in range(SHORT):
+        both = wide * frame[pl.ds(start - j, count)]
+        sums[j] = sums[j] + jnp.sum(both.reshape(count // 8, 8, LANES), axis=0)
+
+
+def own_groups(prod, r, count):
+    block, at = divmod(r, TAPS)
+    ls = slice(block * LANES, (block + 1) * LANES)
+    lane = lax.broadcasted_iota(jnp.int32, (count, LANES), 1) // GROUP
+    total = prod[at : at + count, ls]
+    for n in range(1, PER_TILE):
+        total = jnp.where(lane == n, prod[n * TAPS + at : n * TAPS + at + count, ls], total)
+    return total
+
+
+class Tile:
+    def __init__(self, refs, taps, skip, rep, scratch):
+        (self.q, self.k, self.v, self.g, self.fwd, self.bwd, self.from_left, self.from_right,
+         self.out, self.gq, self.gk, self.gv, self.heads, self.part) = refs
+        (self.qf, self.kf, self.vf, self.xs, self.gs, self.act_q, self.act_k, self.act_v,
+         self.prod_p, self.prod_f, self.prod_b, self.diag) = scratch
+        self.taps, self.skip, self.rep = taps, skip, rep
+        self.rows = self.q.shape[0]
+        self.sums = [[jnp.zeros((8, LANES), F32)] * SHORT for _ in range(3)]
+        self.skip_sum = jnp.zeros((8, LANES), F32)
+
+    def activations(self):
+        rows, taps, qf, kf, vf = self.rows, self.taps, self.qf, self.kf, self.vf
+        from_left, from_right = self.from_left, self.from_right
+        qf[EDGE : EDGE + rows] = self.q[...].astype(F32)
+        kf[EDGE : EDGE + rows] = self.k[...].astype(F32)
+        vf[EDGE : EDGE + rows] = self.v[...].astype(F32)
+        tails = from_left[TAPS:].astype(F32)
+        kf[EDGE - TAIL : EDGE] = tails[:TAIL]
+        vf[EDGE - TAIL : EDGE] = tails[TAIL : 2 * TAIL]
+        qf[EDGE - TAIL : EDGE] = tails[2 * TAIL : 3 * TAIL]
+        qf[EDGE + rows :] = from_right[TAPS - EDGE : TAPS].astype(F32)
+        self.xs[:TAPS] = from_left[:TAPS]
+        self.gs[rows + EDGE :] = from_right[: TAPS - EDGE]
+        grad = from_right[TAPS : TAPS + EDGE].astype(F32) * weight_of(
+            from_right[TAPS + EDGE : TAPS + 2 * EDGE].astype(F32)
+        )
+        a_q = causal(qf, 0, taps, EDGE + rows, EDGE)
+        self.gs[rows : rows + EDGE] = (grad * a_q).astype(BF16)
+        for r in range(0, rows, STEP):
+            a_q = causal(qf, 0, taps, EDGE + r, STEP)
+            a_k = causal(kf, 1, taps, EDGE + r, STEP)
+            a_v = causal(vf, 2, taps, EDGE + r, STEP)
+            self.act_q[r : r + STEP] = a_q
+            self.act_k[r : r + STEP] = a_k
+            self.act_v[r : r + STEP] = a_v
+            gated = (a_k * a_v).astype(BF16)
+            self.xs[TAPS + r : TAPS + r + STEP] = gated
+            grad = self.g[r : r + STEP].astype(F32) * weight_of(self.rep[r : r + STEP])
+            scaled = (grad * a_q).astype(BF16)
+            self.gs[r : r + STEP] = scaled
+            both = scaled.astype(F32) * gated.astype(F32)
+            self.skip_sum = self.skip_sum + jnp.sum(both.reshape(STEP // 8, 8, LANES), axis=0)
+            yield
+
+    def window(self, rows_of):
+        return jnp.concatenate([rows_of[: 2 * TAPS], rows_of[TAPS:]], axis=1)
+
+    def filter_products(self, table, rows_of, prod):
+        whole = table[...].reshape(PER_TILE * TAPS, 2 * TAPS)
+        prod[...] = jnp.dot(whole, self.window(rows_of), preferred_element_type=F32)
+        yield
+
+    def forward_products(self):
+        return self.filter_products(self.fwd, self.xs, self.prod_f)
+
+    def backward_products(self):
+        return self.filter_products(self.bwd, self.gs, self.prod_b)
+
+    def pair_products(self):
+        windows = self.window(self.gs)
+        own_x = jnp.concatenate([self.xs[TAPS : 2 * TAPS], self.xs[2 * TAPS :]], axis=1)
+        lane = lax.broadcasted_iota(jnp.int32, own_x.shape, 1) % LANES // GROUP
+        masked = jnp.concatenate(
+            [jnp.where(lane == n, own_x, jnp.zeros_like(own_x)) for n in range(PER_TILE)],
+            axis=0,
+        )
+        self.prod_p[...] = lax.dot_general(
+            masked, windows, (((1,), (1,)), ((), ())), preferred_element_type=F32
+        )
+        yield
+
+    def query_side(self):
+        for r in range(0, self.rows, STEP):
+            gated = self.xs[TAPS + r : TAPS + r + STEP].astype(F32)
+            filtered = own_groups(self.prod_f, r, STEP) + self.skip * gated
+            self.out[r : r + STEP] = (self.act_q[r : r + STEP] * filtered).astype(BF16)
+            grad = self.g[r : r + STEP].astype(F32) * weight_of(self.rep[r : r + STEP])
+            grads = (grad * filtered).astype(BF16)
+            self.gq[r : r + STEP] = grads
+            short_sums(self.sums[0], grads, self.qf, EDGE + r)
+            yield
+
+    def key_value_side(self):
+        for r in range(0, self.rows, STEP):
+            scaled = self.gs[r : r + STEP].astype(F32)
+            grad_gated = self.skip * scaled + own_groups(self.prod_b, r, STEP)
+            grads = (grad_gated * self.act_v[r : r + STEP]).astype(BF16)
+            self.gk[r : r + STEP] = grads
+            short_sums(self.sums[1], grads, self.kf, EDGE + r)
+            grads = (grad_gated * self.act_k[r : r + STEP]).astype(BF16)
+            self.gv[r : r + STEP] = grads
+            short_sums(self.sums[2], grads, self.vf, EDGE + r)
+            yield
+
+    def diagonals(self):
+        sub = lax.broadcasted_iota(jnp.int32, (8, LANES), 0)
+        lane = lax.broadcasted_iota(jnp.int32, (8, LANES), 1)
+        prod = self.prod_p
+        for n in range(PER_TILE):
+            total = jnp.zeros((8, LANES), F32)
+            for m in range(TAPS // 8):
+                r = n * TAPS + m * 8
+                ring = jnp.where(
+                    lane >= sub + m * 8, prod[r : r + 8, :LANES], prod[r : r + 8, LANES:]
+                )
+                total = total + (pltpu.roll(ring, LANES - 8 * m, 1) if m else ring)
+            self.diag[n * 8 : n * 8 + 8] = total
+            if n % 2:
+                yield
+        lines = self.diag[pl.ds(0, PER_TILE, stride=8)]
+        for r in range(1, 8):
+            row = self.diag[pl.ds(r, PER_TILE, stride=8)]
+            lines = lines + pltpu.roll(row, LANES - r, 1)
+        self.part[:PER_TILE] = lines
+
+    def finish(self):
+        self.heads[:EDGE] = self.gq[:EDGE]
+        self.heads[EDGE : 2 * EDGE] = self.gk[:EDGE]
+        self.heads[2 * EDGE :] = self.gv[:EDGE]
+        every = self.sums[0] + self.sums[1] + self.sums[2] + [self.skip_sum]
+        lines = [jnp.sum(one, axis=0, keepdims=True) for one in every]
+        lines.append(jnp.zeros((PART_ROWS - PER_TILE - len(lines), LANES), F32))
+        self.part[PER_TILE:] = jnp.concatenate(lines, axis=0)
+        yield
+
+
 def main_kernel(
     ids, q, k, v, g, taps_ref, skip_ref, fwd, bwd, from_left, from_right,
-    out, gq, gk, gv, heads, part,
-    qf, kf, vf, xs, gs, act_q, act_k, act_v, prod_p, prod_f, prod_b, diag, rep,
+    out, gq, gk, gv, heads, part, rep, *scratch,
 ):
-    tile = pl.program_id(0)
-
-    @pl.when(tile == 0)
+    @pl.when(pl.program_id(0) == 0)
     def _():
         mark_repeats(ids, rep)
 
-    rows = q.shape[0]
-    step = 64
-    taps = taps_ref[...]
-    skip = skip_ref[...]
-    qf[EDGE : EDGE + rows] = q[...].astype(F32)
-    kf[EDGE : EDGE + rows] = k[...].astype(F32)
-    vf[EDGE : EDGE + rows] = v[...].astype(F32)
-    kf[:EDGE] = from_left[TAPS : TAPS + EDGE].astype(F32)
-    vf[:EDGE] = from_left[TAPS + EDGE : TAPS + 2 * EDGE].astype(F32)
-    qf[:EDGE] = from_left[TAPS + 2 * EDGE : TAPS + 3 * EDGE].astype(F32)
-    qf[EDGE + rows :] = from_right[TAPS - EDGE : TAPS].astype(F32)
-    xs[:TAPS] = from_left[:TAPS]
-    gs[rows + EDGE :] = from_right[: TAPS - EDGE]
-
-    skip_sum = jnp.zeros((8, LANES), F32)
-    for r in range(0, rows, step):
-        a_q = causal(qf, 0, taps, EDGE + r, step)
-        a_k = causal(kf, 1, taps, EDGE + r, step)
-        a_v = causal(vf, 2, taps, EDGE + r, step)
-        act_q[r : r + step] = a_q
-        act_k[r : r + step] = a_k
-        act_v[r : r + step] = a_v
-        gated = (a_k * a_v).astype(BF16)
-        xs[TAPS + r : TAPS + r + step] = gated
-        grad = g[r : r + step].astype(F32) * weight_of(rep[r : r + step])
-        scaled = (grad * a_q).astype(BF16)
-        gs[r : r + step] = scaled
-        both = scaled.astype(F32) * gated.astype(F32)
-        skip_sum = skip_sum + jnp.sum(both.reshape(step // 8, 8, LANES), axis=0)
-    a_q = causal(qf, 0, taps, EDGE + rows, EDGE)
-    grad = from_right[TAPS : TAPS + EDGE].astype(F32) * weight_of(
-        from_right[TAPS + EDGE : TAPS + 2 * EDGE].astype(F32)
-    )
-    gs[rows : rows + EDGE] = (grad * a_q).astype(BF16)
-
-    lane_group = lax.broadcasted_iota(jnp.int32, (8, LANES), 1) // GROUP
-    group2 = jnp.concatenate([lane_group, lane_group], axis=1)
-    win_g = jnp.concatenate([gs[: 2 * TAPS], gs[TAPS:]], axis=1)
-    own_x = jnp.concatenate([xs[TAPS : 2 * TAPS], xs[2 * TAPS :]], axis=1)
-
-    def spread(table, windows, prod):
-        prod[...] = jnp.dot(
-            table[...].reshape(PER_TILE * TAPS, 2 * TAPS), windows, preferred_element_type=F32
+    each = len(scratch) // PER_STEP
+    tiles = []
+    for lt in range(PER_STEP):
+        ls = slice(lt * LANES, (lt + 1) * LANES)
+        tables = slice(lt * PER_TILE, (lt + 1) * PER_TILE)
+        refs = [ref.at[:, ls] for ref in (q, k, v, g)]
+        refs += [fwd.at[tables], bwd.at[tables]]
+        refs += [ref.at[:, ls] for ref in (from_left, from_right, out, gq, gk, gv, heads)]
+        refs += [part.at[lt]]
+        own = scratch[lt * each : (lt + 1) * each]
+        tiles.append(Tile(refs, taps_ref[:, :, ls], skip_ref[:, ls], rep, own))
+    together(tiles[0].activations())
+    for n, tile in enumerate(tiles):
+        following = tiles[n + 1 : n + 2]
+        if n == 0:
+            together(tile.forward_products(), *[t.activations() for t in following])
+        together(tile.backward_products(), tile.query_side())
+        together(tile.pair_products(), tile.key_value_side())
+        together(
+            tile.diagonals(), *[t.forward_products() for t in following], tile.finish()
         )
-
-    def gather(prod, r, count):
-        block, at = divmod(r, TAPS)
-        ls = slice(block * LANES, (block + 1) * LANES)
-        picks = jnp.broadcast_to(lane_group[0:1], (count, LANES))
-        total = prod[at : at + count, ls]
-        for n in range(1, PER_TILE):
-            total = jnp.where(picks == n, prod[n * TAPS + at : n * TAPS + at + count, ls], total)
-        return total
-
-    def short_sums(sums, grads, frame, r):
-        wide_grads = grads.astype(F32)
-        return [
-            total
-            + jnp.sum(
-                (wide_grads * frame[pl.ds(EDGE + r - j, step)]).reshape(step // 8, 8, LANES),
-                axis=0,
-            )
-            for j, total in enumerate(sums)
-        ]
-
-    zeros = [jnp.zeros((8, LANES), F32)] * SHORT
-    sums_q, sums_k, sums_v = zeros, zeros, zeros
-    win_x = jnp.concatenate([xs[: 2 * TAPS], xs[TAPS:]], axis=1)
-    spread(fwd, win_x, prod_f)
-    spread(bwd, win_g, prod_b)
-    wide = jnp.broadcast_to(group2[0:1], (TAPS, 2 * LANES))
-    masked = jnp.concatenate(
-        [jnp.where(wide == n, own_x, jnp.zeros_like(own_x)) for n in range(PER_TILE)], axis=0
-    )
-    prod_p[...] = lax.dot_general(
-        masked, win_g, (((1,), (1,)), ((), ())), preferred_element_type=F32
-    )
-    for r in range(0, rows, step):
-        filtered = gather(prod_f, r, step) + skip * xs[TAPS + r : TAPS + r + step].astype(F32)
-        out[r : r + step] = (act_q[r : r + step] * filtered).astype(BF16)
-        grad = g[r : r + step].astype(F32) * weight_of(rep[r : r + step])
-        grads = (grad * filtered).astype(BF16)
-        gq[r : r + step] = grads
-        sums_q = short_sums(sums_q, grads, qf, r)
-    for r in range(0, rows, step):
-        grad_gated = skip * gs[r : r + step].astype(F32) + gather(prod_b, r, step)
-        grads = (grad_gated * act_v[r : r + step]).astype(BF16)
-        gk[r : r + step] = grads
-        sums_k = short_sums(sums_k, grads, kf, r)
-        grads = (grad_gated * act_k[r : r + step]).astype(BF16)
-        gv[r : r + step] = grads
-        sums_v = short_sums(sums_v, grads, vf, r)
-    sub = lax.broadcasted_iota(jnp.int32, (8, LANES), 0)
-    lane = lax.broadcasted_iota(jnp.int32, (8, LANES), 1)
-    for n in range(PER_TILE):
-        total = jnp.zeros((8, LANES), F32)
-        for m in range(TAPS // 8):
-            r = n * TAPS + m * 8
-            ring = jnp.where(
-                lane >= sub + m * 8, prod_p[r : r + 8, :LANES], prod_p[r : r + 8, LANES:]
-            )
-            total = total + (pltpu.roll(ring, LANES - 8 * m, 1) if m else ring)
-        diag[n * 8 : n * 8 + 8] = total
-    long_part = diag[pl.ds(0, PER_TILE, stride=8)]
-    for r in range(1, 8):
-        long_part = long_part + pltpu.roll(diag[pl.ds(r, PER_TILE, stride=8)], LANES - r, 1)
-    part[0, :PER_TILE] = long_part
-
-    heads[:EDGE] = gq[:EDGE]
-    heads[EDGE : 2 * EDGE] = gk[:EDGE]
-    heads[2 * EDGE :] = gv[:EDGE]
-    lines = [jnp.sum(s, axis=0, keepdims=True) for s in sums_q + sums_k + sums_v + [skip_sum]]
-    lines.append(jnp.zeros((PART_ROWS - PER_TILE - len(lines), LANES), F32))
-    part[0, PER_TILE:] = jnp.concatenate(lines, axis=0)
 
 
 def back_kernel(grads, heads, taps_ref, result, frame):
@@ -268,7 +329,7 @@
 
 def make_edges(ids, q, k, v, g, taps):
     rows, channels = q.shape
-    width = 512
+    width = 1024
     first = pl.BlockSpec((TAPS, width), lambda i: (0, i))
     last = pl.BlockSpec((TAPS, width), lambda i: (rows // TAPS - 1, i))
     ahead = pl.BlockSpec((EDGE, width), lambda i: ((rows - TAPS) // EDGE - 1, i))
@@ -278,9 +339,9 @@
         grid=(channels // width,),
         in_specs=[pl.BlockSpec(memory_space=pltpu.SMEM), first, first, ahead, last, ahead, last]
         + [tail, along_tile(SHORT, width)],
-        out_specs=[columns(TAPS + 3 * EDGE, width), columns(TAPS + 2 * EDGE, width)],
+        out_specs=[columns(TAPS + 2 * EDGE, width), columns(TAPS + 2 * EDGE, width)],
         out_shape=[
-            jax.ShapeDtypeStruct((TAPS + 3 * EDGE, channels), BF16),
+            jax.ShapeDtypeStruct((TAPS + 2 * EDGE, channels), BF16),
             jax.ShapeDtypeStruct((TAPS + 2 * EDGE, channels), BF16),
         ],
         scratch_shapes=[
@@ -315,23 +376,25 @@
 def make_main(ids, q, k, v, g, taps, skip, fwd, bwd, from_left, from_right):
     rows, channels = q.shape
     tiles = channels // LANES
-    wide = pl.BlockSpec((PER_TILE, TAPS, 2 * TAPS), lambda i: (i, 0, 0))
+    wide = pl.BlockSpec((PER_STEP * PER_TILE, TAPS, 2 * TAPS), lambda i: (i, 0, 0))
     big = jax.ShapeDtypeStruct((rows, channels), BF16)
     return pl.pallas_call(
         main_kernel,
-        grid=(tiles,),
+        grid=(tiles // PER_STEP,),
         in_specs=[pl.BlockSpec(memory_space=pltpu.SMEM)]
-        + [columns(rows, LANES)] * 4
-        + [along_tile(SHORT, LANES), columns(1, LANES), wide, wide]
-        + [columns(from_left.shape[0], LANES), columns(from_right.shape[0], LANES)],
-        out_specs=[columns(rows, LANES)] * 4
-        + [columns(3 * EDGE, LANES), pl.BlockSpec((1, PART_ROWS, LANES), lambda i: (i, 0, 0))],
+        + [columns(rows, WIDE)] * 4
+        + [along_tile(SHORT, WIDE), columns(1, WIDE), wide, wide]
+        + [columns(from_left.shape[0], WIDE), columns(from_right.shape[0], WIDE)],
+        out_specs=[columns(rows, WIDE)] * 4
+        + [columns(3 * EDGE, WIDE), pl.BlockSpec((PER_STEP, PART_ROWS, LANES), lambda i: (i, 0, 0))],
         out_shape=[big] * 4
         + [
             jax.ShapeDtypeStruct((3 * EDGE, channels), BF16),
             jax.ShapeDtypeStruct((tiles, PART_ROWS, LANES), F32),
         ],
-        scratch_shapes=[
+        scratch_shapes=[pltpu.VMEM((rows, LANES), F32)]
+        + PER_STEP
+        * [
             pltpu.VMEM((rows + 2 * EDGE, LANES), F32),
             pltpu.VMEM((rows + EDGE, LANES), F32),
             pltpu.VMEM((rows + EDGE, LANES), F32),
@@ -344,7 +407,6 @@
             pltpu.VMEM((PER_TILE * TAPS, 2 * TAPS), F32),
             pltpu.VMEM((PER_TILE * TAPS, 2 * TAPS), F32),
             pltpu.VMEM((PER_TILE * 8, LANES), F32),
-            pltpu.VMEM((rows, LANES), F32),
         ],
         compiler_params=params(),
         name="main",
@@ -353,7 +415,7 @@
 
 def make_back(which, grads, heads, taps):
     rows, channels = grads.shape
-    width = 512
+    width = 1024
     return pl.pallas_call(
         back_kernel,
         grid=(channels // width,),
@@ -371,6 +433,39 @@
         ),
         name="back",
     )(grads, heads, taps)
+
+
+def last_kernel(scale, which, half, other, long_grad, skip_grad, short_grad):
+    mine = which[0]
+    tiles = 2 * half.shape[0] // PART_ROWS
+    for tile in range(tiles):
+        side, at = divmod(tile, tiles // 2)
+        rows = slice(at * PART_ROWS, (at + 1) * PART_ROWS)
+        both = jnp.where(mine == side, half[rows], other[rows]) * scale
+        ls = slice(tile * LANES, (tile + 1) * LANES)
+        long_grad[tile * PER_TILE : (tile + 1) * PER_TILE] = both[:PER_TILE]
+        for i in range(3):
+            first = PER_TILE + i * SHORT
+            short_grad[i, :, ls] = both[first : first + SHORT]
+        skip_grad[ls] = both[PER_TILE + 3 * SHORT]
+
+
+def make_last(half, other, which, scale):
+    tiles = 2 * half.shape[0] // PART_ROWS
+    channels = tiles * LANES
+    return pl.pallas_call(
+        functools.partial(last_kernel, scale),
+        in_specs=[pl.BlockSpec(memory_space=pltpu.SMEM)]
+        + [pl.BlockSpec(memory_space=pltpu.VMEM)] * 2,
+        out_specs=[pl.BlockSpec(memory_space=pltpu.VMEM)] * 3,
+        out_shape=[
+            jax.ShapeDtypeStruct((tiles * PER_TILE, TAPS), F32),
+            jax.ShapeDtypeStruct((channels,), F32),
+            jax.ShapeDtypeStruct((3, SHORT, channels), F32),
+        ],
+        compiler_params=pltpu.CompilerParams(vmem_limit_bytes=4 * MIB),
+        name="last",
+    )(which.reshape(1).astype(jnp.int32), half, other)
 
 
 def from_behind(value, steps):
@@ -428,12 +523,12 @@
         value, result = lax.optimization_barrier((value + got, run(*inputs)))
         done.append(result)
     done += [run(*inputs) for run, inputs in pending]
-    for mask, high in zip(reversed(halving), reversed(mine)):
+    for mask, high in zip(halving[:0:-1], mine[:0:-1]):
         got = swap(value, mask)
         value = jnp.where(
             high, jnp.concatenate([got, value]), jnp.concatenate([value, got])
         )
-    return value, done
+    return value, swap(value, halving[0]), mine[0], done
 
 
 def per_device(
@@ -456,19 +551,11 @@
         (functools.partial(make_back, i), (grads, next_heads, short_filters))
         for i, grads in enumerate((gq, gk, gv))
     ]
-    total, (grad_query, grad_key, grad_value) = total_over_all(
+    half, other, which, (grad_query, grad_key, grad_value) = total_over_all(
         part.reshape(tiles * PART_ROWS, LANES), jobs
     )
     norm_scale = float(length * lax.axis_size("seg") * lax.axis_size("ctx")) ** (-0.5)
-    total = total.reshape(tiles, PART_ROWS, LANES) * norm_scale
-    grad_long = total[:, :PER_TILE].reshape(tiles * PER_TILE, TAPS)
-    short_lines = 3 * SHORT
-    grad_short = (
-        total[:, PER_TILE : PER_TILE + short_lines]
-        .transpose(1, 0, 2)
-        .reshape(3, SHORT, channels)
-    )
-    grad_skip = total[:, PER_TILE + short_lines].reshape(channels)
+    grad_long, grad_skip, grad_short = make_last(half, other, which, norm_scale)
     return out, grad_query, grad_key, grad_value, grad_long, grad_skip, grad_short
 
 

time: 107 us -> 100 us (0.935); the launches traced: 106 us -> 100 us
  Pallas kernels: 49.3 us -> 43.9 us
  starting transfers between devices: 36.5 us -> 40 us
  local copies, waits for them, and re-layouts: 3.11 us -> 1.27 us
  waiting for transfers between devices: 14.7 us -> 12.9 us
    ppermute x10, starting transfers between devices: 19.6 us -> 23.1 us  [swap(): return lax.ppermute(value, AXES, [(s, s ^ mask) for s in range(count)])]
    pallas_call x3, Pallas kernels: 11.8 us -> 9.22 us  [make_back(): pl.pallas_call(back_kernel, grid=(channels // width,), in_specs=[columns(...]
    pallas_call x1 -> x2, Pallas kernels: 21.4 us -> 19 us  [the longest x1 18.2 us: make_main(): pl.pallas_call(main_kernel, grid=(tiles // PER_STEP,), in_specs=[pl.Block...]
    ppermute x3, waiting for transfers between devices: 2.41 us -> 1.01 us  [from_behind(): lax.ppermute(value, AXES, [(s, s + steps) for s in range(first, last)])]
    reshape x2 -> x0, local copies, waits for them, and re-layouts: 1.34 us -> none  [the longest x1 0.7 us: per_device(): grad_short = total[:, PER_TILE:PER_TILE + short_lines].transpose(1, 0, 2)...]
  transfers between devices with their start and end apart: 13 -> 13, of which waited for: 7 -> 7; matrix products, arithmetic and copies ran while one was open for 0% -> 0% of each run, Pallas kernels for 22% -> 21%
where the time goes in v2:
time: 100 us
  Pallas kernels  43.9 us (44%)
  starting transfers between devices  40 us (40%)
  waiting for transfers between devices  12.9 us (13%)
  local copies, waits for them, and re-layouts  1.27 us (1%)
  other arithmetic  1.09 us (1%)
    ppermute x10, starting transfers between devices, swap(): return lax.ppermute(value, AXES, [(s, s ^ mask) for s in range(count)])  23.1 us
    pallas_call x1, Pallas kernels, make_main(): pl.pallas_call(main_kernel, grid=(tiles // PER_STEP,), in_specs=[pl.Block...  18.2 us
    ppermute x3, starting transfers between devices, from_behind(): lax.ppermute(value, AXES, [(s, s + steps) for s in range(first, last)])  16.9 us
    ppermute x10, waiting for transfers between devices, swap(): return lax.ppermute(value, AXES, [(s, s ^ mask) for s in range(count)])  11.9 us
    pallas_call x1, Pallas kernels, make_tables(): pl.pallas_call(tables_kernel, grid=(groups // PER_TILE,), in_specs=[fixed...  11.7 us
    pallas_call x3, Pallas kernels, make_back(): pl.pallas_call(back_kernel, grid=(channels // width,), in_specs=[columns(...  9.22 us
    pallas_call x1, Pallas kernels, make_edges(): pl.pallas_call(edges_kernel, grid=(channels // width,), in_specs=[pl.Bloc...  4.1 us
  transfers between devices with their start and end apart: 13, of which 7 were waited for; matrix products, arithmetic and copies ran while one was open for 0% of the time, Pallas kernels for 21%

profile of v2, /device:TPU:1, one launch (start us, length us, event | category | flops | bytes accessed | tf_op | source)
XLA Modules:
  0.0 100.0 jit_solution(574503668606893661)
XLA Ops:
  0.6 4.1 %edges.1 = (bf16[160,2048]{1,0:T(8,128)(2,1)}, bf16[160,2048]{1,0:T(8,128)(2,1)}) custom-call(s32[256]{0:T(256)} %ids.3, bf16[256,2048]{1,0:T(8,128)(2,1)} %q.3, bf16[256,2048]{1,0:T(8,128)(2,1)} %g.3, bf16[256,2048]{1,0:T(8,128)(2,1)} %k.3, bf16[256,2048]{1,0:T(8,128)(2,1)} %k.3, bf16[256,2048]{1,0:T(8,128)(2,1)} %v.3, bf16[256,2048]{1,0:T(8,128)(2,1)} %v.3, ...), custom_call_target="tpu_custom_call" | custom-call | tf_op jit(solution)/shard_map/edges/pallas_call | solution.py:337
  4.7 4.4 %collective-permute-start = (bf16[160,2048]{1,0:T(8,128)(2,1)}, bf16[160,2048]{1,0:T(8,128)(2,1)S(1)}, u32[]{:S(2)}, u32[]{:S(2)}) collective-permute-start(bf16[160,2048]{1,0:T(8,128)(2,1)} %get-tuple-element.40), channel_id=1, source_target_pairs={{0,1},{1,2},{2,3},{3,4},{4,5},{5,6},{6,7},{7,8},{8,9},{9,10},{10,1... | collective-permute-start | bytes 1966088 | tf_op jit(solution)/shard_map/ppermute | solution.py:474
  9.1 6.4 %collective-permute-start.1 = (bf16[160,2048]{1,0:T(8,128)(2,1)}, bf16[160,2048]{1,0:T(8,128)(2,1)S(1)}, u32[]{:S(2)}, u32[]{:S(2)}) collective-permute-start(bf16[160,2048]{1,0:T(8,128)(2,1)} %get-tuple-element.41), channel_id=1, source_target_pairs={{1,0},{2,1},{3,2},{4,3},{5,4},{6,5},{7,6},{8,7},{9,8},{10,9},{11,1... | collective-permute-start | bytes 1966088 | tf_op jit(solution)/shard_map/ppermute | solution.py:474
  15.6 11.7 %tables.1 = (bf16[128,128,256]{2,1,0:T(8,128)(2,1)}, bf16[128,128,256]{2,1,0:T(8,128)(2,1)}) custom-call(bf16[128,128]{1,0:T(8,128)(2,1)} %taps.1), custom_call_target="tpu_custom_call" | custom-call | bytes 67108864 | tf_op jit(solution)/shard_map/tables/pallas_call | solution.py:361
  27.2 1.0 %collective-permute-done.from_left = bf16[160,2048]{1,0:T(8,128)(2,1)S(1)} collective-permute-done((bf16[160,2048]{1,0:T(8,128)(2,1)}, bf16[160,2048]{1,0:T(8,128)(2,1)S(1)}, u32[]{:S(2)}, u32[]{:S(2)}) %collective-permute-start) | collective-permute-done | bytes 655392 | tf_op jit(solution)/shard_map/ppermute | solution.py:474
  28.2 0.0 copy-start.1
  28.2 0.0 collective-permute-done.1.from_right
  28.2 0.0 copy-start.2
  28.2 0.8 copy-done.1
  29.1 0.2 copy-done.2
  29.3 18.2 %main.1 = (bf16[256,2048]{1,0:T(8,128)(2,1)}, bf16[256,2048]{1,0:T(8,128)(2,1)}, bf16[256,2048]{1,0:T(8,128)(2,1)}, bf16[256,2048]{1,0:T(8,128)(2,1)}, bf16[48,2048]{1,0:T(8,128)(2,1)}, /*index=5*/f32[16,32,128]{2,1,0:T(8,128)}) custom-call(s32[256]{0:T(256)} %ids.3, bf16[256,2048]{1,0:T(8,128)(2,1)} %q.3, bf16[256,2048]{1,0:T(8,128)(2,1)} %k.3, ...), custom_call_target="tpu_custom_call" | custom-call | tf_op jit(solution)/shard_map/main/pallas_call | solution.py:381
  47.5 1.0 slice_select_fusion.1
  48.5 0.2 collective-permute-start.2
  48.7 1.3 %collective-permute-done.2 = f32[256,128]{1,0:T(8,128)S(1)} collective-permute-done((f32[256,128]{1,0:T(8,128)S(1)}, f32[256,128]{1,0:T(8,128)S(1)}, u32[]{:S(2)}, u32[]{:S(2)}) %collective-permute-start.2) | collective-permute-done | bytes 131104 | tf_op jit(solution)/shard_map/ppermute | solution.py:479
  50.0 3.2 %collective-permute-start.3 = (f32[128,128]{1,0:T(8,128)S(1)}, f32[128,128]{1,0:T(8,128)S(1)}, u32[]{:S(2)}, u32[]{:S(2)}) collective-permute-start(f32[128,128]{1,0:T(8,128)S(1)} %slice_select_fusion.2), channel_id=1, source_target_pairs={{0,16},{1,17},{2,18},{3,19},{4,20},{5,21},{6,22},{7,23},{8,24},{9,... | collective-permute-start | bytes 196616 | tf_op jit(solution)/shard_map/ppermute | solution.py:479
  53.2 6.1 %collective-permute-start.5 = (bf16[48,2048]{1,0:T(8,128)(2,1)}, bf16[48,2048]{1,0:T(8,128)(2,1)S(1)}, u32[]{:S(2)}, u32[]{:S(2)}) collective-permute-start(bf16[48,2048]{1,0:T(8,128)(2,1)} %get-tuple-element.45), channel_id=1, source_target_pairs={{1,0},{2,1},{3,2},{4,3},{5,4},{6,5},{7,6},{8,7},{9,8},{10,9},{11,1... | collective-permute-start | bytes 589832 | tf_op jit(solution)/shard_map/ppermute | solution.py:474
  59.3 0.0 collective-permute-done.3
  59.4 1.6 %collective-permute-start.4 = (f32[128,128]{1,0:T(8,128)S(1)}, f32[128,128]{1,0:T(8,128)S(1)}, u32[]{:S(2)}, u32[]{:S(2)}) collective-permute-start(f32[128,128]{1,0:T(8,128)S(1)} %select_add_fusion), channel_id=1, source_target_pairs={{0,48},{1,49},{2,50},{3,51},{4,52},{5,53},{6,54},{7,55},{8,56},{9,... | collective-permute-start | bytes 196616 | tf_op jit(solution)/shard_map/ppermute | solution.py:479
  61.0 3.7 %collective-permute-done.4 = f32[128,128]{1,0:T(8,128)S(1)} collective-permute-done((f32[128,128]{1,0:T(8,128)S(1)}, f32[128,128]{1,0:T(8,128)S(1)}, u32[]{:S(2)}, u32[]{:S(2)}) %collective-permute-start.4) | collective-permute-done | bytes 65568 | tf_op jit(solution)/shard_map/ppermute | solution.py:479
  64.7 0.0 collective-permute-done.5.heads
  64.7 0.0 copy-start
  64.7 0.4 collective-permute-start.6
  65.2 0.2 copy-done
  65.4 3.1 %back.3 = bf16[256,2048]{1,0:T(8,128)(2,1)} custom-call(bf16[256,2048]{1,0:T(8,128)(2,1)} %get-tuple-element.47.grads, bf16[48,2048]{1,0:T(8,128)(2,1)} %copy-done, f32[3,7,2048]{2,1,0:T(8,128)} %taps_ref.6), custom_call_target="tpu_custom_call" | custom-call | flops 7340032 | bytes 4194304 | tf_op jit(solution)/shard_map/back/pallas_call | solution.py:419
  68.5 0.0 collective-permute-done.6
  68.5 1.9 %collective-permute-start.7 = (f32[128,128]{1,0:T(8,128)S(1)}, f32[128,128]{1,0:T(8,128)S(1)}, u32[]{:S(2)}, u32[]{:S(2)}) collective-permute-start(f32[128,128]{1,0:T(8,128)S(1)} %add.47), channel_id=1, source_target_pairs={{0,192},{1,193},{2,194},{3,195},{4,196},{5,197},{6,198},{7,199},{8... | collective-permute-start | bytes 196616 | tf_op jit(solution)/shard_map/ppermute | solution.py:479
  70.4 3.1 %back.4 = bf16[256,2048]{1,0:T(8,128)(2,1)} custom-call(bf16[256,2048]{1,0:T(8,128)(2,1)} %get-tuple-element.54.grads, bf16[48,2048]{1,0:T(8,128)(2,1)} %copy-done, f32[3,7,2048]{2,1,0:T(8,128)} %taps_ref.6), custom_call_target="tpu_custom_call" | custom-call | flops 7340032 | bytes 4194304 | tf_op jit(solution)/shard_map/back/pallas_call | solution.py:419
  73.4 0.0 collective-permute-done.7
  73.5 0.1 collective-permute-start.8
  73.6 3.1 %back.5 = bf16[256,2048]{1,0:T(8,128)(2,1)} custom-call(bf16[256,2048]{1,0:T(8,128)(2,1)} %get-tuple-element.61.grads, bf16[48,2048]{1,0:T(8,128)(2,1)} %copy-done, f32[3,7,2048]{2,1,0:T(8,128)} %taps_ref.6), custom_call_target="tpu_custom_call" | custom-call | flops 7340032 | bytes 4194304 | tf_op jit(solution)/shard_map/back/pallas_call | solution.py:419
  76.7 0.0 collective-permute-done.8
  76.7 3.2 %collective-permute-start.9 = (f32[128,128]{1,0:T(8,128)S(1)}, f32[128,128]{1,0:T(8,128)S(1)}, u32[]{:S(2)}, u32[]{:S(2)}) collective-permute-start(f32[128,128]{1,0:T(8,128)S(1)} %add.49), channel_id=1, source_target_pairs={{0,2},{1,3},{2,0},{3,1},{4,6},{5,7},{6,4},{7,5},{8,10},{9,11},{10,... | collective-permute-start | bytes 196616 | tf_op jit(solution)/shard_map/ppermute | solution.py:479
  79.9 2.4 %collective-permute-done.9 = f32[128,128]{1,0:T(8,128)S(1)} collective-permute-done((f32[128,128]{1,0:T(8,128)S(1)}, f32[128,128]{1,0:T(8,128)S(1)}, u32[]{:S(2)}, u32[]{:S(2)}) %collective-permute-start.9) | collective-permute-done | bytes 65568 | tf_op jit(solution)/shard_map/ppermute | solution.py:479
  82.3 3.4 %collective-permute-start.10 = (f32[128,128]{1,0:T(8,128)S(1)}, f32[128,128]{1,0:T(8,128)S(1)}, u32[]{:S(2)}, u32[]{:S(2)}) collective-permute-start(f32[128,128]{1,0:T(8,128)S(1)} %add.50), channel_id=1, source_target_pairs={{0,6},{1,7},{2,4},{3,5},{4,2},{5,3},{6,0},{7,1},{8,14},{9,15},{10,... | collective-permute-start | bytes 196616 | tf_op jit(solution)/shard_map/ppermute | solution.py:479
  85.7 1.9 %collective-permute-done.10 = f32[128,128]{1,0:T(8,128)S(1)} collective-permute-done((f32[128,128]{1,0:T(8,128)S(1)}, f32[128,128]{1,0:T(8,128)S(1)}, u32[]{:S(2)}, u32[]{:S(2)}) %collective-permute-start.10) | collective-permute-done | bytes 65568 | tf_op jit(solution)/shard_map/ppermute | solution.py:479
  87.6 1.8 %collective-permute-start.11 = (f32[128,128]{1,0:T(8,128)S(1)}, f32[128,128]{1,0:T(8,128)S(1)}, u32[]{:S(2)}, u32[]{:S(2)}) collective-permute-start(f32[128,128]{1,0:T(8,128)S(1)} %add.51), channel_id=1, source_target_pairs={{0,16},{1,17},{2,18},{3,19},{4,20},{5,21},{6,22},{7,23},{8,24},{9,... | collective-permute-start | bytes 196616 | tf_op jit(solution)/shard_map/ppermute | solution.py:479
  89.3 1.7 %collective-permute-done.11 = f32[128,128]{1,0:T(8,128)S(1)} collective-permute-done((f32[128,128]{1,0:T(8,128)S(1)}, f32[128,128]{1,0:T(8,128)S(1)}, u32[]{:S(2)}, u32[]{:S(2)}) %collective-permute-start.11) | collective-permute-done | bytes 65568 | tf_op jit(solution)/shard_map/ppermute | solution.py:479
  91.0 7.3 %collective-permute-start.12 = (f32[256,128]{1,0:T(8,128)S(1)}, f32[256,128]{1,0:T(8,128)S(1)}, u32[]{:S(2)}, u32[]{:S(2)}) collective-permute-start(f32[256,128]{1,0:T(8,128)S(1)} %maximum_select_fusion.half), channel_id=1, source_target_pairs={{0,8},{1,9},{2,10},{3,11},{4,12},{5,13},{6,14},{7,15},{8,0},{9,1},... | collective-permute-start | bytes 393224 | tf_op jit(solution)/shard_map/ppermute | solution.py:479
  98.3 1.0 collective-permute-done.12.other
  99.3 0.7 last.1
  (10 shorter events, 0.1 us)
Async XLA Ops:
  4.7 23.5 %collective-permute-start = (bf16[160,2048]{1,0:T(8,128)(2,1)}, bf16[160,2048]{1,0:T(8,128)(2,1)S(1)}, u32[]{:S(2)}, u32[]{:S(2)}) collective-permute-start(bf16[160,2048]{1,0:T(8,128)(2,1)} %get-tuple-element.40), channel_id=1, source_target_pairs={{0,1},{1,2},{2,3},{3,4},{4,5},{5,6},{6,7},{7,8},{8,9},{9,10},{10,1... | collective-permute-start | bytes 1966088 | tf_op jit(solution)/shard_map/ppermute | solution.py:474
  9.1 19.1 %collective-permute-start.1 = (bf16[160,2048]{1,0:T(8,128)(2,1)}, bf16[160,2048]{1,0:T(8,128)(2,1)S(1)}, u32[]{:S(2)}, u32[]{:S(2)}) collective-permute-start(bf16[160,2048]{1,0:T(8,128)(2,1)} %get-tuple-element.41), channel_id=1, source_target_pairs={{1,0},{2,1},{3,2},{4,3},{5,4},{6,5},{7,6},{8,7},{9,8},{10,9},{11,1... | collective-permute-start | bytes 1966088 | tf_op jit(solution)/shard_map/ppermute | solution.py:474
  28.2 0.8 copy-start.1
  28.2 1.0 %copy-start.2 = (bf16[160,2048]{1,0:T(8,128)(2,1)}, bf16[160,2048]{1,0:T(8,128)(2,1)S(1)}, u32[]{:S(2)}) copy-start(bf16[160,2048]{1,0:T(8,128)(2,1)S(1)} %collective-permute-done.1.from_right) | copy-start | bytes 1966084
  48.5 1.4 %collective-permute-start.2 = (f32[256,128]{1,0:T(8,128)S(1)}, f32[256,128]{1,0:T(8,128)S(1)}, u32[]{:S(2)}, u32[]{:S(2)}) collective-permute-start(f32[256,128]{1,0:T(8,128)S(1)} %bitcast.5), channel_id=1, source_target_pairs={{0,8},{1,9},{2,10},{3,11},{4,12},{5,13},{6,14},{7,15},{8,0},{9,1},... | collective-permute-start | bytes 393224 | tf_op jit(solution)/shard_map/ppermute | solution.py:479
  50.0 9.4 %collective-permute-start.3 = (f32[128,128]{1,0:T(8,128)S(1)}, f32[128,128]{1,0:T(8,128)S(1)}, u32[]{:S(2)}, u32[]{:S(2)}) collective-permute-start(f32[128,128]{1,0:T(8,128)S(1)} %slice_select_fusion.2), channel_id=1, source_target_pairs={{0,16},{1,17},{2,18},{3,19},{4,20},{5,21},{6,22},{7,23},{8,24},{9,... | collective-permute-start | bytes 196616 | tf_op jit(solution)/shard_map/ppermute | solution.py:479
  53.2 11.5 %collective-permute-start.5 = (bf16[48,2048]{1,0:T(8,128)(2,1)}, bf16[48,2048]{1,0:T(8,128)(2,1)S(1)}, u32[]{:S(2)}, u32[]{:S(2)}) collective-permute-start(bf16[48,2048]{1,0:T(8,128)(2,1)} %get-tuple-element.45), channel_id=1, source_target_pairs={{1,0},{2,1},{3,2},{4,3},{5,4},{6,5},{7,6},{8,7},{9,8},{10,9},{11,1... | collective-permute-start | bytes 589832 | tf_op jit(solution)/shard_map/ppermute | solution.py:474
  59.4 5.3 %collective-permute-start.4 = (f32[128,128]{1,0:T(8,128)S(1)}, f32[128,128]{1,0:T(8,128)S(1)}, u32[]{:S(2)}, u32[]{:S(2)}) collective-permute-start(f32[128,128]{1,0:T(8,128)S(1)} %select_add_fusion), channel_id=1, source_target_pairs={{0,48},{1,49},{2,50},{3,51},{4,52},{5,53},{6,54},{7,55},{8,56},{9,... | collective-permute-start | bytes 196616 | tf_op jit(solution)/shard_map/ppermute | solution.py:479
  64.7 0.7 copy-start
  64.7 3.7 %collective-permute-start.6 = (f32[128,128]{1,0:T(8,128)S(1)}, f32[128,128]{1,0:T(8,128)S(1)}, u32[]{:S(2)}, u32[]{:S(2)}) collective-permute-start(f32[128,128]{1,0:T(8,128)S(1)} %add.46), channel_id=1, source_target_pairs={{0,64},{1,65},{2,66},{3,67},{4,68},{5,69},{6,70},{7,71},{8,72},{9,... | collective-permute-start | bytes 196616 | tf_op jit(solution)/shard_map/ppermute | solution.py:479
  68.5 5.0 %collective-permute-start.7 = (f32[128,128]{1,0:T(8,128)S(1)}, f32[128,128]{1,0:T(8,128)S(1)}, u32[]{:S(2)}, u32[]{:S(2)}) collective-permute-start(f32[128,128]{1,0:T(8,128)S(1)} %add.47), channel_id=1, source_target_pairs={{0,192},{1,193},{2,194},{3,195},{4,196},{5,197},{6,198},{7,199},{8... | collective-permute-start | bytes 196616 | tf_op jit(solution)/shard_map/ppermute | solution.py:479
  73.5 3.2 %collective-permute-start.8 = (f32[128,128]{1,0:T(8,128)S(1)}, f32[128,128]{1,0:T(8,128)S(1)}, u32[]{:S(2)}, u32[]{:S(2)}) collective-permute-start(f32[128,128]{1,0:T(8,128)S(1)} %add.48), channel_id=1, source_target_pairs={{0,1},{1,0},{2,3},{3,2},{4,5},{5,4},{6,7},{7,6},{8,9},{9,8},{10,11... | collective-permute-start | bytes 196616 | tf_op jit(solution)/shard_map/ppermute | solution.py:479
  76.7 5.6 %collective-permute-start.9 = (f32[128,128]{1,0:T(8,128)S(1)}, f32[128,128]{1,0:T(8,128)S(1)}, u32[]{:S(2)}, u32[]{:S(2)}) collective-permute-start(f32[128,128]{1,0:T(8,128)S(1)} %add.49), channel_id=1, source_target_pairs={{0,2},{1,3},{2,0},{3,1},{4,6},{5,7},{6,4},{7,5},{8,10},{9,11},{10,... | collective-permute-start | bytes 196616 | tf_op jit(solution)/shard_map/ppermute | solution.py:479
  82.3 5.3 %collective-permute-start.10 = (f32[128,128]{1,0:T(8,128)S(1)}, f32[128,128]{1,0:T(8,128)S(1)}, u32[]{:S(2)}, u32[]{:S(2)}) collective-permute-start(f32[128,128]{1,0:T(8,128)S(1)} %add.50), channel_id=1, source_target_pairs={{0,6},{1,7},{2,4},{3,5},{4,2},{5,3},{6,0},{7,1},{8,14},{9,15},{10,... | collective-permute-start | bytes 196616 | tf_op jit(solution)/shard_map/ppermute | solution.py:479
  87.6 3.4 %collective-permute-start.11 = (f32[128,128]{1,0:T(8,128)S(1)}, f32[128,128]{1,0:T(8,128)S(1)}, u32[]{:S(2)}, u32[]{:S(2)}) collective-permute-start(f32[128,128]{1,0:T(8,128)S(1)} %add.51), channel_id=1, source_target_pairs={{0,16},{1,17},{2,18},{3,19},{4,20},{5,21},{6,22},{7,23},{8,24},{9,... | collective-permute-start | bytes 196616 | tf_op jit(solution)/shard_map/ppermute | solution.py:479
  91.0 8.3 %collective-permute-start.12 = (f32[256,128]{1,0:T(8,128)S(1)}, f32[256,128]{1,0:T(8,128)S(1)}, u32[]{:S(2)}, u32[]{:S(2)}) collective-permute-start(f32[256,128]{1,0:T(8,128)S(1)} %maximum_select_fusion.half), channel_id=1, source_target_pairs={{0,8},{1,9},{2,10},{3,11},{4,12},{5,13},{6,14},{7,15},{8,0},{9,1},... | collective-permute-start | bytes 393224 | tf_op jit(solution)/shard_map/ppermute | solution.py:479

commit v3 on v2

--- a/solution.py
+++ b/solution.py
@@ -280,7 +280,7 @@
         refs = [ref.at[:, ls] for ref in (q, k, v, g)]
         refs += [fwd.at[tables], bwd.at[tables]]
         refs += [ref.at[:, ls] for ref in (from_left, from_right, out, gq, gk, gv, heads)]
-        refs += [part.at[lt]]
+        refs += [part.at[pl.program_id(0) * PER_STEP + lt]]
         own = scratch[lt * each : (lt + 1) * each]
         tiles.append(Tile(refs, taps_ref[:, :, ls], skip_ref[:, ls], rep, own))
     together(tiles[0].activations())
@@ -386,11 +386,11 @@
         + [along_tile(SHORT, WIDE), columns(1, WIDE), wide, wide]
         + [columns(from_left.shape[0], WIDE), columns(from_right.shape[0], WIDE)],
         out_specs=[columns(rows, WIDE)] * 4
-        + [columns(3 * EDGE, WIDE), pl.BlockSpec((PER_STEP, PART_ROWS, LANES), lambda i: (i, 0, 0))],
+        + [columns(3 * EDGE, WIDE), pl.BlockSpec(memory_space=pltpu.VMEM)],
         out_shape=[big] * 4
         + [
             jax.ShapeDtypeStruct((3 * EDGE, channels), BF16),
-            jax.ShapeDtypeStruct((tiles, PART_ROWS, LANES), F32),
+            pltpu.VMEM((tiles, PART_ROWS, LANES), F32),
         ],
         scratch_shapes=[pltpu.VMEM((rows, LANES), F32)]
         + PER_STEP
@@ -479,6 +479,13 @@
     return lax.ppermute(value, AXES, [(s, s ^ mask) for s in range(count)])
 
 
+def joined(value, masks):
+    got = [value] + [swap(value, mask) for mask in masks]
+    while len(got) > 1:
+        got = [one + other for one, other in zip(got[::2], got[1::2])]
+    return got[0]
+
+
 def ring_masks(size):
     masks = []
     span = 1
@@ -499,7 +506,10 @@
     halving = [ctx, cores * ctx]
     doubling = [cores * ctx * m for m in ring_masks(along)]
     doubling += [cores * ctx * along * m for m in ring_masks(seg // (cores * along))]
-    doubling = [m for m in doubling if m not in halving] + ring_masks(ctx)
+    doubling = [(m,) for m in doubling if m not in halving]
+    near = ring_masks(ctx)
+    doubling += [(1, 2, 3)] if len(near) > 1 else [(m,) for m in near]
+    doubling += [(m,) for m in near[2:]]
     mine = []
     done = []
     pending = list(work)
@@ -512,15 +522,14 @@
         mine.append(high)
         got = swap(jnp.where(high, low_part, high_part), mask)
         value = jnp.where(high, high_part, low_part) + got
-    for n, mask in enumerate(doubling):
+    for n, masks in enumerate(doubling):
         job = pending.pop(0) if pending and n >= 1 else None
         if job is None:
-            value = value + swap(value, mask)
+            value = joined(value, masks)
             continue
         run, inputs = job
         value, inputs = lax.optimization_barrier((value, inputs))
-        got = swap(value, mask)
-        value, result = lax.optimization_barrier((value + got, run(*inputs)))
+        value, result = lax.optimization_barrier((joined(value, masks), run(*inputs)))
         done.append(result)
     done += [run(*inputs) for run, inputs in pending]
     for mask, high in zip(halving[:0:-1], mine[:0:-1]):

time: 100 us -> 96.1 us (0.961)
  starting transfers between devices: 40 us -> 38.3 us
  waiting for transfers between devices: 12.9 us -> 11.4 us
    ppermute x10 -> x11, starting transfers between devices: 23.1 us -> 21.4 us  [swap(): return lax.ppermute(value, AXES, [(s, s ^ mask) for s in range(count)])]
    ppermute x10 -> x11, waiting for transfers between devices: 11.9 us -> 10.4 us  [swap(): return lax.ppermute(value, AXES, [(s, s ^ mask) for s in range(count)])]
  transfers between devices with their start and end apart: 13 -> 14, of which waited for: 7 -> 7; matrix products, arithmetic and copies ran while one was open for 0% -> 0% of each run, Pallas kernels for 21% -> 22%
where the time goes in v3:
time: 96.1 us; the launch traced here: 95.8 us
  Pallas kernels  43.9 us (46%)
  starting transfers between devices  38.3 us (40%)
  waiting for transfers between devices  11.4 us (12%)
  local copies, waits for them, and re-layouts  1.27 us (1%)
    ppermute x11, starting transfers between devices, swap(): return lax.ppermute(value, AXES, [(s, s ^ mask) for s in range(count)])  21.4 us
    pallas_call x1, Pallas kernels, make_main(): pl.pallas_call(main_kernel, grid=(tiles // PER_STEP,), in_specs=[pl.Block...  18.2 us
    ppermute x3, starting transfers between devices, from_behind(): lax.ppermute(value, AXES, [(s, s + steps) for s in range(first, last)])  16.9 us
    pallas_call x1, Pallas kernels, make_tables(): pl.pallas_call(tables_kernel, grid=(groups // PER_TILE,), in_specs=[fixed...  11.6 us
    ppermute x11, waiting for transfers between devices, swap(): return lax.ppermute(value, AXES, [(s, s ^ mask) for s in range(count)])  10.4 us
    pallas_call x3, Pallas kernels, make_back(): pl.pallas_call(back_kernel, grid=(channels // width,), in_specs=[columns(...  9.2 us
    pallas_call x1, Pallas kernels, make_edges(): pl.pallas_call(edges_kernel, grid=(channels // width,), in_specs=[pl.Bloc...  4.1 us
  transfers between devices with their start and end apart: 14, of which 7 were waited for; matrix products, arithmetic and copies ran while one was open for 0% of the time, Pallas kernels for 22%

profile of v3, /device:TPU:1, one launch (start us, length us, event | category | flops | bytes accessed | tf_op | source)
XLA Modules:
  0.0 95.8 jit_solution(16373419835809577771)
XLA Ops:
  0.6 4.1 %edges.1 = (bf16[160,2048]{1,0:T(8,128)(2,1)}, bf16[160,2048]{1,0:T(8,128)(2,1)}) custom-call(s32[256]{0:T(256)} %ids.3, bf16[256,2048]{1,0:T(8,128)(2,1)} %q.3, bf16[256,2048]{1,0:T(8,128)(2,1)} %g.3, bf16[256,2048]{1,0:T(8,128)(2,1)} %k.3, bf16[256,2048]{1,0:T(8,128)(2,1)} %k.3, bf16[256,2048]{1,0:T(8,128)(2,1)} %v.3, bf16[256,2048]{1,0:T(8,128)(2,1)} %v.3, ...), custom_call_target="tpu_custom_call" | custom-call | tf_op jit(solution)/shard_map/edges/pallas_call | solution.py:337
  4.7 4.4 %collective-permute-start = (bf16[160,2048]{1,0:T(8,128)(2,1)}, bf16[160,2048]{1,0:T(8,128)(2,1)S(1)}, u32[]{:S(2)}, u32[]{:S(2)}) collective-permute-start(bf16[160,2048]{1,0:T(8,128)(2,1)} %get-tuple-element.40), channel_id=1, source_target_pairs={{0,1},{1,2},{2,3},{3,4},{4,5},{5,6},{6,7},{7,8},{8,9},{9,10},{10,1... | collective-permute-start | bytes 1966088 | tf_op jit(solution)/shard_map/ppermute | solution.py:474
  9.1 6.4 %collective-permute-start.1 = (bf16[160,2048]{1,0:T(8,128)(2,1)}, bf16[160,2048]{1,0:T(8,128)(2,1)S(1)}, u32[]{:S(2)}, u32[]{:S(2)}) collective-permute-start(bf16[160,2048]{1,0:T(8,128)(2,1)} %get-tuple-element.41), channel_id=1, source_target_pairs={{1,0},{2,1},{3,2},{4,3},{5,4},{6,5},{7,6},{8,7},{9,8},{10,9},{11,1... | collective-permute-start | bytes 1966088 | tf_op jit(solution)/shard_map/ppermute | solution.py:474
  15.6 11.6 %tables.1 = (bf16[128,128,256]{2,1,0:T(8,128)(2,1)}, bf16[128,128,256]{2,1,0:T(8,128)(2,1)}) custom-call(bf16[128,128]{1,0:T(8,128)(2,1)} %taps.1), custom_call_target="tpu_custom_call" | custom-call | bytes 67108864 | tf_op jit(solution)/shard_map/tables/pallas_call | solution.py:361
  27.2 1.0 %collective-permute-done.from_left = bf16[160,2048]{1,0:T(8,128)(2,1)S(1)} collective-permute-done((bf16[160,2048]{1,0:T(8,128)(2,1)}, bf16[160,2048]{1,0:T(8,128)(2,1)S(1)}, u32[]{:S(2)}, u32[]{:S(2)}) %collective-permute-start) | collective-permute-done | bytes 655392 | tf_op jit(solution)/shard_map/ppermute | solution.py:474
  28.2 0.0 copy-start.1
  28.2 0.0 collective-permute-done.1.from_right
  28.2 0.0 copy-start.2
  28.2 0.8 copy-done.1
  29.1 0.2 copy-done.2
  29.3 18.2 %main.1 = (bf16[256,2048]{1,0:T(8,128)(2,1)}, bf16[256,2048]{1,0:T(8,128)(2,1)}, bf16[256,2048]{1,0:T(8,128)(2,1)}, bf16[256,2048]{1,0:T(8,128)(2,1)}, bf16[48,2...) custom-call(s32[256]{0:T(256)} %ids.3, bf16[256,2048]{1,0:T(8,128)(2,1)} %q.3, bf16[256,2048]{1,0:T(8,128)(2,1)} %k.3, ...), custom_call_target="tpu_custom_call" | custom-call | tf_op jit(solution)/shard_map/main/pallas_call | solution.py:381
  47.5 0.2 collective-permute-start.2
  47.7 1.3 %collective-permute-done.2 = f32[256,128]{1,0:T(8,128)S(1)} collective-permute-done((f32[256,128]{1,0:T(8,128)S(1)}, f32[256,128]{1,0:T(8,128)S(1)}, u32[]{:S(2)}, u32[]{:S(2)}) %collective-permute-start.2) | collective-permute-done | bytes 131104 | tf_op jit(solution)/shard_map/ppermute | solution.py:479
  49.0 3.2 %collective-permute-start.3 = (f32[128,128]{1,0:T(8,128)S(1)}, f32[128,128]{1,0:T(8,128)S(1)}, u32[]{:S(2)}, u32[]{:S(2)}) collective-permute-start(f32[128,128]{1,0:T(8,128)S(1)} %slice_select_fusion.2), channel_id=1, source_target_pairs={{0,16},{1,17},{2,18},{3,19},{4,20},{5,21},{6,22},{7,23},{8,24},{9,... | collective-permute-start | bytes 196616 | tf_op jit(solution)/shard_map/ppermute | solution.py:479
  52.2 6.1 %collective-permute-start.5 = (bf16[48,2048]{1,0:T(8,128)(2,1)}, bf16[48,2048]{1,0:T(8,128)(2,1)S(1)}, u32[]{:S(2)}, u32[]{:S(2)}) collective-permute-start(bf16[48,2048]{1,0:T(8,128)(2,1)} %get-tuple-element.45), channel_id=1, source_target_pairs={{1,0},{2,1},{3,2},{4,3},{5,4},{6,5},{7,6},{8,7},{9,8},{10,9},{11,1... | collective-permute-start | bytes 589832 | tf_op jit(solution)/shard_map/ppermute | solution.py:474
  58.4 0.0 collective-permute-done.3
  58.4 1.6 %collective-permute-start.4 = (f32[128,128]{1,0:T(8,128)S(1)}, f32[128,128]{1,0:T(8,128)S(1)}, u32[]{:S(2)}, u32[]{:S(2)}) collective-permute-start(f32[128,128]{1,0:T(8,128)S(1)} %select_add_fusion), channel_id=1, source_target_pairs={{0,48},{1,49},{2,50},{3,51},{4,52},{5,53},{6,54},{7,55},{8,56},{9,... | collective-permute-start | bytes 196616 | tf_op jit(solution)/shard_map/ppermute | solution.py:479
  60.1 3.7 %collective-permute-done.4 = f32[128,128]{1,0:T(8,128)S(1)} collective-permute-done((f32[128,128]{1,0:T(8,128)S(1)}, f32[128,128]{1,0:T(8,128)S(1)}, u32[]{:S(2)}, u32[]{:S(2)}) %collective-permute-start.4) | collective-permute-done | bytes 65568 | tf_op jit(solution)/shard_map/ppermute | solution.py:479
  63.8 0.0 collective-permute-done.5.heads
  63.8 0.0 copy-start
  63.8 0.4 collective-permute-start.6
  64.2 0.2 copy-done
  64.5 3.1 %back.3 = bf16[256,2048]{1,0:T(8,128)(2,1)} custom-call(bf16[256,2048]{1,0:T(8,128)(2,1)} %get-tuple-element.47.grads, bf16[48,2048]{1,0:T(8,128)(2,1)} %copy-done, f32[3,7,2048]{2,1,0:T(8,128)} %taps_ref.6), custom_call_target="tpu_custom_call" | custom-call | flops 7340032 | bytes 4194304 | tf_op jit(solution)/shard_map/back/pallas_call | solution.py:419
  67.5 0.0 collective-permute-done.6
  67.5 1.9 %collective-permute-start.7 = (f32[128,128]{1,0:T(8,128)S(1)}, f32[128,128]{1,0:T(8,128)S(1)}, u32[]{:S(2)}, u32[]{:S(2)}) collective-permute-start(f32[128,128]{1,0:T(8,128)S(1)} %add.50), channel_id=1, source_target_pairs={{0,192},{1,193},{2,194},{3,195},{4,196},{5,197},{6,198},{7,199},{8... | collective-permute-start | bytes 196616 | tf_op jit(solution)/shard_map/ppermute | solution.py:479
  69.4 3.1 %back.4 = bf16[256,2048]{1,0:T(8,128)(2,1)} custom-call(bf16[256,2048]{1,0:T(8,128)(2,1)} %get-tuple-element.54.grads, bf16[48,2048]{1,0:T(8,128)(2,1)} %copy-done, f32[3,7,2048]{2,1,0:T(8,128)} %taps_ref.6), custom_call_target="tpu_custom_call" | custom-call | flops 7340032 | bytes 4194304 | tf_op jit(solution)/shard_map/back/pallas_call | solution.py:419
  72.5 0.0 collective-permute-done.7
  72.5 0.9 collective-permute-start.9
  73.4 2.2 %collective-permute-start.10 = (f32[128,128]{1,0:T(8,128)S(1)}, f32[128,128]{1,0:T(8,128)S(1)}, u32[]{:S(2)}, u32[]{:S(2)}) collective-permute-start(f32[128,128]{1,0:T(8,128)S(1)} %add.51), channel_id=1, source_target_pairs={{0,3},{1,2},{2,1},{3,0},{4,7},{5,6},{6,5},{7,4},{8,11},{9,10},{10,... | collective-permute-start | bytes 196616 | tf_op jit(solution)/shard_map/ppermute | solution.py:479
  75.6 0.2 collective-permute-start.8
  75.8 3.1 %back.5 = bf16[256,2048]{1,0:T(8,128)(2,1)} custom-call(bf16[256,2048]{1,0:T(8,128)(2,1)} %get-tuple-element.61.grads, bf16[48,2048]{1,0:T(8,128)(2,1)} %copy-done, f32[3,7,2048]{2,1,0:T(8,128)} %taps_ref.6), custom_call_target="tpu_custom_call" | custom-call | flops 7340032 | bytes 4194304 | tf_op jit(solution)/shard_map/back/pallas_call | solution.py:419
  78.8 0.0 collective-permute-done.9
  78.8 0.0 collective-permute-done.10
  78.9 0.2 collective-permute-done.8
  79.1 5.7 %collective-permute-start.11 = (f32[128,128]{1,0:T(8,128)S(1)}, f32[128,128]{1,0:T(8,128)S(1)}, u32[]{:S(2)}, u32[]{:S(2)}) collective-permute-start(f32[128,128]{1,0:T(8,128)S(1)} %add_add_fusion), channel_id=1, source_target_pairs={{0,6},{1,7},{2,4},{3,5},{4,2},{5,3},{6,0},{7,1},{8,14},{9,15},{10,... | collective-permute-start | bytes 196616 | tf_op jit(solution)/shard_map/ppermute | solution.py:479
  84.8 1.7 %collective-permute-done.11 = f32[128,128]{1,0:T(8,128)S(1)} collective-permute-done((f32[128,128]{1,0:T(8,128)S(1)}, f32[128,128]{1,0:T(8,128)S(1)}, u32[]{:S(2)}, u32[]{:S(2)}) %collective-permute-start.11) | collective-permute-done | bytes 65568 | tf_op jit(solution)/shard_map/ppermute | solution.py:479
  86.5 0.6 collective-permute-start.12
  87.1 2.6 %collective-permute-done.12 = f32[128,128]{1,0:T(8,128)S(1)} collective-permute-done((f32[128,128]{1,0:T(8,128)S(1)}, f32[128,128]{1,0:T(8,128)S(1)}, u32[]{:S(2)}, u32[]{:S(2)}) %collective-permute-start.12) | collective-permute-done | bytes 65568 | tf_op jit(solution)/shard_map/ppermute | solution.py:479
  89.7 4.4 %collective-permute-start.13 = (f32[256,128]{1,0:T(8,128)S(1)}, f32[256,128]{1,0:T(8,128)S(1)}, u32[]{:S(2)}, u32[]{:S(2)}) collective-permute-start(f32[256,128]{1,0:T(8,128)S(1)} %maximum_select_fusion.half), channel_id=1, source_target_pairs={{0,8},{1,9},{2,10},{3,11},{4,12},{5,13},{6,14},{7,15},{8,0},{9,1},... | collective-permute-start | bytes 393224 | tf_op jit(solution)/shard_map/ppermute | solution.py:479
  94.1 1.0 %collective-permute-done.13.other = f32[256,128]{1,0:T(8,128)S(1)} collective-permute-done((f32[256,128]{1,0:T(8,128)S(1)}, f32[256,128]{1,0:T(8,128)S(1)}, u32[]{:S(2)}, u32[]{:S(2)}) %collective-permute-start.13) | collective-permute-done | bytes 131104 | tf_op jit(solution)/shard_map/ppermute | solution.py:479
  95.1 0.7 last.1
  (10 shorter events, 0.1 us)
Async XLA Ops:
  4.7 23.5 %collective-permute-start = (bf16[160,2048]{1,0:T(8,128)(2,1)}, bf16[160,2048]{1,0:T(8,128)(2,1)S(1)}, u32[]{:S(2)}, u32[]{:S(2)}) collective-permute-start(bf16[160,2048]{1,0:T(8,128)(2,1)} %get-tuple-element.40), channel_id=1, source_target_pairs={{0,1},{1,2},{2,3},{3,4},{4,5},{5,6},{6,7},{7,8},{8,9},{9,10},{10,1... | collective-permute-start | bytes 1966088 | tf_op jit(solution)/shard_map/ppermute | solution.py:474
  9.1 19.1 %collective-permute-start.1 = (bf16[160,2048]{1,0:T(8,128)(2,1)}, bf16[160,2048]{1,0:T(8,128)(2,1)S(1)}, u32[]{:S(2)}, u32[]{:S(2)}) collective-permute-start(bf16[160,2048]{1,0:T(8,128)(2,1)} %get-tuple-element.41), channel_id=1, source_target_pairs={{1,0},{2,1},{3,2},{4,3},{5,4},{6,5},{7,6},{8,7},{9,8},{10,9},{11,1... | collective-permute-start | bytes 1966088 | tf_op jit(solution)/shard_map/ppermute | solution.py:474
  28.2 0.8 copy-start.1
  28.2 1.0 %copy-start.2 = (bf16[160,2048]{1,0:T(8,128)(2,1)}, bf16[160,2048]{1,0:T(8,128)(2,1)S(1)}, u32[]{:S(2)}) copy-start(bf16[160,2048]{1,0:T(8,128)(2,1)S(1)} %collective-permute-done.1.from_right) | copy-start | bytes 1966084
  47.5 1.4 %collective-permute-start.2 = (f32[256,128]{1,0:T(8,128)S(1)}, f32[256,128]{1,0:T(8,128)S(1)}, u32[]{:S(2)}, u32[]{:S(2)}) collective-permute-start(f32[256,128]{1,0:T(8,128)S(1)} %bitcast.5), channel_id=1, source_target_pairs={{0,8},{1,9},{2,10},{3,11},{4,12},{5,13},{6,14},{7,15},{8,0},{9,1},... | collective-permute-start | bytes 393224 | tf_op jit(solution)/shard_map/ppermute | solution.py:479
  49.0 9.4 %collective-permute-start.3 = (f32[128,128]{1,0:T(8,128)S(1)}, f32[128,128]{1,0:T(8,128)S(1)}, u32[]{:S(2)}, u32[]{:S(2)}) collective-permute-start(f32[128,128]{1,0:T(8,128)S(1)} %slice_select_fusion.2), channel_id=1, source_target_pairs={{0,16},{1,17},{2,18},{3,19},{4,20},{5,21},{6,22},{7,23},{8,24},{9,... | collective-permute-start | bytes 196616 | tf_op jit(solution)/shard_map/ppermute | solution.py:479
  52.2 11.5 %collective-permute-start.5 = (bf16[48,2048]{1,0:T(8,128)(2,1)}, bf16[48,2048]{1,0:T(8,128)(2,1)S(1)}, u32[]{:S(2)}, u32[]{:S(2)}) collective-permute-start(bf16[48,2048]{1,0:T(8,128)(2,1)} %get-tuple-element.45), channel_id=1, source_target_pairs={{1,0},{2,1},{3,2},{4,3},{5,4},{6,5},{7,6},{8,7},{9,8},{10,9},{11,1... | collective-permute-start | bytes 589832 | tf_op jit(solution)/shard_map/ppermute | solution.py:474
  58.4 5.3 %collective-permute-start.4 = (f32[128,128]{1,0:T(8,128)S(1)}, f32[128,128]{1,0:T(8,128)S(1)}, u32[]{:S(2)}, u32[]{:S(2)}) collective-permute-start(f32[128,128]{1,0:T(8,128)S(1)} %select_add_fusion), channel_id=1, source_target_pairs={{0,48},{1,49},{2,50},{3,51},{4,52},{5,53},{6,54},{7,55},{8,56},{9,... | collective-permute-start | bytes 196616 | tf_op jit(solution)/shard_map/ppermute | solution.py:479
  63.8 0.7 copy-start
  63.8 3.7 %collective-permute-start.6 = (f32[128,128]{1,0:T(8,128)S(1)}, f32[128,128]{1,0:T(8,128)S(1)}, u32[]{:S(2)}, u32[]{:S(2)}) collective-permute-start(f32[128,128]{1,0:T(8,128)S(1)} %add.49), channel_id=1, source_target_pairs={{0,64},{1,65},{2,66},{3,67},{4,68},{5,69},{6,70},{7,71},{8,72},{9,... | collective-permute-start | bytes 196616 | tf_op jit(solution)/shard_map/ppermute | solution.py:479
  67.5 5.0 %collective-permute-start.7 = (f32[128,128]{1,0:T(8,128)S(1)}, f32[128,128]{1,0:T(8,128)S(1)}, u32[]{:S(2)}, u32[]{:S(2)}) collective-permute-start(f32[128,128]{1,0:T(8,128)S(1)} %add.50), channel_id=1, source_target_pairs={{0,192},{1,193},{2,194},{3,195},{4,196},{5,197},{6,198},{7,199},{8... | collective-permute-start | bytes 196616 | tf_op jit(solution)/shard_map/ppermute | solution.py:479
  72.5 6.3 %collective-permute-start.9 = (f32[128,128]{1,0:T(8,128)S(1)}, f32[128,128]{1,0:T(8,128)S(1)}, u32[]{:S(2)}, u32[]{:S(2)}) collective-permute-start(f32[128,128]{1,0:T(8,128)S(1)} %add.51), channel_id=1, source_target_pairs={{0,2},{1,3},{2,0},{3,1},{4,6},{5,7},{6,4},{7,5},{8,10},{9,11},{10,... | collective-permute-start | bytes 196616 | tf_op jit(solution)/shard_map/ppermute | solution.py:479
  73.4 5.4 %collective-permute-start.10 = (f32[128,128]{1,0:T(8,128)S(1)}, f32[128,128]{1,0:T(8,128)S(1)}, u32[]{:S(2)}, u32[]{:S(2)}) collective-permute-start(f32[128,128]{1,0:T(8,128)S(1)} %add.51), channel_id=1, source_target_pairs={{0,3},{1,2},{2,1},{3,0},{4,7},{5,6},{6,5},{7,4},{8,11},{9,10},{10,... | collective-permute-start | bytes 196616 | tf_op jit(solution)/shard_map/ppermute | solution.py:479
  75.6 3.5 %collective-permute-start.8 = (f32[128,128]{1,0:T(8,128)S(1)}, f32[128,128]{1,0:T(8,128)S(1)}, u32[]{:S(2)}, u32[]{:S(2)}) collective-permute-start(f32[128,128]{1,0:T(8,128)S(1)} %add.51), channel_id=1, source_target_pairs={{0,1},{1,0},{2,3},{3,2},{4,5},{5,4},{6,7},{7,6},{8,9},{9,8},{10,11... | collective-permute-start | bytes 196616 | tf_op jit(solution)/shard_map/ppermute | solution.py:479
  79.1 7.4 %collective-permute-start.11 = (f32[128,128]{1,0:T(8,128)S(1)}, f32[128,128]{1,0:T(8,128)S(1)}, u32[]{:S(2)}, u32[]{:S(2)}) collective-permute-start(f32[128,128]{1,0:T(8,128)S(1)} %add_add_fusion), channel_id=1, source_target_pairs={{0,6},{1,7},{2,4},{3,5},{4,2},{5,3},{6,0},{7,1},{8,14},{9,15},{10,... | collective-permute-start | bytes 196616 | tf_op jit(solution)/shard_map/ppermute | solution.py:479
  86.5 3.2 %collective-permute-start.12 = (f32[128,128]{1,0:T(8,128)S(1)}, f32[128,128]{1,0:T(8,128)S(1)}, u32[]{:S(2)}, u32[]{:S(2)}) collective-permute-start(f32[128,128]{1,0:T(8,128)S(1)} %add.55), channel_id=1, source_target_pairs={{0,16},{1,17},{2,18},{3,19},{4,20},{5,21},{6,22},{7,23},{8,24},{9,... | collective-permute-start | bytes 196616 | tf_op jit(solution)/shard_map/ppermute | solution.py:479
  89.7 5.4 %collective-permute-start.13 = (f32[256,128]{1,0:T(8,128)S(1)}, f32[256,128]{1,0:T(8,128)S(1)}, u32[]{:S(2)}, u32[]{:S(2)}) collective-permute-start(f32[256,128]{1,0:T(8,128)S(1)} %maximum_select_fusion.half), channel_id=1, source_target_pairs={{0,8},{1,9},{2,10},{3,11},{4,12},{5,13},{6,14},{7,15},{8,0},{9,1},... | collective-permute-start | bytes 393224 | tf_op jit(solution)/shard_map/ppermute | solution.py:479

commit v4 on v3

--- a/solution.py
+++ b/solution.py
@@ -495,6 +495,11 @@
     return masks
 
 
+def ring_steps(size):
+    masks = ring_masks(size)
+    return [(1, 2, 3)] + [(m,) for m in masks[2:]] if len(masks) > 1 else [(m,) for m in masks]
+
+
 def total_over_all(value, work):
     ctx = lax.axis_size("ctx")
     seg = lax.axis_size("seg")
@@ -504,12 +509,10 @@
     while along * along * cores < seg:
         along *= 2
     halving = [ctx, cores * ctx]
-    doubling = [cores * ctx * m for m in ring_masks(along)]
-    doubling += [cores * ctx * along * m for m in ring_masks(seg // (cores * along))]
-    doubling = [(m,) for m in doubling if m not in halving]
-    near = ring_masks(ctx)
-    doubling += [(1, 2, 3)] if len(near) > 1 else [(m,) for m in near]
-    doubling += [(m,) for m in near[2:]]
+    x_unit, y_unit = cores * ctx, cores * ctx * along
+    doubling = [(x_unit * m,) for m in ring_masks(along) if x_unit * m not in halving]
+    doubling += [tuple(y_unit * m for m in step) for step in ring_steps(seg // (cores * along))]
+    doubling += ring_steps(ctx)
     mine = []
     done = []
     pending = list(work)

time: 96.1 us -> 94.1 us (0.979)
  starting transfers between devices: 38.3 us -> 36.6 us
    ppermute x11 -> x12, starting transfers between devices: 21.4 us -> 19.7 us  [swap(): return lax.ppermute(value, AXES, [(s, s ^ mask) for s in range(count)])]
    ppermute x11 -> x12, waiting for transfers between devices: 10.4 us -> 10.2 us  [swap(): return lax.ppermute(value, AXES, [(s, s ^ mask) for s in range(count)])]
  transfers between devices with their start and end apart: 14 -> 15, of which waited for: 7 -> 7; matrix products, arithmetic and copies ran while one was open for 0% -> 0% of each run, Pallas kernels for 22% -> 22%
where the time goes in v4:
time: 94.1 us; the launch traced here: 93.8 us
  Pallas kernels  44 us (47%)
  starting transfers between devices  36.6 us (39%)
  waiting for transfers between devices  11.2 us (12%)
  local copies, waits for them, and re-layouts  1.05 us (1%)
    ppermute x12, starting transfers between devices, swap(): return lax.ppermute(value, AXES, [(s, s ^ mask) for s in range(count)])  19.7 us
    pallas_call x1, Pallas kernels, make_main(): pl.pallas_call(main_kernel, grid=(tiles // PER_STEP,), in_specs=[pl.Block...  18.2 us
    ppermute x3, starting transfers between devices, from_behind(): lax.ppermute(value, AXES, [(s, s + steps) for s in range(first, last)])  16.9 us
    pallas_call x1, Pallas kernels, make_tables(): pl.pallas_call(tables_kernel, grid=(groups // PER_TILE,), in_specs=[fixed...  11.7 us
    ppermute x12, waiting for transfers between devices, swap(): return lax.ppermute(value, AXES, [(s, s ^ mask) for s in range(count)])  10.2 us
    pallas_call x3, Pallas kernels, make_back(): pl.pallas_call(back_kernel, grid=(channels // width,), in_specs=[columns(...  9.21 us
    pallas_call x1, Pallas kernels, make_edges(): pl.pallas_call(edges_kernel, grid=(channels // width,), in_specs=[pl.Bloc...  4.1 us
  transfers between devices with their start and end apart: 15, of which 7 were waited for; matrix products, arithmetic and copies ran while one was open for 0% of the time, Pallas kernels for 22%

profile of v4, /device:TPU:1, one launch (start us, length us, event | category | flops | bytes accessed | tf_op | source)
XLA Modules:
  0.0 93.8 jit_solution(8397625725498702704)
XLA Ops:
  0.6 4.1 %edges.1 = (bf16[160,2048]{1,0:T(8,128)(2,1)}, bf16[160,2048]{1,0:T(8,128)(2,1)}) custom-call(s32[256]{0:T(256)} %ids.3, bf16[256,2048]{1,0:T(8,128)(2,1)} %q.3, bf16[256,2048]{1,0:T(8,128)(2,1)} %g.3, bf16[256,2048]{1,0:T(8,128)(2,1)} %k.3, bf16[256,2048]{1,0:T(8,128)(2,1)} %k.3, bf16[256,2048]{1,0:T(8,128)(2,1)} %v.3, bf16[256,2048]{1,0:T(8,128)(2,1)} %v.3, ...), custom_call_target="tpu_custom_call" | custom-call | tf_op jit(solution)/shard_map/edges/pallas_call | solution.py:337
  4.7 4.4 %collective-permute-start = (bf16[160,2048]{1,0:T(8,128)(2,1)}, bf16[160,2048]{1,0:T(8,128)(2,1)S(1)}, u32[]{:S(2)}, u32[]{:S(2)}) collective-permute-start(bf16[160,2048]{1,0:T(8,128)(2,1)} %get-tuple-element.40), channel_id=1, source_target_pairs={{0,1},{1,2},{2,3},{3,4},{4,5},{5,6},{6,7},{7,8},{8,9},{9,10},{10,1... | collective-permute-start | bytes 1966088 | tf_op jit(solution)/shard_map/ppermute | solution.py:474
  9.1 6.4 %collective-permute-start.1 = (bf16[160,2048]{1,0:T(8,128)(2,1)}, bf16[160,2048]{1,0:T(8,128)(2,1)S(1)}, u32[]{:S(2)}, u32[]{:S(2)}) collective-permute-start(bf16[160,2048]{1,0:T(8,128)(2,1)} %get-tuple-element.41), channel_id=1, source_target_pairs={{1,0},{2,1},{3,2},{4,3},{5,4},{6,5},{7,6},{8,7},{9,8},{10,9},{11,1... | collective-permute-start | bytes 1966088 | tf_op jit(solution)/shard_map/ppermute | solution.py:474
  15.6 11.7 %tables.1 = (bf16[128,128,256]{2,1,0:T(8,128)(2,1)}, bf16[128,128,256]{2,1,0:T(8,128)(2,1)}) custom-call(bf16[128,128]{1,0:T(8,128)(2,1)} %taps.1), custom_call_target="tpu_custom_call" | custom-call | bytes 67108864 | tf_op jit(solution)/shard_map/tables/pallas_call | solution.py:361
  27.3 1.0 %collective-permute-done.from_left = bf16[160,2048]{1,0:T(8,128)(2,1)S(1)} collective-permute-done((bf16[160,2048]{1,0:T(8,128)(2,1)}, bf16[160,2048]{1,0:T(8,128)(2,1)S(1)}, u32[]{:S(2)}, u32[]{:S(2)}) %collective-permute-start) | collective-permute-done | bytes 655392 | tf_op jit(solution)/shard_map/ppermute | solution.py:474
  28.2 0.0 copy-start.1
  28.2 0.0 collective-permute-done.1.from_right
  28.2 0.0 copy-start.2
  28.2 0.8 copy-done.1
  29.1 0.2 copy-done.2
  29.3 18.2 %main.1 = (bf16[256,2048]{1,0:T(8,128)(2,1)}, bf16[256,2048]{1,0:T(8,128)(2,1)}, bf16[256,2048]{1,0:T(8,128)(2,1)}, bf16[256,2048]{1,0:T(8,128)(2,1)}, bf16[48,2...) custom-call(s32[256]{0:T(256)} %ids.3, bf16[256,2048]{1,0:T(8,128)(2,1)} %q.3, bf16[256,2048]{1,0:T(8,128)(2,1)} %k.3, ...), custom_call_target="tpu_custom_call" | custom-call | tf_op jit(solution)/shard_map/main/pallas_call | solution.py:381
  47.5 0.2 collective-permute-start.2
  47.7 1.3 %collective-permute-done.2 = f32[256,128]{1,0:T(8,128)S(1)} collective-permute-done((f32[256,128]{1,0:T(8,128)S(1)}, f32[256,128]{1,0:T(8,128)S(1)}, u32[]{:S(2)}, u32[]{:S(2)}) %collective-permute-start.2) | collective-permute-done | bytes 131104 | tf_op jit(solution)/shard_map/ppermute | solution.py:479
  49.0 3.2 %collective-permute-start.3 = (f32[128,128]{1,0:T(8,128)S(1)}, f32[128,128]{1,0:T(8,128)S(1)}, u32[]{:S(2)}, u32[]{:S(2)}) collective-permute-start(f32[128,128]{1,0:T(8,128)S(1)} %slice_select_fusion.2), channel_id=1, source_target_pairs={{0,16},{1,17},{2,18},{3,19},{4,20},{5,21},{6,22},{7,23},{8,24},{9,... | collective-permute-start | bytes 196616 | tf_op jit(solution)/shard_map/ppermute | solution.py:479
  52.2 6.1 %collective-permute-start.5 = (bf16[48,2048]{1,0:T(8,128)(2,1)}, bf16[48,2048]{1,0:T(8,128)(2,1)S(1)}, u32[]{:S(2)}, u32[]{:S(2)}) collective-permute-start(bf16[48,2048]{1,0:T(8,128)(2,1)} %get-tuple-element.45), channel_id=1, source_target_pairs={{1,0},{2,1},{3,2},{4,3},{5,4},{6,5},{7,6},{8,7},{9,8},{10,9},{11,1... | collective-permute-start | bytes 589832 | tf_op jit(solution)/shard_map/ppermute | solution.py:474
  58.4 0.0 collective-permute-done.3
  58.4 1.6 %collective-permute-start.4 = (f32[128,128]{1,0:T(8,128)S(1)}, f32[128,128]{1,0:T(8,128)S(1)}, u32[]{:S(2)}, u32[]{:S(2)}) collective-permute-start(f32[128,128]{1,0:T(8,128)S(1)} %select_add_fusion), channel_id=1, source_target_pairs={{0,48},{1,49},{2,50},{3,51},{4,52},{5,53},{6,54},{7,55},{8,56},{9,... | collective-permute-start | bytes 196616 | tf_op jit(solution)/shard_map/ppermute | solution.py:479
  60.1 3.7 %collective-permute-done.4 = f32[128,128]{1,0:T(8,128)S(1)} collective-permute-done((f32[128,128]{1,0:T(8,128)S(1)}, f32[128,128]{1,0:T(8,128)S(1)}, u32[]{:S(2)}, u32[]{:S(2)}) %collective-permute-start.4) | collective-permute-done | bytes 65568 | tf_op jit(solution)/shard_map/ppermute | solution.py:479
  63.8 0.0 collective-permute-done.5.heads
  63.8 0.0 copy-start
  63.8 2.1 %collective-permute-start.7 = (f32[128,128]{1,0:T(8,128)S(1)}, f32[128,128]{1,0:T(8,128)S(1)}, u32[]{:S(2)}, u32[]{:S(2)}) collective-permute-start(f32[128,128]{1,0:T(8,128)S(1)} %add.52), channel_id=1, source_target_pairs={{0,128},{1,129},{2,130},{3,131},{4,132},{5,133},{6,134},{7,135},{8... | collective-permute-start | bytes 196616 | tf_op jit(solution)/shard_map/ppermute | solution.py:479
  65.9 0.8 collective-permute-start.8
  66.6 0.0 collective-permute-start.6
  66.6 0.0 copy-done
  66.6 3.1 %back.3 = bf16[256,2048]{1,0:T(8,128)(2,1)} custom-call(bf16[256,2048]{1,0:T(8,128)(2,1)} %get-tuple-element.47.grads, bf16[48,2048]{1,0:T(8,128)(2,1)} %copy-done, f32[3,7,2048]{2,1,0:T(8,128)} %taps_ref.6), custom_call_target="tpu_custom_call" | custom-call | flops 7340032 | bytes 4194304 | tf_op jit(solution)/shard_map/back/pallas_call | solution.py:419
  69.7 0.0 collective-permute-done.7
  69.7 1.1 %collective-permute-done.8 = f32[128,128]{1,0:T(8,128)S(1)} collective-permute-done((f32[128,128]{1,0:T(8,128)S(1)}, f32[128,128]{1,0:T(8,128)S(1)}, u32[]{:S(2)}, u32[]{:S(2)}) %collective-permute-start.8) | collective-permute-done | bytes 65568 | tf_op jit(solution)/shard_map/ppermute | solution.py:479
  70.8 0.0 collective-permute-done.6
  70.8 0.3 collective-permute-start.10
  71.1 2.2 %collective-permute-start.11 = (f32[128,128]{1,0:T(8,128)S(1)}, f32[128,128]{1,0:T(8,128)S(1)}, u32[]{:S(2)}, u32[]{:S(2)}) collective-permute-start(f32[128,128]{1,0:T(8,128)S(1)} %add_add_fusion.1), channel_id=1, source_target_pairs={{0,3},{1,2},{2,1},{3,0},{4,7},{5,6},{6,5},{7,4},{8,11},{9,10},{10,... | collective-permute-start | bytes 196616 | tf_op jit(solution)/shard_map/ppermute | solution.py:479
  73.3 0.2 collective-permute-start.9
  73.5 3.1 %back.4 = bf16[256,2048]{1,0:T(8,128)(2,1)} custom-call(bf16[256,2048]{1,0:T(8,128)(2,1)} %get-tuple-element.54.grads, bf16[48,2048]{1,0:T(8,128)(2,1)} %copy-done, f32[3,7,2048]{2,1,0:T(8,128)} %taps_ref.6), custom_call_target="tpu_custom_call" | custom-call | flops 7340032 | bytes 4194304 | tf_op jit(solution)/shard_map/back/pallas_call | solution.py:419
  76.6 0.0 collective-permute-done.10
  76.6 0.0 collective-permute-done.11
  76.6 0.4 collective-permute-done.9
  77.0 5.9 %collective-permute-start.12 = (f32[128,128]{1,0:T(8,128)S(1)}, f32[128,128]{1,0:T(8,128)S(1)}, u32[]{:S(2)}, u32[]{:S(2)}) collective-permute-start(f32[128,128]{1,0:T(8,128)S(1)} %add_add_fusion), channel_id=1, source_target_pairs={{0,6},{1,7},{2,4},{3,5},{4,2},{5,3},{6,0},{7,1},{8,14},{9,15},{10,... | collective-permute-start | bytes 196616 | tf_op jit(solution)/shard_map/ppermute | solution.py:479
  82.9 3.1 %back.5 = bf16[256,2048]{1,0:T(8,128)(2,1)} custom-call(bf16[256,2048]{1,0:T(8,128)(2,1)} %get-tuple-element.61.grads, bf16[48,2048]{1,0:T(8,128)(2,1)} %copy-done, f32[3,7,2048]{2,1,0:T(8,128)} %taps_ref.6), custom_call_target="tpu_custom_call" | custom-call | flops 7340032 | bytes 4194304 | tf_op jit(solution)/shard_map/back/pallas_call | solution.py:419
  85.9 0.0 collective-permute-done.12
  86.0 0.4 collective-permute-start.13
  86.3 2.8 %collective-permute-done.13 = f32[128,128]{1,0:T(8,128)S(1)} collective-permute-done((f32[128,128]{1,0:T(8,128)S(1)}, f32[128,128]{1,0:T(8,128)S(1)}, u32[]{:S(2)}, u32[]{:S(2)}) %collective-permute-start.13) | collective-permute-done | bytes 65568 | tf_op jit(solution)/shard_map/ppermute | solution.py:479
  89.2 2.9 %collective-permute-start.14 = (f32[256,128]{1,0:T(8,128)S(1)}, f32[256,128]{1,0:T(8,128)S(1)}, u32[]{:S(2)}, u32[]{:S(2)}) collective-permute-start(f32[256,128]{1,0:T(8,128)S(1)} %maximum_select_fusion.half), channel_id=1, source_target_pairs={{0,8},{1,9},{2,10},{3,11},{4,12},{5,13},{6,14},{7,15},{8,0},{9,1},... | collective-permute-start | bytes 393224 | tf_op jit(solution)/shard_map/ppermute | solution.py:479
  92.0 1.0 %collective-permute-done.14.other = f32[256,128]{1,0:T(8,128)S(1)} collective-permute-done((f32[256,128]{1,0:T(8,128)S(1)}, f32[256,128]{1,0:T(8,128)S(1)}, u32[]{:S(2)}, u32[]{:S(2)}) %collective-permute-start.14) | collective-permute-done | bytes 131104 | tf_op jit(solution)/shard_map/ppermute | solution.py:479
  93.0 0.7 last.1
  (9 shorter events, 0.1 us)
Async XLA Ops:
  4.7 23.5 %collective-permute-start = (bf16[160,2048]{1,0:T(8,128)(2,1)}, bf16[160,2048]{1,0:T(8,128)(2,1)S(1)}, u32[]{:S(2)}, u32[]{:S(2)}) collective-permute-start(bf16[160,2048]{1,0:T(8,128)(2,1)} %get-tuple-element.40), channel_id=1, source_target_pairs={{0,1},{1,2},{2,3},{3,4},{4,5},{5,6},{6,7},{7,8},{8,9},{9,10},{10,1... | collective-permute-start | bytes 1966088 | tf_op jit(solution)/shard_map/ppermute | solution.py:474
  9.1 19.1 %collective-permute-start.1 = (bf16[160,2048]{1,0:T(8,128)(2,1)}, bf16[160,2048]{1,0:T(8,128)(2,1)S(1)}, u32[]{:S(2)}, u32[]{:S(2)}) collective-permute-start(bf16[160,2048]{1,0:T(8,128)(2,1)} %get-tuple-element.41), channel_id=1, source_target_pairs={{1,0},{2,1},{3,2},{4,3},{5,4},{6,5},{7,6},{8,7},{9,8},{10,9},{11,1... | collective-permute-start | bytes 1966088 | tf_op jit(solution)/shard_map/ppermute | solution.py:474
  28.2 0.8 copy-start.1
  28.2 1.0 %copy-start.2 = (bf16[160,2048]{1,0:T(8,128)(2,1)}, bf16[160,2048]{1,0:T(8,128)(2,1)S(1)}, u32[]{:S(2)}) copy-start(bf16[160,2048]{1,0:T(8,128)(2,1)S(1)} %collective-permute-done.1.from_right) | copy-start | bytes 1966084
  47.5 1.4 %collective-permute-start.2 = (f32[256,128]{1,0:T(8,128)S(1)}, f32[256,128]{1,0:T(8,128)S(1)}, u32[]{:S(2)}, u32[]{:S(2)}) collective-permute-start(f32[256,128]{1,0:T(8,128)S(1)} %bitcast.5), channel_id=1, source_target_pairs={{0,8},{1,9},{2,10},{3,11},{4,12},{5,13},{6,14},{7,15},{8,0},{9,1},... | collective-permute-start | bytes 393224 | tf_op jit(solution)/shard_map/ppermute | solution.py:479
  49.0 9.4 %collective-permute-start.3 = (f32[128,128]{1,0:T(8,128)S(1)}, f32[128,128]{1,0:T(8,128)S(1)}, u32[]{:S(2)}, u32[]{:S(2)}) collective-permute-start(f32[128,128]{1,0:T(8,128)S(1)} %slice_select_fusion.2), channel_id=1, source_target_pairs={{0,16},{1,17},{2,18},{3,19},{4,20},{5,21},{6,22},{7,23},{8,24},{9,... | collective-permute-start | bytes 196616 | tf_op jit(solution)/shard_map/ppermute | solution.py:479
  52.2 11.5 %collective-permute-start.5 = (bf16[48,2048]{1,0:T(8,128)(2,1)}, bf16[48,2048]{1,0:T(8,128)(2,1)S(1)}, u32[]{:S(2)}, u32[]{:S(2)}) collective-permute-start(bf16[48,2048]{1,0:T(8,128)(2,1)} %get-tuple-element.45), channel_id=1, source_target_pairs={{1,0},{2,1},{3,2},{4,3},{5,4},{6,5},{7,6},{8,7},{9,8},{10,9},{11,1... | collective-permute-start | bytes 589832 | tf_op jit(solution)/shard_map/ppermute | solution.py:474
  58.4 5.3 %collective-permute-start.4 = (f32[128,128]{1,0:T(8,128)S(1)}, f32[128,128]{1,0:T(8,128)S(1)}, u32[]{:S(2)}, u32[]{:S(2)}) collective-permute-start(f32[128,128]{1,0:T(8,128)S(1)} %select_add_fusion), channel_id=1, source_target_pairs={{0,48},{1,49},{2,50},{3,51},{4,52},{5,53},{6,54},{7,55},{8,56},{9,... | collective-permute-start | bytes 196616 | tf_op jit(solution)/shard_map/ppermute | solution.py:479
  63.8 2.9 %copy-start = (bf16[48,2048]{1,0:T(8,128)(2,1)}, bf16[48,2048]{1,0:T(8,128)(2,1)S(1)}, u32[]{:S(2)}) copy-start(bf16[48,2048]{1,0:T(8,128)(2,1)S(1)} %collective-permute-done.5.heads) | copy-start | bytes 589828
  63.8 5.9 %collective-permute-start.7 = (f32[128,128]{1,0:T(8,128)S(1)}, f32[128,128]{1,0:T(8,128)S(1)}, u32[]{:S(2)}, u32[]{:S(2)}) collective-permute-start(f32[128,128]{1,0:T(8,128)S(1)} %add.52), channel_id=1, source_target_pairs={{0,128},{1,129},{2,130},{3,131},{4,132},{5,133},{6,134},{7,135},{8... | collective-permute-start | bytes 196616 | tf_op jit(solution)/shard_map/ppermute | solution.py:479
  65.9 4.9 %collective-permute-start.8 = (f32[128,128]{1,0:T(8,128)S(1)}, f32[128,128]{1,0:T(8,128)S(1)}, u32[]{:S(2)}, u32[]{:S(2)}) collective-permute-start(f32[128,128]{1,0:T(8,128)S(1)} %add.52), channel_id=1, source_target_pairs={{0,192},{1,193},{2,194},{3,195},{4,196},{5,197},{6,198},{7,199},{8... | collective-permute-start | bytes 196616 | tf_op jit(solution)/shard_map/ppermute | solution.py:479
  66.6 4.1 %collective-permute-start.6 = (f32[128,128]{1,0:T(8,128)S(1)}, f32[128,128]{1,0:T(8,128)S(1)}, u32[]{:S(2)}, u32[]{:S(2)}) collective-permute-start(f32[128,128]{1,0:T(8,128)S(1)} %add.52), channel_id=1, source_target_pairs={{0,64},{1,65},{2,66},{3,67},{4,68},{5,69},{6,70},{7,71},{8,72},{9,... | collective-permute-start | bytes 196616 | tf_op jit(solution)/shard_map/ppermute | solution.py:479
  70.8 5.8 %collective-permute-start.10 = (f32[128,128]{1,0:T(8,128)S(1)}, f32[128,128]{1,0:T(8,128)S(1)}, u32[]{:S(2)}, u32[]{:S(2)}) collective-permute-start(f32[128,128]{1,0:T(8,128)S(1)} %add_add_fusion.1), channel_id=1, source_target_pairs={{0,2},{1,3},{2,0},{3,1},{4,6},{5,7},{6,4},{7,5},{8,10},{9,11},{10,... | collective-permute-start | bytes 196616 | tf_op jit(solution)/shard_map/ppermute | solution.py:479
  71.1 5.5 %collective-permute-start.11 = (f32[128,128]{1,0:T(8,128)S(1)}, f32[128,128]{1,0:T(8,128)S(1)}, u32[]{:S(2)}, u32[]{:S(2)}) collective-permute-start(f32[128,128]{1,0:T(8,128)S(1)} %add_add_fusion.1), channel_id=1, source_target_pairs={{0,3},{1,2},{2,1},{3,0},{4,7},{5,6},{6,5},{7,4},{8,11},{9,10},{10,... | collective-permute-start | bytes 196616 | tf_op jit(solution)/shard_map/ppermute | solution.py:479
  73.3 3.7 %collective-permute-start.9 = (f32[128,128]{1,0:T(8,128)S(1)}, f32[128,128]{1,0:T(8,128)S(1)}, u32[]{:S(2)}, u32[]{:S(2)}) collective-permute-start(f32[128,128]{1,0:T(8,128)S(1)} %add_add_fusion.1), channel_id=1, source_target_pairs={{0,1},{1,0},{2,3},{3,2},{4,5},{5,4},{6,7},{7,6},{8,9},{9,8},{10,11... | collective-permute-start | bytes 196616 | tf_op jit(solution)/shard_map/ppermute | solution.py:479
  77.0 8.9 %collective-permute-start.12 = (f32[128,128]{1,0:T(8,128)S(1)}, f32[128,128]{1,0:T(8,128)S(1)}, u32[]{:S(2)}, u32[]{:S(2)}) collective-permute-start(f32[128,128]{1,0:T(8,128)S(1)} %add_add_fusion), channel_id=1, source_target_pairs={{0,6},{1,7},{2,4},{3,5},{4,2},{5,3},{6,0},{7,1},{8,14},{9,15},{10,... | collective-permute-start | bytes 196616 | tf_op jit(solution)/shard_map/ppermute | solution.py:479
  86.0 3.2 %collective-permute-start.13 = (f32[128,128]{1,0:T(8,128)S(1)}, f32[128,128]{1,0:T(8,128)S(1)}, u32[]{:S(2)}, u32[]{:S(2)}) collective-permute-start(f32[128,128]{1,0:T(8,128)S(1)} %add.59), channel_id=1, source_target_pairs={{0,16},{1,17},{2,18},{3,19},{4,20},{5,21},{6,22},{7,23},{8,24},{9,... | collective-permute-start | bytes 196616 | tf_op jit(solution)/shard_map/ppermute | solution.py:479
  89.2 3.9 %collective-permute-start.14 = (f32[256,128]{1,0:T(8,128)S(1)}, f32[256,128]{1,0:T(8,128)S(1)}, u32[]{:S(2)}, u32[]{:S(2)}) collective-permute-start(f32[256,128]{1,0:T(8,128)S(1)} %maximum_select_fusion.half), channel_id=1, source_target_pairs={{0,8},{1,9},{2,10},{3,11},{4,12},{5,13},{6,14},{7,15},{8,0},{9,1},... | collective-permute-start | bytes 393224 | tf_op jit(solution)/shard_map/ppermute | solution.py:479

commit v5 on v4

--- a/solution.py
+++ b/solution.py
@@ -83,7 +83,7 @@
         left[TAPS + EDGE : TAPS + 2 * EDGE, ls] = rep[:EDGE].astype(BF16)
 
 
-def tables_kernel(taps, fwd, bwd, plain, backwards):
+def tables_kernel(taps, skip_in, fwd, bwd, skip, plain, backwards):
     row = lax.broadcasted_iota(jnp.int32, (TAPS, TAPS), 0)
     col = lax.broadcasted_iota(jnp.int32, (TAPS, TAPS), 1)
     tile = pl.program_id(0)
@@ -93,6 +93,7 @@
         mirror = ((row + col == TAPS) | ((row == 0) & (col == 0))).astype(BF16)
         plain[...] = taps[...].astype(F32)
         backwards[...] = jnp.dot(taps[...], mirror, preferred_element_type=F32)
+        skip[...] = skip_in[...]
 
     first = pl.multiple_of(tile * PER_TILE, PER_TILE)
     plain_rows = plain[pl.ds(first, PER_TILE)]
@@ -355,22 +356,23 @@
     )(ids, q, g, k, k, v, v, q, taps)
 
 
-def make_tables(long_filter):
+def make_tables(long_filter, skip):
     groups = long_filter.shape[0]
     wide = pl.BlockSpec((PER_TILE, TAPS, 2 * TAPS), lambda i: (i, 0, 0))
     return pl.pallas_call(
         tables_kernel,
         grid=(groups // PER_TILE,),
-        in_specs=[fixed(long_filter.shape)],
-        out_specs=[wide, wide],
-        out_shape=[jax.ShapeDtypeStruct((groups, TAPS, 2 * TAPS), BF16)] * 2,
+        in_specs=[fixed(long_filter.shape), fixed(skip.shape)],
+        out_specs=[wide, wide, fixed(skip.shape)],
+        out_shape=[jax.ShapeDtypeStruct((groups, TAPS, 2 * TAPS), BF16)] * 2
+        + [jax.ShapeDtypeStruct(skip.shape, F32)],
         scratch_shapes=[pltpu.VMEM((groups, TAPS), F32)] * 2,
         compiler_params=params(),
         cost_estimate=pl.CostEstimate(
             flops=0, bytes_accessed=32 * groups * TAPS * TAPS, transcendentals=0
         ),
         name="tables",
-    )(long_filter)
+    )(long_filter, skip)
 
 
 def make_main(ids, q, k, v, g, taps, skip, fwd, bwd, from_left, from_right):
@@ -553,10 +555,10 @@
     )
     from_left = from_behind(to_right, 1)
     from_right = from_behind(to_left, -1)
-    fwd, bwd = make_tables(long_filter)
+    fwd, bwd, skip = make_tables(long_filter, skip_gain.reshape(1, channels))
     out, gq, gk, gv, heads, part = make_main(
         token_ids, query_in, key_in, value_in, out_grad, short_filters,
-        skip_gain.reshape(1, channels), fwd, bwd, from_left, from_right,
+        skip, fwd, bwd, from_left, from_right,
     )
     next_heads = from_behind(heads, -1)
     jobs = [

time: 94.1 us -> 94.1 us (level)
  no operation moved by 1% of the time
where the time goes in v5:
time: 94.1 us; the launch traced here: 93.8 us
  Pallas kernels  44 us (47%)
  starting transfers between devices  36.6 us (39%)
  waiting for transfers between devices  11.2 us (12%)
  local copies, waits for them, and re-layouts  1.05 us (1%)
    ppermute x12, starting transfers between devices, swap(): return lax.ppermute(value, AXES, [(s, s ^ mask) for s in range(count)])  19.7 us
    pallas_call x1, Pallas kernels, make_main(): pl.pallas_call(main_kernel, grid=(tiles // PER_STEP,), in_specs=[pl.Block...  18.2 us
    ppermute x3, starting transfers between devices, from_behind(): lax.ppermute(value, AXES, [(s, s + steps) for s in range(first, last)])  16.9 us
    pallas_call x1, Pallas kernels, make_tables(): pl.pallas_call(tables_kernel, grid=(groups // PER_TILE,), in_specs=[fixed...  11.7 us
    ppermute x12, waiting for transfers between devices, swap(): return lax.ppermute(value, AXES, [(s, s ^ mask) for s in range(count)])  10.2 us
    pallas_call x3, Pallas kernels, make_back(): pl.pallas_call(back_kernel, grid=(channels // width,), in_specs=[columns(...  9.21 us
    pallas_call x1, Pallas kernels, make_edges(): pl.pallas_call(edges_kernel, grid=(channels // width,), in_specs=[pl.Bloc...  4.1 us
  transfers between devices with their start and end apart: 15, of which 7 were waited for; matrix products, arithmetic and copies ran while one was open for 0% of the time, Pallas kernels for 22%

profile of v5, /device:TPU:1, one launch (start us, length us, event | category | flops | bytes accessed | tf_op | source)
XLA Modules:
  0.0 93.8 jit_solution(15936491155373099463)
XLA Ops:
  0.6 4.1 %edges.1 = (bf16[160,2048]{1,0:T(8,128)(2,1)}, bf16[160,2048]{1,0:T(8,128)(2,1)}) custom-call(s32[256]{0:T(256)} %ids.3, bf16[256,2048]{1,0:T(8,128)(2,1)} %q.3, bf16[256,2048]{1,0:T(8,128)(2,1)} %g.3, bf16[256,2048]{1,0:T(8,128)(2,1)} %k.3, bf16[256,2048]{1,0:T(8,128)(2,1)} %k.3, bf16[256,2048]{1,0:T(8,128)(2,1)} %v.3, bf16[256,2048]{1,0:T(8,128)(2,1)} %v.3, ...), custom_call_target="tpu_custom_call" | custom-call | tf_op jit(solution)/shard_map/edges/pallas_call | solution.py:338
  4.7 4.4 %collective-permute-start = (bf16[160,2048]{1,0:T(8,128)(2,1)}, bf16[160,2048]{1,0:T(8,128)(2,1)S(1)}, u32[]{:S(2)}, u32[]{:S(2)}) collective-permute-start(bf16[160,2048]{1,0:T(8,128)(2,1)} %get-tuple-element.42), channel_id=1, source_target_pairs={{0,1},{1,2},{2,3},{3,4},{4,5},{5,6},{6,7},{7,8},{8,9},{9,10},{10,1... | collective-permute-start | bytes 1966088 | tf_op jit(solution)/shard_map/ppermute | solution.py:476
  9.1 6.4 %collective-permute-start.1 = (bf16[160,2048]{1,0:T(8,128)(2,1)}, bf16[160,2048]{1,0:T(8,128)(2,1)S(1)}, u32[]{:S(2)}, u32[]{:S(2)}) collective-permute-start(bf16[160,2048]{1,0:T(8,128)(2,1)} %get-tuple-element.43), channel_id=1, source_target_pairs={{1,0},{2,1},{3,2},{4,3},{5,4},{6,5},{7,6},{8,7},{9,8},{10,9},{11,1... | collective-permute-start | bytes 1966088 | tf_op jit(solution)/shard_map/ppermute | solution.py:476
  15.6 11.7 %tables.1 = (bf16[128,128,256]{2,1,0:T(8,128)(2,1)}, bf16[128,128,256]{2,1,0:T(8,128)(2,1)}, f32[1,2048]{1,0:T(1,128)}) custom-call(bf16[128,128]{1,0:T(8,128)(2,1)} %taps.1, f32[1,2048]{1,0:T(1,128)} %bitcast.6), custom_call_target="tpu_custom_call" | custom-call | bytes 67108864 | tf_op jit(solution)/shard_map/tables/pallas_call | solution.py:362
  27.3 1.0 %collective-permute-done.from_left = bf16[160,2048]{1,0:T(8,128)(2,1)S(1)} collective-permute-done((bf16[160,2048]{1,0:T(8,128)(2,1)}, bf16[160,2048]{1,0:T(8,128)(2,1)S(1)}, u32[]{:S(2)}, u32[]{:S(2)}) %collective-permute-start) | collective-permute-done | bytes 655392 | tf_op jit(solution)/shard_map/ppermute | solution.py:476
  28.2 0.0 copy-start.1
  28.2 0.0 collective-permute-done.1.from_right
  28.2 0.0 copy-start.2
  28.2 0.8 copy-done.1
  29.1 0.2 copy-done.2
  29.3 18.2 %main.1 = (bf16[256,2048]{1,0:T(8,128)(2,1)}, bf16[256,2048]{1,0:T(8,128)(2,1)}, bf16[256,2048]{1,0:T(8,128)(2,1)}, bf16[256,2048]{1,0:T(8,128)(2,1)}, bf16[48,2...) custom-call(s32[256]{0:T(256)} %ids.3, bf16[256,2048]{1,0:T(8,128)(2,1)} %q.3, bf16[256,2048]{1,0:T(8,128)(2,1)} %k.3, ...), custom_call_target="tpu_custom_call" | custom-call | tf_op jit(solution)/shard_map/main/pallas_call | solution.py:383
  47.5 0.2 collective-permute-start.2
  47.7 1.3 %collective-permute-done.2 = f32[256,128]{1,0:T(8,128)S(1)} collective-permute-done((f32[256,128]{1,0:T(8,128)S(1)}, f32[256,128]{1,0:T(8,128)S(1)}, u32[]{:S(2)}, u32[]{:S(2)}) %collective-permute-start.2) | collective-permute-done | bytes 131104 | tf_op jit(solution)/shard_map/ppermute | solution.py:481
  49.0 3.2 %collective-permute-start.3 = (f32[128,128]{1,0:T(8,128)S(1)}, f32[128,128]{1,0:T(8,128)S(1)}, u32[]{:S(2)}, u32[]{:S(2)}) collective-permute-start(f32[128,128]{1,0:T(8,128)S(1)} %slice_select_fusion.2), channel_id=1, source_target_pairs={{0,16},{1,17},{2,18},{3,19},{4,20},{5,21},{6,22},{7,23},{8,24},{9,... | collective-permute-start | bytes 196616 | tf_op jit(solution)/shard_map/ppermute | solution.py:481
  52.2 6.1 %collective-permute-start.5 = (bf16[48,2048]{1,0:T(8,128)(2,1)}, bf16[48,2048]{1,0:T(8,128)(2,1)S(1)}, u32[]{:S(2)}, u32[]{:S(2)}) collective-permute-start(bf16[48,2048]{1,0:T(8,128)(2,1)} %get-tuple-element.47), channel_id=1, source_target_pairs={{1,0},{2,1},{3,2},{4,3},{5,4},{6,5},{7,6},{8,7},{9,8},{10,9},{11,1... | collective-permute-start | bytes 589832 | tf_op jit(solution)/shard_map/ppermute | solution.py:476
  58.4 0.0 collective-permute-done.3
  58.4 1.6 %collective-permute-start.4 = (f32[128,128]{1,0:T(8,128)S(1)}, f32[128,128]{1,0:T(8,128)S(1)}, u32[]{:S(2)}, u32[]{:S(2)}) collective-permute-start(f32[128,128]{1,0:T(8,128)S(1)} %select_add_fusion), channel_id=1, source_target_pairs={{0,48},{1,49},{2,50},{3,51},{4,52},{5,53},{6,54},{7,55},{8,56},{9,... | collective-permute-start | bytes 196616 | tf_op jit(solution)/shard_map/ppermute | solution.py:481
  60.1 3.7 %collective-permute-done.4 = f32[128,128]{1,0:T(8,128)S(1)} collective-permute-done((f32[128,128]{1,0:T(8,128)S(1)}, f32[128,128]{1,0:T(8,128)S(1)}, u32[]{:S(2)}, u32[]{:S(2)}) %collective-permute-start.4) | collective-permute-done | bytes 65568 | tf_op jit(solution)/shard_map/ppermute | solution.py:481
  63.8 0.0 collective-permute-done.5.heads
  63.8 0.0 copy-start
  63.8 2.1 %collective-permute-start.7 = (f32[128,128]{1,0:T(8,128)S(1)}, f32[128,128]{1,0:T(8,128)S(1)}, u32[]{:S(2)}, u32[]{:S(2)}) collective-permute-start(f32[128,128]{1,0:T(8,128)S(1)} %add.52), channel_id=1, source_target_pairs={{0,128},{1,129},{2,130},{3,131},{4,132},{5,133},{6,134},{7,135},{8... | collective-permute-start | bytes 196616 | tf_op jit(solution)/shard_map/ppermute | solution.py:481
  65.9 0.8 collective-permute-start.8
  66.6 0.0 collective-permute-start.6
  66.6 0.0 copy-done
  66.6 3.1 %back.3 = bf16[256,2048]{1,0:T(8,128)(2,1)} custom-call(bf16[256,2048]{1,0:T(8,128)(2,1)} %get-tuple-element.49.grads, bf16[48,2048]{1,0:T(8,128)(2,1)} %copy-done, f32[3,7,2048]{2,1,0:T(8,128)} %taps_ref.6), custom_call_target="tpu_custom_call" | custom-call | flops 7340032 | bytes 4194304 | tf_op jit(solution)/shard_map/back/pallas_call | solution.py:421
  69.7 0.0 collective-permute-done.7
  69.7 1.1 %collective-permute-done.8 = f32[128,128]{1,0:T(8,128)S(1)} collective-permute-done((f32[128,128]{1,0:T(8,128)S(1)}, f32[128,128]{1,0:T(8,128)S(1)}, u32[]{:S(2)}, u32[]{:S(2)}) %collective-permute-start.8) | collective-permute-done | bytes 65568 | tf_op jit(solution)/shard_map/ppermute | solution.py:481
  70.8 0.0 collective-permute-done.6
  70.8 0.3 collective-permute-start.10
  71.1 2.2 %collective-permute-start.11 = (f32[128,128]{1,0:T(8,128)S(1)}, f32[128,128]{1,0:T(8,128)S(1)}, u32[]{:S(2)}, u32[]{:S(2)}) collective-permute-start(f32[128,128]{1,0:T(8,128)S(1)} %add_add_fusion.1), channel_id=1, source_target_pairs={{0,3},{1,2},{2,1},{3,0},{4,7},{5,6},{6,5},{7,4},{8,11},{9,10},{10,... | collective-permute-start | bytes 196616 | tf_op jit(solution)/shard_map/ppermute | solution.py:481
  73.3 0.2 collective-permute-start.9
  73.5 3.1 %back.4 = bf16[256,2048]{1,0:T(8,128)(2,1)} custom-call(bf16[256,2048]{1,0:T(8,128)(2,1)} %get-tuple-element.56.grads, bf16[48,2048]{1,0:T(8,128)(2,1)} %copy-done, f32[3,7,2048]{2,1,0:T(8,128)} %taps_ref.6), custom_call_target="tpu_custom_call" | custom-call | flops 7340032 | bytes 4194304 | tf_op jit(solution)/shard_map/back/pallas_call | solution.py:421
  76.6 0.0 collective-permute-done.10
  76.6 0.0 collective-permute-done.11
  76.6 0.4 collective-permute-done.9
  77.0 5.9 %collective-permute-start.12 = (f32[128,128]{1,0:T(8,128)S(1)}, f32[128,128]{1,0:T(8,128)S(1)}, u32[]{:S(2)}, u32[]{:S(2)}) collective-permute-start(f32[128,128]{1,0:T(8,128)S(1)} %add_add_fusion), channel_id=1, source_target_pairs={{0,6},{1,7},{2,4},{3,5},{4,2},{5,3},{6,0},{7,1},{8,14},{9,15},{10,... | collective-permute-start | bytes 196616 | tf_op jit(solution)/shard_map/ppermute | solution.py:481
  82.9 3.1 %back.5 = bf16[256,2048]{1,0:T(8,128)(2,1)} custom-call(bf16[256,2048]{1,0:T(8,128)(2,1)} %get-tuple-element.63.grads, bf16[48,2048]{1,0:T(8,128)(2,1)} %copy-done, f32[3,7,2048]{2,1,0:T(8,128)} %taps_ref.6), custom_call_target="tpu_custom_call" | custom-call | flops 7340032 | bytes 4194304 | tf_op jit(solution)/shard_map/back/pallas_call | solution.py:421
  85.9 0.0 collective-permute-done.12
  86.0 0.4 collective-permute-start.13
  86.3 2.8 %collective-permute-done.13 = f32[128,128]{1,0:T(8,128)S(1)} collective-permute-done((f32[128,128]{1,0:T(8,128)S(1)}, f32[128,128]{1,0:T(8,128)S(1)}, u32[]{:S(2)}, u32[]{:S(2)}) %collective-permute-start.13) | collective-permute-done | bytes 65568 | tf_op jit(solution)/shard_map/ppermute | solution.py:481
  89.2 2.9 %collective-permute-start.14 = (f32[256,128]{1,0:T(8,128)S(1)}, f32[256,128]{1,0:T(8,128)S(1)}, u32[]{:S(2)}, u32[]{:S(2)}) collective-permute-start(f32[256,128]{1,0:T(8,128)S(1)} %maximum_select_fusion.half), channel_id=1, source_target_pairs={{0,8},{1,9},{2,10},{3,11},{4,12},{5,13},{6,14},{7,15},{8,0},{9,1},... | collective-permute-start | bytes 393224 | tf_op jit(solution)/shard_map/ppermute | solution.py:481
  92.0 1.0 %collective-permute-done.14.other = f32[256,128]{1,0:T(8,128)S(1)} collective-permute-done((f32[256,128]{1,0:T(8,128)S(1)}, f32[256,128]{1,0:T(8,128)S(1)}, u32[]{:S(2)}, u32[]{:S(2)}) %collective-permute-start.14) | collective-permute-done | bytes 131104 | tf_op jit(solution)/shard_map/ppermute | solution.py:481
  93.0 0.7 last.1
  (9 shorter events, 0.1 us)
Async XLA Ops:
  4.7 23.5 %collective-permute-start = (bf16[160,2048]{1,0:T(8,128)(2,1)}, bf16[160,2048]{1,0:T(8,128)(2,1)S(1)}, u32[]{:S(2)}, u32[]{:S(2)}) collective-permute-start(bf16[160,2048]{1,0:T(8,128)(2,1)} %get-tuple-element.42), channel_id=1, source_target_pairs={{0,1},{1,2},{2,3},{3,4},{4,5},{5,6},{6,7},{7,8},{8,9},{9,10},{10,1... | collective-permute-start | bytes 1966088 | tf_op jit(solution)/shard_map/ppermute | solution.py:476
  9.1 19.1 %collective-permute-start.1 = (bf16[160,2048]{1,0:T(8,128)(2,1)}, bf16[160,2048]{1,0:T(8,128)(2,1)S(1)}, u32[]{:S(2)}, u32[]{:S(2)}) collective-permute-start(bf16[160,2048]{1,0:T(8,128)(2,1)} %get-tuple-element.43), channel_id=1, source_target_pairs={{1,0},{2,1},{3,2},{4,3},{5,4},{6,5},{7,6},{8,7},{9,8},{10,9},{11,1... | collective-permute-start | bytes 1966088 | tf_op jit(solution)/shard_map/ppermute | solution.py:476
  28.2 0.8 copy-start.1
  28.2 1.0 %copy-start.2 = (bf16[160,2048]{1,0:T(8,128)(2,1)}, bf16[160,2048]{1,0:T(8,128)(2,1)S(1)}, u32[]{:S(2)}) copy-start(bf16[160,2048]{1,0:T(8,128)(2,1)S(1)} %collective-permute-done.1.from_right) | copy-start | bytes 1966084
  47.5 1.4 %collective-permute-start.2 = (f32[256,128]{1,0:T(8,128)S(1)}, f32[256,128]{1,0:T(8,128)S(1)}, u32[]{:S(2)}, u32[]{:S(2)}) collective-permute-start(f32[256,128]{1,0:T(8,128)S(1)} %bitcast.5), channel_id=1, source_target_pairs={{0,8},{1,9},{2,10},{3,11},{4,12},{5,13},{6,14},{7,15},{8,0},{9,1},... | collective-permute-start | bytes 393224 | tf_op jit(solution)/shard_map/ppermute | solution.py:481
  49.0 9.4 %collective-permute-start.3 = (f32[128,128]{1,0:T(8,128)S(1)}, f32[128,128]{1,0:T(8,128)S(1)}, u32[]{:S(2)}, u32[]{:S(2)}) collective-permute-start(f32[128,128]{1,0:T(8,128)S(1)} %slice_select_fusion.2), channel_id=1, source_target_pairs={{0,16},{1,17},{2,18},{3,19},{4,20},{5,21},{6,22},{7,23},{8,24},{9,... | collective-permute-start | bytes 196616 | tf_op jit(solution)/shard_map/ppermute | solution.py:481
  52.2 11.5 %collective-permute-start.5 = (bf16[48,2048]{1,0:T(8,128)(2,1)}, bf16[48,2048]{1,0:T(8,128)(2,1)S(1)}, u32[]{:S(2)}, u32[]{:S(2)}) collective-permute-start(bf16[48,2048]{1,0:T(8,128)(2,1)} %get-tuple-element.47), channel_id=1, source_target_pairs={{1,0},{2,1},{3,2},{4,3},{5,4},{6,5},{7,6},{8,7},{9,8},{10,9},{11,1... | collective-permute-start | bytes 589832 | tf_op jit(solution)/shard_map/ppermute | solution.py:476
  58.4 5.3 %collective-permute-start.4 = (f32[128,128]{1,0:T(8,128)S(1)}, f32[128,128]{1,0:T(8,128)S(1)}, u32[]{:S(2)}, u32[]{:S(2)}) collective-permute-start(f32[128,128]{1,0:T(8,128)S(1)} %select_add_fusion), channel_id=1, source_target_pairs={{0,48},{1,49},{2,50},{3,51},{4,52},{5,53},{6,54},{7,55},{8,56},{9,... | collective-permute-start | bytes 196616 | tf_op jit(solution)/shard_map/ppermute | solution.py:481
  63.8 2.9 %copy-start = (bf16[48,2048]{1,0:T(8,128)(2,1)}, bf16[48,2048]{1,0:T(8,128)(2,1)S(1)}, u32[]{:S(2)}) copy-start(bf16[48,2048]{1,0:T(8,128)(2,1)S(1)} %collective-permute-done.5.heads) | copy-start | bytes 589828
  63.8 5.9 %collective-permute-start.7 = (f32[128,128]{1,0:T(8,128)S(1)}, f32[128,128]{1,0:T(8,128)S(1)}, u32[]{:S(2)}, u32[]{:S(2)}) collective-permute-start(f32[128,128]{1,0:T(8,128)S(1)} %add.52), channel_id=1, source_target_pairs={{0,128},{1,129},{2,130},{3,131},{4,132},{5,133},{6,134},{7,135},{8... | collective-permute-start | bytes 196616 | tf_op jit(solution)/shard_map/ppermute | solution.py:481
  65.9 4.9 %collective-permute-start.8 = (f32[128,128]{1,0:T(8,128)S(1)}, f32[128,128]{1,0:T(8,128)S(1)}, u32[]{:S(2)}, u32[]{:S(2)}) collective-permute-start(f32[128,128]{1,0:T(8,128)S(1)} %add.52), channel_id=1, source_target_pairs={{0,192},{1,193},{2,194},{3,195},{4,196},{5,197},{6,198},{7,199},{8... | collective-permute-start | bytes 196616 | tf_op jit(solution)/shard_map/ppermute | solution.py:481
  66.6 4.1 %collective-permute-start.6 = (f32[128,128]{1,0:T(8,128)S(1)}, f32[128,128]{1,0:T(8,128)S(1)}, u32[]{:S(2)}, u32[]{:S(2)}) collective-permute-start(f32[128,128]{1,0:T(8,128)S(1)} %add.52), channel_id=1, source_target_pairs={{0,64},{1,65},{2,66},{3,67},{4,68},{5,69},{6,70},{7,71},{8,72},{9,... | collective-permute-start | bytes 196616 | tf_op jit(solution)/shard_map/ppermute | solution.py:481
  70.8 5.8 %collective-permute-start.10 = (f32[128,128]{1,0:T(8,128)S(1)}, f32[128,128]{1,0:T(8,128)S(1)}, u32[]{:S(2)}, u32[]{:S(2)}) collective-permute-start(f32[128,128]{1,0:T(8,128)S(1)} %add_add_fusion.1), channel_id=1, source_target_pairs={{0,2},{1,3},{2,0},{3,1},{4,6},{5,7},{6,4},{7,5},{8,10},{9,11},{10,... | collective-permute-start | bytes 196616 | tf_op jit(solution)/shard_map/ppermute | solution.py:481
  71.1 5.5 %collective-permute-start.11 = (f32[128,128]{1,0:T(8,128)S(1)}, f32[128,128]{1,0:T(8,128)S(1)}, u32[]{:S(2)}, u32[]{:S(2)}) collective-permute-start(f32[128,128]{1,0:T(8,128)S(1)} %add_add_fusion.1), channel_id=1, source_target_pairs={{0,3},{1,2},{2,1},{3,0},{4,7},{5,6},{6,5},{7,4},{8,11},{9,10},{10,... | collective-permute-start | bytes 196616 | tf_op jit(solution)/shard_map/ppermute | solution.py:481
  73.3 3.7 %collective-permute-start.9 = (f32[128,128]{1,0:T(8,128)S(1)}, f32[128,128]{1,0:T(8,128)S(1)}, u32[]{:S(2)}, u32[]{:S(2)}) collective-permute-start(f32[128,128]{1,0:T(8,128)S(1)} %add_add_fusion.1), channel_id=1, source_target_pairs={{0,1},{1,0},{2,3},{3,2},{4,5},{5,4},{6,7},{7,6},{8,9},{9,8},{10,11... | collective-permute-start | bytes 196616 | tf_op jit(solution)/shard_map/ppermute | solution.py:481
  77.0 8.9 %collective-permute-start.12 = (f32[128,128]{1,0:T(8,128)S(1)}, f32[128,128]{1,0:T(8,128)S(1)}, u32[]{:S(2)}, u32[]{:S(2)}) collective-permute-start(f32[128,128]{1,0:T(8,128)S(1)} %add_add_fusion), channel_id=1, source_target_pairs={{0,6},{1,7},{2,4},{3,5},{4,2},{5,3},{6,0},{7,1},{8,14},{9,15},{10,... | collective-permute-start | bytes 196616 | tf_op jit(solution)/shard_map/ppermute | solution.py:481
  86.0 3.2 %collective-permute-start.13 = (f32[128,128]{1,0:T(8,128)S(1)}, f32[128,128]{1,0:T(8,128)S(1)}, u32[]{:S(2)}, u32[]{:S(2)}) collective-permute-start(f32[128,128]{1,0:T(8,128)S(1)} %add.59), channel_id=1, source_target_pairs={{0,16},{1,17},{2,18},{3,19},{4,20},{5,21},{6,22},{7,23},{8,24},{9,... | collective-permute-start | bytes 196616 | tf_op jit(solution)/shard_map/ppermute | solution.py:481
  89.2 3.9 %collective-permute-start.14 = (f32[256,128]{1,0:T(8,128)S(1)}, f32[256,128]{1,0:T(8,128)S(1)}, u32[]{:S(2)}, u32[]{:S(2)}) collective-permute-start(f32[256,128]{1,0:T(8,128)S(1)} %maximum_select_fusion.half), channel_id=1, source_target_pairs={{0,8},{1,9},{2,10},{3,11},{4,12},{5,13},{6,14},{7,15},{8,0},{9,1},... | collective-permute-start | bytes 393224 | tf_op jit(solution)/shard_map/ppermute | solution.py:481
